TPU v7x, 32 devices: a whole 2x2x4 slice. The times are simulated.
32 devices in a mesh: dp: 8 (over y, x, core), fsdp: 4 (over z).
Axes of the slice: x: 2, y: 2, z: 4, core: 2. Of those that a mesh axis runs over, the one named last changes fastest.
Arguments:
- tokens: bfloat16 [8192, 1536], P(('dp', 'fsdp')), may hold values from -6 to 6
- doc_lengths: int32 [128], P(('dp', 'fsdp')), may hold values from 0 to 256, as said below
- norm_gain: bfloat16 [1536], P(('dp', 'fsdp')), may hold values from 0.5 to 1.5
- w_attn_in: bfloat16 [1536, 6144], P(('dp', 'fsdp')), may hold values from -0.15625 to 0.15625
- w_rates: bfloat16 [1536, 72], P(('dp', 'fsdp')), may hold values from -0.15625 to 0.15625
- rate_bias: float32 [72], replicated, may hold values from -2 to 6
- q_gain: bfloat16 [1536], P(('dp', 'fsdp')), may hold values from 0.5 to 1.5
- k_gain: bfloat16 [1536], P(('dp', 'fsdp')), may hold values from 0.5 to 1.5
- w_out: bfloat16 [1536, 1536], P(('dp', 'fsdp')), may hold values from -0.75 to 0.75
- ffn_gain: bfloat16 [1536], P(('dp', 'fsdp')), may hold values from 0.5 to 1.5
- w_gate_up: bfloat16 [1536, 8192], P(('dp', 'fsdp')), may hold values from -0.15625 to 0.15625
- w_down: bfloat16 [4096, 1536], P(('dp', 'fsdp')), may hold values from -0.09375 to 0.09375
- cotangent: bfloat16 [8192, 1536], P(('dp', 'fsdp')), may hold values from -6 to 6
Outputs:
- layer_out: bfloat16 [8192, 1536], P(('dp', 'fsdp'))
- d_tokens: float32 [8192, 1536], P(('dp', 'fsdp'))
- d_norm_gain: float32 [1536], P(('dp', 'fsdp'))
- d_w_attn_in: float32 [1536, 6144], P(('dp', 'fsdp'))
- d_w_rates: float32 [1536, 72], P(('dp', 'fsdp'))
- d_rate_bias: float32 [72], replicated
- d_q_gain: float32 [1536], P(('dp', 'fsdp'))
- d_k_gain: float32 [1536], P(('dp', 'fsdp'))
- d_w_out: float32 [1536, 1536], P(('dp', 'fsdp'))
- d_ffn_gain: float32 [1536], P(('dp', 'fsdp'))
- d_w_gate_up: float32 [1536, 8192], P(('dp', 'fsdp'))
- d_w_down: float32 [4096, 1536], P(('dp', 'fsdp'))
Inputs may be any that keep to these rules, and one draw needn't show every extreme that they name: `doc_lengths`: consecutive groups of 4 entries belong to one bucket, in the order of the buckets, and give that bucket's document lengths in order (zero allowed); each group sums to at most 256, rows past the sum are padding. In every draw some bucket holds one document of 256 rows.
All inputs are finite; a program needn't handle non-finite values.
Results may differ from a plain program's by a relative error of at most 0.012.
Values may be sent and summed in bfloat16 or wider, within the bound.
No kernel may reach another device: no remote copies, remote signals or barrier semaphores. Data moves between devices by JAX's collectives and lax.ppermute only.
A program may use at most 448 MiB of HBM per device.

v0:
```python
import jax
import jax.numpy as jnp
from jax import lax
from jax.sharding import PartitionSpec as P

HEADS = 24
HEAD_DIM = 64


EPS = 1e-06
NEG = -1e30


def normed(field_in):
    factor = lax.rsqrt(jnp.mean(field_in * field_in, axis=-1, keepdims=True) + EPS)
    return (field_in * factor, factor)


def norm_back(normal, factor, grad_in):
    return factor * (grad_in - normal * jnp.mean(grad_in * normal, axis=-1, keepdims=True))


def outer_sum(left_side, right_side):
    return lax.dot_general(
        left_side, right_side, (((0,), (0,)), ((), ())), preferred_element_type=jnp.float32
    )


def times_rows(grad_low, weight_rows):
    return lax.dot_general(
        grad_low, weight_rows, (((1,), (1,)), ((), ())), preferred_element_type=jnp.float32
    )


def shift_prev(field_in, same_prev):
    return jnp.concatenate([jnp.zeros_like(field_in[:1]), field_in[:-1]], axis=0) * same_prev


def shift_next(field_in):
    return jnp.concatenate([field_in[1:], jnp.zeros_like(field_in[:1])], axis=0)


def mix_forward(current, mix_rate, same_prev):
    previous = shift_prev(current, same_prev)
    mix_three = mix_rate[:, :, None]
    return (mix_three * previous + (1.0 - mix_three) * current, previous)


def mix_back(grad_in, mix_rate, current, previous, same_prev):
    mix_three = mix_rate[:, :, None]
    d_current = (1.0 - mix_three) * grad_in + shift_next(mix_three * grad_in * same_prev)
    d_rate = jnp.sum(grad_in * (previous - current), axis=-1) * mix_rate * (1.0 - mix_rate)
    return (d_current, d_rate)


def score_block(q_low, k_low, decay_sum, scale_qk):
    raw_scores = jnp.einsum("thd,shd->hts", q_low, k_low, preferred_element_type=jnp.float32)
    decay_t = decay_sum.T
    return raw_scores * scale_qk + decay_t[:, :, None] - decay_t[:, None, :]


def to_owners(gradient_terms):
    shares = lax.axis_size(("dp", "fsdp"))
    packed = jnp.concatenate([term.reshape(shares, -1) for term in gradient_terms], axis=1)
    owned = lax.psum_scatter(packed, ("dp", "fsdp"), scatter_dimension=0, tiled=True)
    owned = owned.reshape(-1)
    results = []
    offset = 0
    for term in gradient_terms:
        amount = term.size // shares
        results.append(
            owned[offset : offset + amount].reshape((term.shape[0] // shares,) + term.shape[1:])
        )
        offset = offset + amount
    return tuple(results)


def body(
    tokens,
    doc_lengths,
    norm_gain,
    w_attn_in,
    w_rates,
    rate_bias,
    q_gain,
    k_gain,
    w_out,
    ffn_gain,
    w_gate_up,
    w_down,
    cotangent,
):
    tok_rows = tokens.shape[0]
    width = tokens.shape[1]
    head_count = HEADS
    head_size = HEAD_DIM
    ff_width = w_gate_up.shape[1] // 2
    proj_cols = w_attn_in.shape[1]
    rate_cols = w_rates.shape[1]
    scale_qk = head_size ** (-0.5)
    doc_ends = jnp.cumsum(doc_lengths)
    places = jnp.arange(tok_rows, dtype=jnp.int32)
    segment = jnp.sum((doc_ends[None, :] <= places[:, None]).astype(jnp.int32), axis=1)
    live_rows = (places < doc_ends[-1]).astype(jnp.float32)[:, None]
    same_prev = jnp.concatenate([jnp.zeros((1,), dtype=bool), segment[1:] == segment[:-1]]).astype(
        jnp.float32
    )[:, None, None]
    allowed = (places[:, None] >= places[None, :]) & (segment[:, None] == segment[None, :])
    stream_in = tokens.astype(jnp.float32)
    normal_one, factor_one = normed(stream_in)
    store_d = 1
    store_f = 1
    full_proj = jnp.zeros((store_d, proj_cols), jnp.bfloat16)
    full_rate = jnp.zeros((store_d, rate_cols), jnp.bfloat16)
    piece_gain = lax.all_gather(norm_gain, ("dp", "fsdp"), axis=0, tiled=True)
    piece_proj = lax.all_gather(w_attn_in, ("dp", "fsdp"), axis=0, tiled=True)
    piece_rate = lax.all_gather(w_rates, ("dp", "fsdp"), axis=0, tiled=True)
    piece_q = lax.all_gather(q_gain, ("dp", "fsdp"), axis=0, tiled=True)
    piece_k = lax.all_gather(k_gain, ("dp", "fsdp"), axis=0, tiled=True)
    part_low = (normal_one * piece_gain.astype(jnp.float32)).astype(jnp.bfloat16)
    projected = jnp.dot(part_low, piece_proj, preferred_element_type=jnp.float32)
    rate_pre = jnp.dot(part_low, piece_rate, preferred_element_type=jnp.float32)
    gain_one = piece_gain
    gain_q = piece_q
    gain_k = piece_k
    projected, rate_pre, gain_one, gain_q, gain_k, full_proj, full_rate = (
        projected,
        rate_pre,
        gain_one,
        gain_q,
        gain_k,
        full_proj,
        full_rate,
    )
    hidden_one = (normal_one * gain_one.astype(jnp.float32)).astype(jnp.bfloat16)
    rate_all = rate_pre + rate_bias
    query_raw = projected[:, 0:width].reshape(tok_rows, head_count, head_size)
    key_raw = projected[:, width : 2 * width].reshape(tok_rows, head_count, head_size)
    value_raw = projected[:, 2 * width : 3 * width].reshape(tok_rows, head_count, head_size)
    gate_pre = projected[:, 3 * width :].reshape(tok_rows, head_count, head_size)
    forget_pre = rate_all[:, :head_count]
    key_mix = jax.nn.sigmoid(rate_all[:, head_count : 2 * head_count])
    value_mix = jax.nn.sigmoid(rate_all[:, 2 * head_count :])
    decay_sum = jnp.cumsum(jax.nn.log_sigmoid(forget_pre), axis=0)
    key_mixed, key_prev = mix_forward(key_raw, key_mix, same_prev)
    value_mixed, value_prev = mix_forward(value_raw, value_mix, same_prev)
    gain_q3 = gain_q.astype(jnp.float32).reshape(head_count, head_size)
    gain_k3 = gain_k.astype(jnp.float32).reshape(head_count, head_size)
    q_normal, q_factor = normed(query_raw)
    k_normal, k_factor = normed(key_mixed)
    q_low = (q_normal * gain_q3).astype(jnp.bfloat16)
    k_low = (k_normal * gain_k3).astype(jnp.bfloat16)
    v_low = value_mixed.astype(jnp.bfloat16)
    scores = score_block(q_low, k_low, decay_sum, scale_qk)
    masked = jnp.where(allowed[None], scores, NEG)
    row_top = jnp.max(masked, axis=-1, keepdims=True)
    exp_terms = jnp.exp(masked - row_top)
    row_total = jnp.sum(exp_terms, axis=-1, keepdims=True)
    attn_prob = exp_terms / row_total
    log_total = row_top + jnp.log(row_total)
    attended = jnp.einsum(
        "hts,shd->thd", attn_prob.astype(jnp.bfloat16), v_low, preferred_element_type=jnp.float32
    )
    out_gate = jax.nn.sigmoid(gate_pre)
    mixed_low = ((attended * out_gate).reshape(tok_rows, width) * live_rows).astype(jnp.bfloat16)
    full_mix = jnp.zeros((store_d, width), jnp.bfloat16)
    total_out = jnp.dot(
        mixed_low,
        lax.all_gather(w_out, ("dp", "fsdp"), axis=0, tiled=True),
        preferred_element_type=jnp.float32,
    )
    attn_out, full_mix = (total_out, full_mix)
    stream_mid = stream_in + attn_out
    normal_two, factor_two = normed(stream_mid)
    full_gu = jnp.zeros((store_d, 2 * ff_width), jnp.bfloat16)
    piece_gain = lax.all_gather(ffn_gain, ("dp", "fsdp"), axis=0, tiled=True)
    piece_gu = lax.all_gather(w_gate_up, ("dp", "fsdp"), axis=0, tiled=True)
    part_low = (normal_two * piece_gain.astype(jnp.float32)).astype(jnp.bfloat16)
    gate_up = jnp.dot(part_low, piece_gu, preferred_element_type=jnp.float32)
    gain_two = piece_gain
    gate_up, gain_two, full_gu = (gate_up, gain_two, full_gu)
    hidden_two = (normal_two * gain_two.astype(jnp.float32)).astype(jnp.bfloat16)
    gate_val = gate_up[:, :ff_width]
    up_val = gate_up[:, ff_width:]
    gate_sig = jax.nn.sigmoid(gate_val)
    act_low = (gate_val * gate_sig * up_val * live_rows).astype(jnp.bfloat16)
    full_down = jnp.zeros((store_f, width), jnp.bfloat16)
    total_out = jnp.dot(
        act_low,
        lax.all_gather(w_down, ("dp", "fsdp"), axis=0, tiled=True),
        preferred_element_type=jnp.float32,
    )
    ffn_out, full_down = (total_out, full_down)
    layer_out = (stream_mid + ffn_out).astype(jnp.bfloat16)
    grad_out = cotangent.astype(jnp.float32)
    down_term = outer_sum(act_low, cotangent)
    d_act = times_rows(cotangent, lax.all_gather(w_down, ("dp", "fsdp"), axis=0, tiled=True))
    d_act = d_act * live_rows
    d_gate = d_act * up_val * gate_sig * (1.0 + gate_val * (1.0 - gate_sig))
    d_up = d_act * gate_val * gate_sig
    d_gu_low = jnp.concatenate([d_gate, d_up], axis=1).astype(jnp.bfloat16)
    d_hidden_two = times_rows(
        d_gu_low, lax.all_gather(w_gate_up, ("dp", "fsdp"), axis=0, tiled=True)
    )
    d_gain_two = jnp.sum(d_hidden_two * normal_two, axis=0)
    d_w_down, d_w_gate_up, d_ffn_gain = to_owners(
        (down_term, outer_sum(hidden_two, d_gu_low), d_gain_two)
    )
    grad_mid = grad_out + norm_back(
        normal_two, factor_two, d_hidden_two * gain_two.astype(jnp.float32)
    )
    grad_mid_low = grad_mid.astype(jnp.bfloat16)
    d_w_mix = outer_sum(mixed_low, grad_mid_low)
    d_mixed = times_rows(grad_mid_low, lax.all_gather(w_out, ("dp", "fsdp"), axis=0, tiled=True))
    d_mixed3 = (d_mixed * live_rows).reshape(tok_rows, head_count, head_size)
    d_att_low = (d_mixed3 * out_gate).astype(jnp.bfloat16)
    d_gate_pre = d_mixed3 * attended * out_gate * (1.0 - out_gate)
    scores_again = score_block(q_low, k_low, decay_sum, scale_qk)
    prob_again = jnp.exp(jnp.where(allowed[None], scores_again - log_total, NEG))
    prob_low = prob_again.astype(jnp.bfloat16)
    d_value = jnp.einsum("hts,thd->shd", prob_low, d_att_low, preferred_element_type=jnp.float32)
    d_prob = jnp.einsum("thd,shd->hts", d_att_low, v_low, preferred_element_type=jnp.float32)
    d_scores = prob_again * (d_prob - jnp.sum(prob_again * d_prob, axis=-1, keepdims=True))
    ds_low = d_scores.astype(jnp.bfloat16)
    d_q_hat = (
        jnp.einsum("hts,shd->thd", ds_low, k_low, preferred_element_type=jnp.float32) * scale_qk
    )
    d_k_hat = (
        jnp.einsum("hts,thd->shd", ds_low, q_low, preferred_element_type=jnp.float32) * scale_qk
    )
    d_decay = (
        jnp.sum(ds_low, axis=-1, dtype=jnp.float32) - jnp.sum(ds_low, axis=-2, dtype=jnp.float32)
    ).T
    d_q_gain = jnp.sum(d_q_hat * q_normal, axis=0).reshape(width)
    d_query = norm_back(q_normal, q_factor, d_q_hat * gain_q3)
    d_k_gain = jnp.sum(d_k_hat * k_normal, axis=0).reshape(width)
    d_key_mixed = norm_back(k_normal, k_factor, d_k_hat * gain_k3)
    d_key, d_key_mix = mix_back(d_key_mixed, key_mix, key_raw, key_prev, same_prev)
    d_val, d_value_mix = mix_back(d_value, value_mix, value_raw, value_prev, same_prev)
    d_log_keep = jnp.cumsum(d_decay[::-1], axis=0)[::-1]
    d_forget = d_log_keep * jax.nn.sigmoid(-forget_pre)
    d_rates = jnp.concatenate([d_forget, d_key_mix, d_value_mix], axis=1)
    d_rate_bias = lax.psum(jnp.sum(d_rates, axis=0), ("dp", "fsdp"))
    d_rates_low = d_rates.astype(jnp.bfloat16)
    d_proj_low = jnp.concatenate(
        [
            d_query.reshape(tok_rows, width),
            d_key.reshape(tok_rows, width),
            d_val.reshape(tok_rows, width),
            d_gate_pre.reshape(tok_rows, width),
        ],
        axis=1,
    ).astype(jnp.bfloat16)
    d_w_out, d_q_gain_own, d_k_gain_own = to_owners((d_w_mix, d_q_gain, d_k_gain))
    piece_proj = lax.all_gather(w_attn_in, ("dp", "fsdp"), axis=0, tiled=True)
    piece_rate = lax.all_gather(w_rates, ("dp", "fsdp"), axis=0, tiled=True)
    d_hidden_one = times_rows(d_proj_low, piece_proj) + times_rows(d_rates_low, piece_rate)
    d_gain_one = jnp.sum(d_hidden_one * normal_one, axis=0)
    d_w_attn_in, d_w_rates, d_norm_gain = to_owners(
        (outer_sum(hidden_one, d_proj_low), outer_sum(hidden_one, d_rates_low), d_gain_one)
    )
    d_tokens = grad_mid + norm_back(
        normal_one, factor_one, d_hidden_one * gain_one.astype(jnp.float32)
    )
    return (
        layer_out,
        d_tokens,
        d_norm_gain,
        d_w_attn_in,
        d_w_rates,
        d_rate_bias,
        d_q_gain_own,
        d_k_gain_own,
        d_w_out,
        d_ffn_gain,
        d_w_gate_up,
        d_w_down,
    )


def solution(mesh):
    in_specs = (
        P(("dp", "fsdp"), None),
        P(("dp", "fsdp")),
        P(("dp", "fsdp")),
        P(("dp", "fsdp"), None),
        P(("dp", "fsdp"), None),
        P(),
        P(("dp", "fsdp")),
        P(("dp", "fsdp")),
        P(("dp", "fsdp"), None),
        P(("dp", "fsdp")),
        P(("dp", "fsdp"), None),
        P(("dp", "fsdp"), None),
        P(("dp", "fsdp"), None),
    )
    out_specs = (
        P(("dp", "fsdp"), None),
        P(("dp", "fsdp"), None),
        P(("dp", "fsdp")),
        P(("dp", "fsdp"), None),
        P(("dp", "fsdp"), None),
        P(),
        P(("dp", "fsdp")),
        P(("dp", "fsdp")),
        P(("dp", "fsdp"), None),
        P(("dp", "fsdp")),
        P(("dp", "fsdp"), None),
        P(("dp", "fsdp"), None),
    )
    return jax.shard_map(body, mesh=mesh, in_specs=in_specs, out_specs=out_specs, check_vma=False)
```

profile of v0, /device:TPU:0, one launch (start us, length us, event | category | flops | bytes accessed | tf_op | source)
XLA Modules:
  0.0 2588.8 jit_solution(10549024077756973587)
XLA Ops:
  12.7 43.4 %all-reduce.12 = (bf16[1536]{0:T(1024)(128)(2,1)S(1)}, bf16[1536]{0:T(1024)(128)(2,1)S(1)}, bf16[1536]{0:T(1024)(128)(2,1)S(1)}, bf16[1536]{0:T(1024)(128)(2,1)S(1)}) all-reduce(bf16[1536]{0:T(1024)(128)(2,1)S(1)} %dynamic-update-slice, bf16[1536]{0:T(1024)(128)(2,1)S(1)} %dynamic-update-slice.1, ...), channel_id=1, replica_groups=mesh['dp'=8,'fsdp'=4] {'dp','fsdp'}, use_global_device_ids=true, to_apply=%add.4 | all-reduce | flops 6144 | bytes 24576
  56.3 74.1 %all_gather.33 = bf16[1536,72]{1,0:T(8,128)(2,1)S(1)} all-gather(bf16[48,72]{1,0:T(8,128)(2,1)S(1)} %copy-done.50), channel_id=1, replica_groups=mesh['dp'=8,'fsdp'=4] {'dp','fsdp'}, dimensions={0}, use_global_device_ids=true | all-gather | bytes 228096 | tf_op jit(solution)/shard_map/all_gather | solution.py:117
  134.2 8.8 all-gather.5.cloned.1.call-done
  143.0 9.6 fusion.70
  190.3 18.4 all-gather.7.cloned.1.call-done
  214.3 150.7 %all-gather.9.cloned.1.call-done = bf16[1536,8192]{1,0:T(8,128)(2,1)} async-done(((bf16[48,8192]{1,0:T(8,128)(2,1)}), bf16[1536,8192]{1,0:T(8,128)(2,1)}) %all-gather.9.cloned.1.call-update) | async-done | bytes 25165840 | tf_op jit(solution)/shard_map/all_gather | solution.py:177
  365.1 14.2 fusion.67
  379.3 82.8 %all-gather.11.cloned.1.call-done = bf16[4096,1536]{1,0:T(8,128)(2,1)} async-done(((bf16[128,1536]{1,0:T(8,128)(2,1)}), bf16[4096,1536]{1,0:T(8,128)(2,1)}) %all-gather.11.cloned.1.call-update) | async-done | bytes 12582928 | tf_op jit(solution)/shard_map/all_gather | solution.py:190
  462.1 11.2 multiply_convert_fusion.2
  473.2 13.9 multiply_reduce_fusion.1
  529.3 22.3 fusion.8
  563.1 16.6 fusion.40
  579.7 11.2 fusion.20
  607.3 10.1 fusion.76
  617.4 26.1 %reshape.316 = f32[32,196608]{1,0:T(8,128)} reshape(f32[4096,1536]{1,0:T(8,128)} %fusion.76) | data formatting | bytes 50331648 | tf_op jit(solution)/shard_map/reshape | solution.py:64
  643.5 35.9 %reshape.309 = f32[32,294912]{1,0:T(8,128)} reshape(f32[1536,6144]{1,0:T(8,128)} %fusion.40) | data formatting | bytes 75497472 | tf_op jit(solution)/shard_map/reshape | solution.py:64
  679.4 45.4 %reshape.317 = f32[32,393216]{1,0:T(8,128)} reshape(f32[1536,8192]{1,0:T(8,128)} %fusion.8) | data formatting | bytes 100663296 | tf_op jit(solution)/shard_map/reshape | solution.py:64
  727.5 26.0 %pad_maximum_fusion.1 = f32[32,298416]{1,0:T(8,128)} fusion(f32[32,48]{1,0:T(8,128)S(1)} %reshape.311, f32[32,3456]{1,0:T(8,128)S(1)} %copy-done.31, f32[32,294912]{1,0:T(8,128)} %reshape.309), kind=kLoop, calls=%fused_computation.1 | loop fusion | flops 19098624 | bytes 76394496 | tf_op jit(solution)/shard_map/concatenate | solution.py:64
  753.5 50.0 %pad_maximum_fusion = f32[32,589872]{1,0:T(8,128)} fusion(f32[32,48]{1,0:T(8,128)S(1)} %reshape.318, f32[32,393216]{1,0:T(8,128)} %reshape.317, f32[32,196608]{1,0:T(8,128)} %reshape.316), kind=kLoop, calls=%fused_computation | loop fusion | flops 37751808 | bytes 151007232 | tf_op jit(solution)/shard_map/concatenate | solution.py:64
  804.4 40.8 %psum.7 = f32[72]{0:T(128)} all-reduce(f32[72]{0:T(128)S(1)} %fusion.47), channel_id=1, replica_groups=mesh['dp'=8,'fsdp'=4] {'dp','fsdp'}, use_global_device_ids=true, to_apply=%region_24.25 | all-reduce | flops 72 | bytes 576 | tf_op jit(solution)/shard_map/psum | solution.py:243
  856.3 1670.4 %all-reduce.15.cloned.1.call-done = (f32[32,298416]{1,0:T(8,128)}, f32[32,73824]{1,0:T(8,128)}, f32[32,589872]{1,0:T(8,128)}) async-done(((f32[32,298416]{1,0:T(8,128)}, f32[32,73824]{1,0:T(8,128)}, f32[32,589872]{1,0:T(8,128)}), (f32[32,298416]{1,0:T(8,128)}, f32[32,73824]{1,0:T(8,128)}, f32[32,589872]{1,0:T(8,128)})) %all-reduce.15.cloned.1.call-update) | async-done | bytes 123150352
  2526.7 14.0 dynamic-slice_reduce_fusion.1
  2542.0 10.0 dynamic-slice_reduce_fusion.2
  2559.4 18.8 dynamic-slice_reduce_fusion
  (246 shorter events, 149.1 us)
Async XLA Ops:
  7.2 49.1 %copy-start.50 = (bf16[48,72]{1,0:T(8,128)(2,1)S(1)}, bf16[48,72]{1,0:T(8,128)(2,1)}, u32[]{:S(2)}) copy-start(bf16[48,72]{1,0:T(8,128)(2,1)} %param.17) | copy-start | bytes 20740
  7.2 123.2 %copy-start.12 = (bf16[256,1536]{1,0:T(8,128)(2,1)S(1)}, bf16[256,1536]{1,0:T(8,128)(2,1)}, u32[]{:S(2)}) copy-start(bf16[256,1536]{1,0:T(8,128)(2,1)} %param.13) | copy-start | bytes 2359300
  7.3 124.0 %copy-start.62 = (f32[72]{0:T(128)S(1)}, f32[72]{0:T(128)}, u32[]{:S(2)}) copy-start(f32[72]{0:T(128)} %param.18) | copy-start | bytes 868
  7.3 135.8 %all-gather.5.cloned.1.call-start = ((), (), s32[]{:S(2)}) async-start(), calls=%async_computation | async-start | bytes 19464192 | tf_op jit(solution)/shard_map/all_gather | solution.py:116
  8.0 200.7 %all-gather.7.cloned.1.call-start = ((), (), s32[]{:S(2)}) async-start(), calls=%async_computation.1 | async-start | bytes 4866048 | tf_op jit(solution)/shard_map/all_gather | solution.py:169
  8.7 356.3 %all-gather.9.cloned.1.call-start = ((), (), s32[]{:S(2)}) async-start(), calls=%async_computation.2 | async-start | bytes 25952256 | tf_op jit(solution)/shard_map/all_gather | solution.py:177
  9.5 452.6 %all-gather.11.cloned.1.call-start = ((), (), s32[]{:S(2)}) async-start(), calls=%async_computation.3 | async-start | bytes 12976128 | tf_op jit(solution)/shard_map/all_gather | solution.py:190
  10.1 2516.7 %all-reduce.15.cloned.1.call-start = ((), (), s32[]{:S(2)}) async-start(), calls=%async_computation.4 | async-start | bytes 246349824
  11.1 162.8 %copy-start.48 = (f32[256]{0:T(256)}, f32[256]{0:T(256)S(1)}, u32[]{:S(2)}) copy-start(f32[256]{0:T(256)S(1)} %add_convert_fusion.3) | copy-start | bytes 3076
  56.1 523.6 %copy-start.34 = (f32[1536]{0:T(1024)}, f32[1536]{0:T(1024)S(1)}, u32[]{:S(2)}) copy-start(f32[1536]{0:T(1024)S(1)} %convert_element_type.86) | copy-start | bytes 18436
  131.2 448.5 %copy-start.44 = (f32[256]{0:T(256)}, f32[256]{0:T(256)S(1)}, u32[]{:S(2)}) copy-start(f32[256]{0:T(256)S(1)} %add_rsqrt_fusion.3) | copy-start | bytes 3076
  133.4 75.3 %copy-start.53 = (f32[256]{0:T(256)}, f32[256]{0:T(256)S(1)}, u32[]{:S(2)}) copy-start(f32[256]{0:T(256)S(1)} %compare_convert_fusion) | copy-start | bytes 3076
  365.1 97.0 %copy-start.54 = (f32[256]{0:T(256)S(1)}, f32[256]{0:T(256)}, u32[]{:S(2)}) copy-start(f32[256]{0:T(256)} %copy-done.53) | copy-start | bytes 3076
  473.2 13.9 copy-start.30
  473.2 13.9 copy-start.24
  529.3 22.3 copy-start.52
  563.1 16.6 copy-start.26
  563.1 16.6 copy-start.27
  679.4 48.1 %copy-start.31 = (f32[32,3456]{1,0:T(8,128)S(1)}, f32[32,3456]{1,0:T(8,128)}, u32[]{:S(2)}) copy-start(f32[32,3456]{1,0:T(8,128)} %reshape.310) | copy-start | bytes 1327108
  803.6 41.7 %copy-start.56 = (f32[256]{0:T(256)S(1)}, f32[256]{0:T(256)}, u32[]{:S(2)}) copy-start(f32[256]{0:T(256)} %get-tuple-element.21) | copy-start | bytes 3076
  803.6 41.7 %copy-start.4 = (f32[256,1536]{1,0:T(8,128)S(1)}, f32[256,1536]{1,0:T(8,128)}, u32[]{:S(2)}) copy-start(f32[256,1536]{1,0:T(8,128)} %copy-done.2) | copy-start | bytes 4718596
  803.6 41.7 %copy-start.15 = (bf16[256,1536]{1,0:T(8,128)(2,1)S(1)}, bf16[256,1536]{1,0:T(8,128)(2,1)}, u32[]{:S(2)}) copy-start(bf16[256,1536]{1,0:T(8,128)(2,1)} %param.13) | copy-start | bytes 2359300
  803.6 41.7 %copy-start.35 = (f32[1536]{0:T(1024)S(1)}, f32[1536]{0:T(1024)}, u32[]{:S(2)}) copy-start(f32[1536]{0:T(1024)} %copy-done.34) | copy-start | bytes 18436
  803.6 41.7 %copy-start.45 = (f32[256]{0:T(256)S(1)}, f32[256]{0:T(256)}, u32[]{:S(2)}) copy-start(f32[256]{0:T(256)} %copy-done.44) | copy-start | bytes 3076
  (46 other events, 162.0 us)
Sparse Core Ops, SparseCore 0:
  10.9 132.0 all-gather.4
  145.8 62.8 all-gather.6
  211.6 153.4 all-gather.8
  367.8 94.2 all-gather.10
  803.8 1722.8 all-reduce.14
where the time goes:
time: 2600 us; the launch traced here: 2590 us
  waiting for transfers between devices  1930 us (74%)
  local copies, waits for them, and re-layouts  216 us (8%)
  blocking collectives  158 us (6%)
  matrix products  156 us (6%)
  other arithmetic  109 us (4%)
    unnamed x6, waiting for transfers between devices  1670 us
    all_gather x1, waiting for transfers between devices, body(): piece_gu = lax.all_gather(w_gate_up, ('dp', 'fsdp'), axis=0, tiled=True)  151 us
    reshape x7, local copies, waits for them, and re-layouts, to_owners(): term.reshape(shares, -1)  118 us
    all_gather x1, waiting for transfers between devices, body(): lax.all_gather(w_down, ('dp', 'fsdp'), axis=0, tiled=True)  82.8 us
    concatenate x2, other arithmetic, to_owners(): jnp.concatenate([term.reshape(shares, -1) for term in gradient_terms], ax...  76 us
    all_gather x1, blocking collectives, body(): piece_rate = lax.all_gather(w_rates, ('dp', 'fsdp'), axis=0, tiled=True)  74.1 us
    dot_general x5, matrix products, outer_sum(): lax.dot_general(left_side, right_side, (((0,), (0,)), ((), ())), preferre...  55.6 us
  transfers between devices with their start and end apart: 5, of which 5 were waited for; matrix products, arithmetic and copies ran while one was open for 3% of the time, Pallas kernels for 0%

commit v1 on v0

v1 whole, which is shorter than its diff:
```python
import functools

import jax
import jax.numpy as jnp
from jax import lax
from jax.experimental import pallas as pl
from jax.experimental.pallas import tpu as pltpu
from jax.sharding import Mesh
from jax.sharding import PartitionSpec as P

HEADS = 24
HEAD_DIM = 64
EPS = 1e-06
NEG = -1e30
TP = 8
OWN = HEADS // TP
BLOCK = OWN * HEAD_DIM
CORE = 4 * BLOCK
EXTRA = 128
WIDE = CORE + EXTRA
RATES = 3 * OWN
GAIN_AT = RATES
LENS_AT = RATES + 4
OFFSETS = (0, 2, 4, 6, 1, 3, 5, 7)
F32 = jnp.float32
BF16 = jnp.bfloat16


def flip(array, offset):
    return lax.ppermute(array, "tp", [(i, i ^ offset) for i in range(TP)])


def gather_rows(own):
    half = jnp.concatenate([own, flip(own, 2), flip(own, 4), flip(own, 6)], axis=0)
    return jnp.concatenate([half, flip(half, 1)], axis=0)


def scatter_rows(part):
    rows = part.shape[0] // TP
    half = part[: 4 * rows].astype(F32) + flip(part[4 * rows :], 1).astype(F32)
    low = half[rows:].astype(BF16)
    return (
        half[:rows]
        + flip(low[:rows], 2).astype(F32)
        + flip(low[rows : 2 * rows], 4).astype(F32)
        + flip(low[2 * rows :], 6).astype(F32)
    )


def normed(field_in):
    factor = lax.rsqrt(jnp.mean(field_in * field_in, axis=-1, keepdims=True) + EPS)
    return field_in * factor, factor


def norm_back(normal, factor, grad_in):
    return factor * (grad_in - normal * jnp.mean(grad_in * normal, axis=-1, keepdims=True))


def dot(a, b, dims=((1,), (0,)), precision=None):
    return lax.dot_general(a, b, (dims, ((), ())), precision=precision, preferred_element_type=F32)


def columns_out(weight, blocks):
    rows = weight.shape[0]
    cut = weight.reshape(rows, blocks, TP, -1)
    return cut.transpose(2, 0, 1, 3).reshape(TP, rows, -1)


def columns_in(cut, blocks):
    rows = cut.shape[1]
    return cut.reshape(TP, rows, blocks, -1).transpose(1, 2, 0, 3).reshape(rows, -1)


def own_share(part, share):
    columns = part.shape[1]
    part = part.reshape(TP, share, -1, columns).transpose(1, 0, 2, 3).reshape(-1, columns)
    return lax.psum_scatter(part, "sh", scatter_dimension=0, tiled=True).reshape(TP, -1, columns)


def head_masks(rows, width):
    lane = lax.broadcasted_iota(jnp.int32, (rows, width), 1)
    return [(lane >= h * HEAD_DIM) & (lane < (h + 1) * HEAD_DIM) for h in range(OWN)]


def spread(values, width, rows):
    lane = lax.broadcasted_iota(jnp.int32, (rows, width), 1)
    out = jnp.broadcast_to(values[OWN - 1], (rows, width))
    for h in range(OWN - 2, -1, -1):
        out = jnp.where(lane < (h + 1) * HEAD_DIM, values[h], out)
    return out


def head_sums(field_in, masks):
    return [jnp.sum(jnp.where(m, field_in, 0.0), axis=-1, keepdims=True) for m in masks]


def places_of(lens_ref, bucket, rows):
    ends = []
    total = jnp.int32(0)
    for j in range(lens_ref.shape[1]):
        total = total + lens_ref[bucket, j]
        ends.append(total)

    def segment(place):
        seg = jnp.zeros(place.shape, jnp.int32)
        for end in ends:
            seg = seg + (end <= place).astype(jnp.int32)
        return seg

    col = lax.broadcasted_iota(jnp.int32, (rows, 1), 0)
    row = lax.broadcasted_iota(jnp.int32, (1, rows), 1)
    seg_col = segment(col)
    allowed = (row <= col) & (segment(row) == seg_col)
    live = (col < total).astype(F32)
    same_prev = ((col > 0) & (seg_col == segment(col - 1))).astype(F32)
    return allowed, live, same_prev


def front(lens_ref, proj_ref, bias_ref, gains_ref, bucket):
    rows = proj_ref.shape[0]
    allowed, live, same_prev = places_of(lens_ref, bucket, rows)
    q = proj_ref[:, 0:BLOCK]
    k = proj_ref[:, BLOCK : 2 * BLOCK]
    v = proj_ref[:, 2 * BLOCK : 3 * BLOCK]
    og = proj_ref[:, 3 * BLOCK : CORE]
    rate = proj_ref[:, CORE:WIDE] + bias_ref[0:1, :]
    sig = jax.nn.sigmoid(rate)
    log_keep = jnp.minimum(rate, 0.0) - jnp.log1p(jnp.exp(-jnp.abs(rate)))
    tri = (
        lax.broadcasted_iota(jnp.int32, (rows, rows), 1)
        <= lax.broadcasted_iota(jnp.int32, (rows, rows), 0)
    ).astype(F32)
    decay = dot(tri, log_keep, precision=lax.Precision.HIGHEST)
    decay_t = decay.T
    masks = head_masks(rows, BLOCK)
    ak = spread([sig[:, OWN + h : OWN + h + 1] for h in range(OWN)], BLOCK, rows)
    av = spread([sig[:, 2 * OWN + h : 2 * OWN + h + 1] for h in range(OWN)], BLOCK, rows)
    k_prev = pltpu.roll(k, 1, 0) * same_prev
    v_prev = pltpu.roll(v, 1, 0) * same_prev
    ks = ak * k_prev + (1.0 - ak) * k
    vs = av * v_prev + (1.0 - av) * v

    def head_norm(u):
        sums = head_sums(u * u, masks)
        factor = spread([lax.rsqrt(s * (1.0 / HEAD_DIM) + EPS) for s in sums], BLOCK, rows)
        return u * factor, factor

    qn, rq = head_norm(q)
    kn, rk = head_norm(ks)
    q_gain, k_gain = gains_ref[0:1, 0:BLOCK], gains_ref[1:2, 0:BLOCK]
    qb = (qn * q_gain).astype(BF16)
    kb = (kn * k_gain).astype(BF16)
    vb = vs.astype(BF16)
    return dict(
        rows=rows, allowed=allowed, live=live, same_prev=same_prev, k=k, v=v, og=og, rate=rate, sig=sig,
        decay=decay, decay_t=decay_t, masks=masks, ak=ak, av=av, k_prev=k_prev, v_prev=v_prev,
        qn=qn, rq=rq, kn=kn, rk=rk, q_gain=q_gain, k_gain=k_gain, qb=qb, kb=kb, vb=vb, tri=tri,
    )


def scores_of(f, h):
    qm = jnp.where(f["masks"][h], f["qb"], jnp.zeros_like(f["qb"]))
    s = dot(qm, f["kb"], ((1,), (1,))) * HEAD_DIM**-0.5
    s = s + f["decay"][:, h : h + 1] - f["decay_t"][h : h + 1, :]
    return jnp.where(f["allowed"], s, NEG)


def attn_fwd_kernel(lens_ref, proj_ref, bias_ref, gains_ref, mixed_ref, att_ref, lse_ref):
    f = front(lens_ref, proj_ref, bias_ref, gains_ref, pl.program_id(0))
    rows = f["rows"]
    lane = lax.broadcasted_iota(jnp.int32, (rows, EXTRA), 1)
    att = jnp.zeros((rows, BLOCK), F32)
    lse_all = jnp.zeros((rows, EXTRA), F32)
    for h in range(OWN):
        s = scores_of(f, h)
        top = jnp.max(s, axis=-1, keepdims=True)
        e = jnp.exp(s - top)
        total = jnp.sum(e, axis=-1, keepdims=True)
        prob = (e / total).astype(BF16)
        att = att + dot(prob, jnp.where(f["masks"][h], f["vb"], jnp.zeros_like(f["vb"])))
        lse_all = jnp.where(lane == h, top + jnp.log(total), lse_all)
    att_ref[...] = att
    lse_ref[...] = lse_all
    mixed_ref[...] = (att * jax.nn.sigmoid(f["og"]) * f["live"]).astype(BF16)


def attn_bwd_kernel(
    lens_ref, proj_ref, bias_ref, gains_ref, att_ref, lse_ref, grad_ref, w_ref, dp_ref, sums_ref
):
    bucket = pl.program_id(0)
    f = front(lens_ref, proj_ref, bias_ref, gains_ref, bucket)
    rows, masks = f["rows"], f["masks"]
    dm = dot(grad_ref[...], w_ref[...], ((1,), (1,))) * f["live"]
    g = jax.nn.sigmoid(f["og"])
    dab = (dm * g).astype(BF16)
    dog = dm * att_ref[...] * g * (1.0 - g)
    zero = jnp.zeros((rows, BLOCK), BF16)
    lane = lax.broadcasted_iota(jnp.int32, (rows, EXTRA), 1)
    dqb = jnp.zeros((rows, BLOCK), F32)
    dkb = jnp.zeros((rows, BLOCK), F32)
    dvb = jnp.zeros((rows, BLOCK), F32)
    dc = jnp.zeros((rows, EXTRA), F32)
    for h in range(OWN):
        s = scores_of(f, h)
        p = jnp.exp(s - lse_ref[:, h : h + 1])
        dab_h = jnp.where(masks[h], dab, zero)
        dvb = dvb + dot(p.astype(BF16), dab_h, ((0,), (0,)))
        dp = dot(dab_h, f["vb"], ((1,), (1,)))
        ds = p * (dp - jnp.sum(p * dp, axis=-1, keepdims=True))
        dsb = ds.astype(BF16)
        dqb = dqb + dot(dsb, jnp.where(masks[h], f["kb"], zero))
        dkb = dkb + dot(dsb, jnp.where(masks[h], f["qb"], zero), ((0,), (0,)))
        ones = (lane == h).astype(BF16)
        dc = dc + dot(dsb, ones) - dot(dsb, ones, ((0,), (0,)))
    dqb = dqb * HEAD_DIM**-0.5
    dkb = dkb * HEAD_DIM**-0.5

    def back(n, r, e):
        means = spread([s * (1.0 / HEAD_DIM) for s in head_sums(e * n, masks)], BLOCK, rows)
        return r * (e - n * means)

    dq = back(f["qn"], f["rq"], dqb * f["q_gain"])
    dks = back(f["kn"], f["rk"], dkb * f["k_gain"])
    last = lax.broadcasted_iota(jnp.int32, (rows, 1), 0) == rows - 1

    def mix_back(grad, rate, cur, prev):
        ahead = pltpu.roll(rate * grad * f["same_prev"], rows - 1, 0)
        d_cur = (1.0 - rate) * grad + jnp.where(last, 0.0, ahead)
        return d_cur, head_sums(grad * (prev - cur), masks)

    dk, dak = mix_back(dks, f["ak"], f["k"], f["k_prev"])
    dv, dav = mix_back(dvb, f["av"], f["v"], f["v_prev"])
    keep = dot(f["tri"], dc, ((0,), (0,)), precision=lax.Precision.HIGHEST)
    sig = f["sig"]
    drate = keep * (1.0 - sig)
    slope = sig * (1.0 - sig)
    for h in range(OWN):
        drate = jnp.where(lane == OWN + h, dak[h] * slope, drate)
        drate = jnp.where(lane == 2 * OWN + h, dav[h] * slope, drate)
    drate = jnp.where(lane < RATES, drate, 0.0)
    dp_ref[:, 0:BLOCK] = dq.astype(BF16)
    dp_ref[:, BLOCK : 2 * BLOCK] = dk.astype(BF16)
    dp_ref[:, 2 * BLOCK : 3 * BLOCK] = dv.astype(BF16)
    dp_ref[:, 3 * BLOCK : CORE] = dog.astype(BF16)
    dp_ref[:, CORE:WIDE] = drate.astype(BF16)

    @pl.when(bucket == 0)
    def _():
        sums_ref[...] = jnp.zeros_like(sums_ref)

    sums_ref[0:1, 0:BLOCK] += jnp.sum(dqb * f["qn"], axis=0, keepdims=True)
    sums_ref[1:2, 0:BLOCK] += jnp.sum(dkb * f["kn"], axis=0, keepdims=True)
    sums_ref[2:3, 0:EXTRA] += jnp.sum(drate, axis=0, keepdims=True)


SMEM = pl.BlockSpec(memory_space=pltpu.SMEM)


def rows_spec(rows, width):
    return pl.BlockSpec((rows, width), lambda i: (i, 0))


def whole_spec(shape):
    return pl.BlockSpec(shape, lambda i: (0,) * len(shape))


def attn_fwd(lens, proj, bias, gains):
    buckets = lens.shape[0]
    rows = proj.shape[0] // buckets
    total = proj.shape[0]
    return pl.pallas_call(
        attn_fwd_kernel,
        grid=(buckets,),
        in_specs=[SMEM, rows_spec(rows, WIDE), whole_spec(bias.shape), whole_spec(gains.shape)],
        out_specs=[rows_spec(rows, BLOCK), rows_spec(rows, BLOCK), rows_spec(rows, EXTRA)],
        out_shape=[
            jax.ShapeDtypeStruct((total, BLOCK), BF16),
            jax.ShapeDtypeStruct((total, BLOCK), F32),
            jax.ShapeDtypeStruct((total, EXTRA), F32),
        ],
        compiler_params=pltpu.CompilerParams(vmem_limit_bytes=40 * 2**20),
        name="attn_fwd",
    )(lens, proj, bias, gains)


def attn_bwd(lens, proj, bias, gains, att, lse, grad, weight):
    buckets = lens.shape[0]
    rows = proj.shape[0] // buckets
    total = proj.shape[0]
    return pl.pallas_call(
        attn_bwd_kernel,
        grid=(buckets,),
        in_specs=[
            SMEM,
            rows_spec(rows, WIDE),
            whole_spec(bias.shape),
            whole_spec(gains.shape),
            rows_spec(rows, BLOCK),
            rows_spec(rows, EXTRA),
            rows_spec(rows, grad.shape[1]),
            whole_spec(weight.shape),
        ],
        out_specs=[rows_spec(rows, WIDE), whole_spec((8, 2 * EXTRA))],
        out_shape=[
            jax.ShapeDtypeStruct((total, WIDE), BF16),
            jax.ShapeDtypeStruct((8, 2 * EXTRA), F32),
        ],
        compiler_params=pltpu.CompilerParams(vmem_limit_bytes=40 * 2**20),
        name="attn_bwd",
    )(lens, proj, bias, gains, att, lse, grad, weight)


def body(
    tokens,
    doc_lengths,
    norm_gain,
    w_attn_in,
    w_rates,
    rate_bias,
    q_gain,
    k_gain,
    w_out,
    ffn_gain,
    w_gate_up,
    w_down,
    cotangent,
):
    place = lax.axis_index("tp")
    share = lax.axis_size("sh")
    tok_rows, width = tokens.shape
    own_rows = w_attn_in.shape[0]
    ff_own = w_gate_up.shape[1] // (2 * TP)
    offsets = jnp.array(OFFSETS, jnp.int32)

    gains = jnp.stack([norm_gain, q_gain, k_gain, ffn_gain], axis=1)
    lens_pad = jnp.zeros((own_rows, doc_lengths.shape[0]), BF16).at[0].set(doc_lengths.astype(BF16))
    beside = jnp.concatenate([gains, lens_pad], axis=1)
    beside = jnp.broadcast_to(beside[None], (TP,) + beside.shape)
    pad = EXTRA - RATES - beside.shape[2]
    out_in = jnp.concatenate(
        [
            columns_out(w_attn_in, 4),
            columns_out(w_rates, 3),
            beside,
            jnp.zeros((TP, own_rows, pad), BF16),
        ],
        axis=2,
    )
    got_in = lax.all_to_all(out_in, "tp", 0, 0, tiled=True)
    w_in = lax.all_gather(got_in, "sh", axis=1).reshape(width, WIDE)
    w_mix = lax.all_gather(w_out, "sh", axis=0, tiled=True)
    got_gu = lax.all_to_all(columns_out(w_gate_up, 2), "tp", 0, 0, tiled=True)
    w_gu = lax.all_gather(got_gu, "sh", axis=1).reshape(width, 2 * ff_own)
    w_dn = lax.all_gather(w_down, "sh", axis=0, tiled=True)

    lens_all = got_in[:, 0, CORE + LENS_AT : CORE + LENS_AT + doc_lengths.shape[0]].astype(jnp.int32)
    lens = lens_all[place ^ offsets]
    gains_all = w_in[:, CORE + GAIN_AT : CORE + GAIN_AT + 4].astype(F32).T
    gain_one = gains_all[0:1]
    gain_two = gains_all[3:4]
    gain_heads = lax.dynamic_slice(gains_all[1:3], (0, place * BLOCK), (2, BLOCK))
    gain_heads = jnp.pad(gain_heads, ((0, 6), (0, 2 * EXTRA - BLOCK)))
    bias = lax.dynamic_index_in_dim(rate_bias.reshape(3, TP, OWN), place, 1, False).reshape(1, RATES)
    bias = jnp.pad(bias, ((0, 7), (0, EXTRA - RATES)))

    tok_all = gather_rows(tokens)
    cot_all = gather_rows(cotangent)
    n1_all, _ = normed(tok_all.astype(F32))
    h1_all = (n1_all * gain_one).astype(BF16)
    proj = dot(h1_all, w_in)
    mixed, att, lse = attn_fwd(lens, proj, bias, gain_heads)
    x2 = tokens.astype(F32) + scatter_rows(dot(mixed, w_mix).astype(BF16))
    n2, r2 = normed(x2)
    h2_all = gather_rows((n2 * gain_two).astype(BF16))

    ends = jnp.sum(lens, axis=1)
    live = (jnp.arange(tok_rows)[None, :] < ends[:, None]).astype(F32).reshape(-1, 1)
    gu = dot(h2_all, w_gu)
    gate, up = gu[:, :ff_own], gu[:, ff_own:]
    sg = jax.nn.sigmoid(gate)
    ab = (gate * sg * up * live).astype(BF16)
    da = dot(cot_all, w_dn, ((1,), (1,))) * live
    dgu = jnp.concatenate([da * up * sg * (1.0 + gate * (1.0 - sg)), da * gate * sg], axis=1).astype(BF16)
    dh2 = scatter_rows(dot(dgu, w_gu, ((1,), (1,))).astype(BF16))
    layer_out = (x2 + scatter_rows(dot(ab, w_dn).astype(BF16))).astype(BF16)
    dw_dn = dot(ab, cot_all, ((0,), (0,))).astype(BF16)
    dw_gu = dot(h2_all, dgu, ((0,), (0,))).astype(BF16)
    d_w_down = lax.psum_scatter(dw_dn, "sh", scatter_dimension=0, tiled=True).astype(F32)
    dw_gu = own_share(dw_gu, share)
    d_w_gate_up = columns_in(lax.all_to_all(dw_gu, "tp", 0, 0, tiled=True), 2).astype(F32)

    dx2 = cotangent.astype(F32) + norm_back(n2, r2, dh2 * gain_two)
    dxb_all = gather_rows(dx2.astype(BF16))
    dw_mix = dot(mixed, dxb_all, ((0,), (0,))).astype(BF16)
    d_w_out = lax.psum_scatter(dw_mix, "sh", scatter_dimension=0, tiled=True).astype(F32)
    dp, sums = attn_bwd(lens, proj, bias, gain_heads, att, lse, dxb_all, w_mix)
    dw_in = dot(h1_all, dp, ((0,), (0,))).astype(BF16)

    at_row = jnp.arange(width)
    in_own = (at_row // BLOCK == place)[:, None]
    qk_sums = jnp.tile(sums[0:2, 0:BLOCK].T, (TP, 1))
    qk_sums = jnp.where(in_own, qk_sums, 0.0)
    bias_sums = jnp.pad(sums[2, 0:RATES], (0, own_rows - RATES))
    bias_sums = jnp.tile(bias_sums[:, None], (width // own_rows, 1))
    beside = jnp.concatenate([qk_sums, bias_sums], axis=1).astype(BF16)
    dw_in = jnp.concatenate(
        [dw_in[:, : CORE + RATES], beside, jnp.zeros((width, EXTRA - RATES - 3), BF16)], axis=1
    )
    dw_in = own_share(dw_in, share)
    dw_in = lax.all_to_all(dw_in, "tp", 0, 0, tiled=True)
    d_w_attn_in = columns_in(dw_in[:, :, :CORE], 4).astype(F32)
    d_w_rates = columns_in(dw_in[:, :, CORE : CORE + RATES], 3).astype(F32)
    small = dw_in[:, :, CORE + RATES : CORE + RATES + 3].astype(F32)
    d_q_gain = jnp.sum(small[:, :, 0], axis=0)
    d_k_gain = jnp.sum(small[:, :, 1], axis=0)
    d_rate_bias = small[:, :RATES, 2].reshape(TP, 3, OWN).transpose(1, 0, 2).reshape(-1)

    dh1 = scatter_rows(dot(dp, w_in, ((1,), (1,))).astype(BF16))
    n1, r1 = normed(tokens.astype(F32))
    d_tokens = dx2 + norm_back(n1, r1, dh1 * gain_one)

    d_norm_gain = (
        jnp.sum(w_attn_in.astype(F32) * d_w_attn_in, axis=1)
        + jnp.sum(w_rates.astype(F32) * d_w_rates, axis=1)
    ) / norm_gain.astype(F32)
    d_ffn_gain = jnp.sum(w_gate_up.astype(F32) * d_w_gate_up, axis=1) / ffn_gain.astype(F32)
    return (
        layer_out,
        d_tokens,
        d_norm_gain,
        d_w_attn_in,
        d_w_rates,
        d_rate_bias,
        d_q_gain,
        d_k_gain,
        d_w_out,
        d_ffn_gain,
        d_w_gate_up,
        d_w_down,
    )


def solution(mesh):
    devices = mesh.devices.reshape(TP, -1)
    grid = Mesh(devices, ("tp", "sh"))
    rows = P(("tp", "sh"), None)
    flat = P(("tp", "sh"))
    in_specs = (rows, flat, flat, rows, rows, P(), flat, flat, rows, flat, rows, rows, rows)
    out_specs = (rows, rows, flat, rows, rows, P(), flat, flat, rows, flat, rows, rows)
    return jax.shard_map(body, mesh=grid, in_specs=in_specs, out_specs=out_specs, check_vma=False)
```

time: 2600 us -> 668 us (0.26)
  waiting for transfers between devices: 1930 us -> 276 us
  blocking collectives: 158 us -> 38.2 us
  local copies, waits for them, and re-layouts: 216 us -> 99.4 us
  matrix products: 156 us -> 79.1 us
  Pallas kernels: 0 us -> 53.3 us
  other arithmetic: 109 us -> 59.9 us
  starting transfers between devices: 0.19 us -> 42.8 us
    unnamed x6 -> x7, waiting for transfers between devices: 1670 us -> 0.12 us
    ppermute x0 -> x32, waiting for transfers between devices: none -> 229 us  [flip(): return lax.ppermute(array, 'tp', [(i, i ^ offset) for i in range(TP)])]
    all_gather x4 -> x3, waiting for transfers between devices: 261 us -> 32.2 us  [the longest x1 24.4 us: body(): w_in = lax.all_gather(got_in, 'sh', axis=1).reshape(width, WIDE)]
    reshape x13 -> x11, local copies, waits for them, and re-layouts: 126 us -> 14.7 us  [the longest x4 6.54 us: columns_out(): cut = weight.reshape(rows, blocks, TP, -1)]
    dot_general x21 -> x11, matrix products: 156 us -> 79.1 us  [dot(): lax.dot_general(a, b, (dims, ((), ())), precision=precision, preferred_el...]
    concatenate x2 -> x6, other arithmetic: 76 us -> 15.5 us  [the longest x4 8.64 us: gather_rows(): jnp.concatenate([own, flip(own, 2), flip(own, 4), flip(own, 6)], axis=0)]
    pallas_call x0 -> x2, Pallas kernels: none -> 53.3 us  [the longest x1 32.7 us: attn_bwd(): pl.pallas_call(attn_bwd_kernel, grid=(buckets,), in_specs=[SMEM, rows_spe...]
    all_gather x1, blocking collectives: 74.1 us -> 21.4 us  [body(): w_mix = lax.all_gather(w_out, 'sh', axis=0, tiled=True)]
  transfers between devices with their start and end apart: 5 -> 42, of which waited for: 5 -> 25; matrix products, arithmetic and copies ran while one was open for 3% -> 28% of each run, Pallas kernels for 0% -> 5%
where the time goes in v1:
time: 668 us; the launch traced here: 664 us
  waiting for transfers between devices  276 us (41%)
  local copies, waits for them, and re-layouts  99.4 us (15%)
  matrix products  79.1 us (12%)
  other arithmetic  59.9 us (9%)
  Pallas kernels  53.3 us (8%)
  starting transfers between devices  42.8 us (6%)
  blocking collectives  38.2 us (6%)
  between operations  15.2 us (2%)
    ppermute x32, waiting for transfers between devices, flip(): return lax.ppermute(array, 'tp', [(i, i ^ offset) for i in range(TP)])  229 us
    dot_general x11, matrix products, dot(): lax.dot_general(a, b, (dims, ((), ())), precision=precision, preferred_el...  79.1 us
    unnamed x130, local copies, waits for them, and re-layouts  33.5 us
    pallas_call x1, Pallas kernels, attn_bwd(): pl.pallas_call(attn_bwd_kernel, grid=(buckets,), in_specs=[SMEM, rows_spe...  32.7 us
    ppermute x32, starting transfers between devices, flip(): return lax.ppermute(array, 'tp', [(i, i ^ offset) for i in range(TP)])  30.3 us
    all_gather x1, waiting for transfers between devices, body(): w_in = lax.all_gather(got_in, 'sh', axis=1).reshape(width, WIDE)  24.4 us
    all_gather x1, blocking collectives, body(): w_mix = lax.all_gather(w_out, 'sh', axis=0, tiled=True)  21.4 us
    pallas_call x1, Pallas kernels, attn_fwd(): pl.pallas_call(attn_fwd_kernel, grid=(buckets,), in_specs=[SMEM, rows_spe...  20.6 us
  transfers between devices with their start and end apart: 42, of which 25 were waited for; matrix products, arithmetic and copies ran while one was open for 28% of the time, Pallas kernels for 5%

profile of v1, /device:TPU:0, one launch (start us, length us, event | category | flops | bytes accessed | tf_op | source)
XLA Modules:
  0.0 663.9 jit_solution(15666650011742930974)
XLA Ops:
  29.8 16.1 %collective-permute-done.1 = bf16[256,1536]{1,0:T(8,128)(2,1)S(1)} collective-permute-done((bf16[256,1536]{1,0:T(8,128)(2,1)}, bf16[256,1536]{1,0:T(8,128)(2,1)S(1)}, u32[]{:S(2)}, u32[]{:S(2)}) %collective-permute-start.1) | collective-permute-done | bytes 786464 | tf_op jit(solution)/shard_map/ppermute | solution.py:30
  55.7 21.4 %all_gather.20.w_ref = bf16[192,1536]{1,0:T(8,128)(2,1)S(1)} all-gather(bf16[48,1536]{1,0:T(8,128)(2,1)S(1)} %copy-done.35), channel_id=1, replica_groups=mesh['dp'=8,'fsdp'=4] {'fsdp'}, dimensions={0}, use_global_device_ids=true | all-gather | bytes 737280 | tf_op jit(solution)/shard_map/all_gather | solution.py:351
  91.5 24.4 %all-gather.8.cloned.1.call-done = bf16[8,192,896]{2,0,1:T(8,128)(2,1)} async-done(((bf16[8,48,896]{2,0,1:T(8,128)(2,1)}), bf16[8,192,896]{2,0,1:T(8,128)(2,1)}) %all-gather.8.cloned.1.call-update) | async-done | bytes 2752528 | tf_op jit(solution)/shard_map/all_gather | solution.py:350
  120.8 9.7 %fusion.7.proj_ref = f32[2048,896]{1,0:T(8,128)S(1)} fusion(bf16[1536,896]{1,0:T(8,128)(2,1)} %bitcast.87, bf16[2048,1536]{1,0:T(8,128)(2,1)} %constant_dynamic-update-slice_fusion, f32[1536]{0:T(1024)S(1)} %get-tuple-element.109, f32[2048]{0:T(1024)S(1)} %add_rsqrt_fusion), kind=kOutput, calls=%fused_computation.34 | convolution fusion | flops 5649727488 | bytes 16398336 | tf_op jit(solution)/shard_map/dot_general | solution.py:60
  130.5 20.6 %attn_fwd.1 = (bf16[2048,192]{1,0:T(8,128)(2,1)S(1)}, f32[2048,192]{1,0:T(8,128)S(1)}, f32[2048,128]{1,0:T(8,128)S(1)}) custom-call(s32[8,4]{1,0:T(8,128)S(1)} %gather_fusion, f32[2048,896]{1,0:T(8,128)S(1)} %fusion.7.proj_ref, f32[8,128]{1,0:T(8,128)S(1)} %pad.15.bias_ref, f32[8,256]{1,0:T(8,128)S(1)} %pad.16.gains_ref), custom_call_target="tpu_custom_call" | custom-call | tf_op jit(solution)/shard_map/attn_fwd/pallas_call | solution.py:271
  161.5 16.8 %all_to_all.20 = bf16[8,48,1024]{2,1,0:T(8,128)(2,1)} all-to-all(bf16[8,48,1024]{2,1,0:T(8,128)(2,1)} %reshape.210), channel_id=1, replica_groups=mesh['dp'=8,'fsdp'=4] {'dp'}, dimensions={0} | all-to-all | bytes 1572864 | tf_op jit(solution)/shard_map/all_to_all | solution.py:352
  188.9 15.0 %collective-permute-done.5 = bf16[256,1536]{1,0:T(8,128)(2,1)S(1)} collective-permute-done((bf16[256,1536]{1,0:T(8,128)(2,1)S(1)}, bf16[256,1536]{1,0:T(8,128)(2,1)S(1)}, u32[]{:S(2)}, u32[]{:S(2)}) %collective-permute-start.5) | collective-permute-done | bytes 786464 | tf_op jit(solution)/shard_map/ppermute | solution.py:30
  204.3 17.1 %collective-permute-done.7 = bf16[256,1536]{1,0:T(8,128)(2,1)S(1)} collective-permute-done((bf16[256,1536]{1,0:T(8,128)(2,1)S(1)}, bf16[256,1536]{1,0:T(8,128)(2,1)S(1)}, u32[]{:S(2)}, u32[]{:S(2)}) %collective-permute-start.7) | collective-permute-done | bytes 786464 | tf_op jit(solution)/shard_map/ppermute | solution.py:30
  221.4 18.8 %collective-permute-done.6 = bf16[256,1536]{1,0:T(8,128)(2,1)S(1)} collective-permute-done((bf16[256,1536]{1,0:T(8,128)(2,1)S(1)}, bf16[256,1536]{1,0:T(8,128)(2,1)S(1)}, u32[]{:S(2)}, u32[]{:S(2)}) %collective-permute-start.6) | collective-permute-done | bytes 786464 | tf_op jit(solution)/shard_map/ppermute | solution.py:30
  246.2 27.6 %collective-permute-done.17 = bf16[256,1536]{1,0:T(8,128)(2,1)S(1)} collective-permute-done((bf16[256,1536]{1,0:T(8,128)(2,1)S(1)}, bf16[256,1536]{1,0:T(8,128)(2,1)S(1)}, u32[]{:S(2)}, u32[]{:S(2)}) %collective-permute-start.17) | collective-permute-done | bytes 786464 | tf_op jit(solution)/shard_map/ppermute | solution.py:30
  276.1 11.7 %collective-permute-done.9 = bf16[256,1536]{1,0:T(8,128)(2,1)S(1)} collective-permute-done((bf16[256,1536]{1,0:T(8,128)(2,1)S(1)}, bf16[256,1536]{1,0:T(8,128)(2,1)S(1)}, u32[]{:S(2)}, u32[]{:S(2)}) %collective-permute-start.9) | collective-permute-done | bytes 786464 | tf_op jit(solution)/shard_map/ppermute | solution.py:30
  307.0 11.9 %fusion.40 = f32[2048,1024]{0,1:T(8,128)} fusion(bf16[2048,1536]{1,0:T(8,128)(2,1)} %constant_dynamic-update-slice_fusion.5, bf16[1536,1024]{1,0:T(8,128)(2,1)} %bitcast.111), kind=kOutput, calls=%fused_computation.131 | convolution fusion | flops 6442450944 | bytes 17825792 | tf_op jit(solution)/shard_map/dot_general | solution.py:60
  326.7 9.6 %multiply_convert_fusion.1 = (bf16[2048,512]{0,1:T(8,128)(2,1)S(1)}, bf16[2048,512]{0,1:T(8,128)(2,1)S(1)}, bf16[2048,512]{0,1:T(8,128)(2,1)S(1)}) fusion(f32[2048,1024]{0,1:T(8,128)} %fusion.40, f32[2048]{0:T(1024)S(1)} %bitcast.106, bf16[2048,1536]{1,0:T(8,128)(2,1)} %constant_dynamic-update-slice_fusion.10, ...), kind=kOutput, calls=%fused_computation.17 | convolution fusion | flops 3240099840 | bytes 22552576 | tf_op jit(solution)/shard_map/dot_general | solution.py:60
  381.7 9.6 %collective-permute-done.21 = bf16[256,1536]{1,0:T(8,128)(2,1)S(1)} collective-permute-done((bf16[256,1536]{1,0:T(8,128)(2,1)S(1)}, bf16[256,1536]{1,0:T(8,128)(2,1)S(1)}, u32[]{:S(2)}, u32[]{:S(2)}) %collective-permute-start.21) | collective-permute-done | bytes 786464 | tf_op jit(solution)/shard_map/ppermute | solution.py:30
  392.8 16.3 %collective-permute-done.23 = bf16[256,1536]{1,0:T(8,128)(2,1)S(1)} collective-permute-done((bf16[256,1536]{1,0:T(8,128)(2,1)S(1)}, bf16[256,1536]{1,0:T(8,128)(2,1)S(1)}, u32[]{:S(2)}, u32[]{:S(2)}) %collective-permute-start.23) | collective-permute-done | bytes 786464 | tf_op jit(solution)/shard_map/ppermute | solution.py:30
  411.0 14.1 %collective-permute-done.13 = bf16[256,1536]{1,0:T(8,128)(2,1)S(1)} collective-permute-done((bf16[256,1536]{1,0:T(8,128)(2,1)S(1)}, bf16[256,1536]{1,0:T(8,128)(2,1)S(1)}, u32[]{:S(2)}, u32[]{:S(2)}) %collective-permute-start.13) | collective-permute-done | bytes 786464 | tf_op jit(solution)/shard_map/ppermute | solution.py:30
  425.1 17.0 %collective-permute-done.15 = bf16[256,1536]{1,0:T(8,128)(2,1)S(1)} collective-permute-done((bf16[256,1536]{1,0:T(8,128)(2,1)S(1)}, bf16[256,1536]{1,0:T(8,128)(2,1)S(1)}, u32[]{:S(2)}, u32[]{:S(2)}) %collective-permute-start.15) | collective-permute-done | bytes 786464 | tf_op jit(solution)/shard_map/ppermute | solution.py:30
  451.2 17.9 %collective-permute-done.26 = bf16[256,1536]{1,0:T(8,128)(2,1)S(1)} collective-permute-done((bf16[256,1536]{1,0:T(8,128)(2,1)S(1)}, bf16[256,1536]{1,0:T(8,128)(2,1)S(1)}, u32[]{:S(2)}, u32[]{:S(2)}) %collective-permute-start.26) | collective-permute-done | bytes 786464 | tf_op jit(solution)/shard_map/ppermute | solution.py:30
  469.1 13.6 %collective-permute-done.25 = bf16[256,1536]{1,0:T(8,128)(2,1)S(1)} collective-permute-done((bf16[256,1536]{1,0:T(8,128)(2,1)S(1)}, bf16[256,1536]{1,0:T(8,128)(2,1)S(1)}, u32[]{:S(2)}, u32[]{:S(2)}) %collective-permute-start.25) | collective-permute-done | bytes 786464 | tf_op jit(solution)/shard_map/ppermute | solution.py:30
  501.5 32.7 %attn_bwd.1 = (bf16[2048,896]{1,0:T(8,128)(2,1)S(1)}, f32[8,256]{1,0:T(8,128)S(1)}) custom-call(s32[8,4]{1,0:T(8,128)S(1)} %gather_fusion, f32[2048,896]{1,0:T(8,128)} %copy-done.1, f32[8,128]{1,0:T(8,128)S(1)} %pad.15.bias_ref, f32[8,256]{1,0:T(8,128)S(1)} %pad.16.gains_ref, f32[2048,192]{1,0:T(8,128)S(1)} %copy-done.3, ...), custom_call_target="tpu_custom_call" | custom-call | tf_op jit(solution)/shard_map/attn_bwd/pallas_call | solution.py:290
  534.2 8.8 %convolution_convert_fusion = bf16[2048,1536]{1,0:T(8,128)(2,1)} fusion(bf16[2048,896]{1,0:T(8,128)(2,1)S(1)} %get-tuple-element.32, bf16[1536,896]{1,0:T(8,128)(2,1)S(1)} %bitcast.88), kind=kOutput, calls=%fused_computation.6 | convolution fusion | flops 5640290304 | bytes 12713984 | tf_op jit(solution)/shard_map/dot_general | solution.py:60
  545.4 10.9 %fusion.5 = bf16[1536,896]{0,1:T(8,128)(2,1)} fusion(bf16[2048,896]{1,0:T(8,128)(2,1)} %copy-done.4, bf16[2048,1536]{1,0:T(8,128)(2,1)} %constant_dynamic-update-slice_fusion, f32[1536]{0:T(1024)S(1)} %copy-done.37, f32[2048]{0:T(1024)S(1)} %copy-done.39), kind=kOutput, calls=%fused_computation.33 | convolution fusion | flops 5649727488 | bytes 12728320 | tf_op jit(solution)/shard_map/dot_general | solution.py:60
  596.9 9.1 %collective-permute-done.29 = bf16[256,1536]{1,0:T(8,128)(2,1)} collective-permute-done((bf16[256,1536]{1,0:T(8,128)(2,1)}, bf16[256,1536]{1,0:T(8,128)(2,1)}, u32[]{:S(2)}, u32[]{:S(2)}) %collective-permute-start.29) | collective-permute-done | bytes 786464 | tf_op jit(solution)/shard_map/ppermute | solution.py:30
  606.0 17.5 %collective-permute-done.31 = bf16[256,1536]{1,0:T(8,128)(2,1)} collective-permute-done((bf16[256,1536]{1,0:T(8,128)(2,1)}, bf16[256,1536]{1,0:T(8,128)(2,1)}, u32[]{:S(2)}, u32[]{:S(2)}) %collective-permute-start.31) | collective-permute-done | bytes 786464 | tf_op jit(solution)/shard_map/ppermute | solution.py:30
  (325 shorter events, 260.5 us)
Async XLA Ops:
  11.1 34.7 %collective-permute-start.1 = (bf16[256,1536]{1,0:T(8,128)(2,1)}, bf16[256,1536]{1,0:T(8,128)(2,1)S(1)}, u32[]{:S(2)}, u32[]{:S(2)}) collective-permute-start(bf16[256,1536]{1,0:T(8,128)(2,1)} %param.16), channel_id=1, source_target_pairs={{0,16},{4,20},{8,24},{12,28},{16,0},{20,4},{24,8},{28,12},{1,17},{... | collective-permute-start | bytes 2359304 | tf_op jit(solution)/shard_map/ppermute | solution.py:30
  11.7 35.6 %collective-permute-start = (bf16[256,1536]{1,0:T(8,128)(2,1)}, bf16[256,1536]{1,0:T(8,128)(2,1)}, u32[]{:S(2)}, u32[]{:S(2)}) collective-permute-start(bf16[256,1536]{1,0:T(8,128)(2,1)} %param.16), channel_id=1, source_target_pairs={{0,8},{4,12},{8,0},{12,4},{16,24},{20,28},{24,16},{28,20},{1,9},{5... | collective-permute-start | bytes 2359304 | tf_op jit(solution)/shard_map/ppermute | solution.py:30
  28.4 87.5 %all-gather.8.cloned.1.call-start = ((), (), s32[]{:S(2)}) async-start(), calls=%async_computation.13 | async-start | bytes 3440640 | tf_op jit(solution)/shard_map/all_gather | solution.py:350
  55.4 251.6 %all-gather.10.cloned.1.call-start = ((), (), s32[]{:S(2)}) async-start(), calls=%async_computation.14 | async-start | bytes 3932160 | tf_op jit(solution)/shard_map/all_gather | solution.py:353
  178.3 148.4 %all-gather.6.cloned.1.call-start = ((), (), s32[]{:S(2)}) async-start(), calls=%async_computation.8 | async-start | bytes 1966080 | tf_op jit(solution)/shard_map/all_gather | solution.py:354
  183.9 37.5 %collective-permute-start.7 = (bf16[256,1536]{1,0:T(8,128)(2,1)S(1)}, bf16[256,1536]{1,0:T(8,128)(2,1)S(1)}, u32[]{:S(2)}, u32[]{:S(2)}) collective-permute-start(bf16[256,1536]{1,0:T(8,128)(2,1)S(1)} %get-tuple-element.138), channel_id=1, source_target_pairs={{0,24},{4,28},{8,16},{12,20},{16,8},{20,12},{24,0},{28,4},{1,25},{... | collective-permute-start | bytes 2359304 | tf_op jit(solution)/shard_map/ppermute | solution.py:30
  186.0 54.2 %collective-permute-start.6 = (bf16[256,1536]{1,0:T(8,128)(2,1)S(1)}, bf16[256,1536]{1,0:T(8,128)(2,1)S(1)}, u32[]{:S(2)}, u32[]{:S(2)}) collective-permute-start(bf16[256,1536]{1,0:T(8,128)(2,1)S(1)} %get-tuple-element.139), channel_id=1, source_target_pairs={{0,16},{4,20},{8,24},{12,28},{16,0},{20,4},{24,8},{28,12},{1,17},{... | collective-permute-start | bytes 2359304 | tf_op jit(solution)/shard_map/ppermute | solution.py:30
  186.8 57.5 %collective-permute-start.18 = (bf16[256,1536]{1,0:T(8,128)(2,1)S(1)}, bf16[256,1536]{1,0:T(8,128)(2,1)S(1)}, u32[]{:S(2)}, u32[]{:S(2)}) collective-permute-start(bf16[256,1536]{1,0:T(8,128)(2,1)S(1)} %copy-done.10), channel_id=1, source_target_pairs={{0,24},{4,28},{8,16},{12,20},{16,8},{20,12},{24,0},{28,4},{1,25},{... | collective-permute-start | bytes 2359304 | tf_op jit(solution)/shard_map/ppermute | solution.py:30
  187.5 86.3 %collective-permute-start.17 = (bf16[256,1536]{1,0:T(8,128)(2,1)S(1)}, bf16[256,1536]{1,0:T(8,128)(2,1)S(1)}, u32[]{:S(2)}, u32[]{:S(2)}) collective-permute-start(bf16[256,1536]{1,0:T(8,128)(2,1)S(1)} %copy-done.10), channel_id=1, source_target_pairs={{0,16},{4,20},{8,24},{12,28},{16,0},{20,4},{24,8},{28,12},{1,17},{... | collective-permute-start | bytes 2359304 | tf_op jit(solution)/shard_map/ppermute | solution.py:30
  203.8 70.1 %collective-permute-start.16 = (bf16[256,1536]{1,0:T(8,128)(2,1)S(1)}, bf16[256,1536]{1,0:T(8,128)(2,1)S(1)}, u32[]{:S(2)}, u32[]{:S(2)}) collective-permute-start(bf16[256,1536]{1,0:T(8,128)(2,1)S(1)} %copy-done.10), channel_id=1, source_target_pairs={{0,8},{4,12},{8,0},{12,4},{16,24},{20,28},{24,16},{28,20},{1,9},{5... | collective-permute-start | bytes 2359304 | tf_op jit(solution)/shard_map/ppermute | solution.py:30
  243.6 44.2 %collective-permute-start.9 = (bf16[256,1536]{1,0:T(8,128)(2,1)S(1)}, bf16[256,1536]{1,0:T(8,128)(2,1)S(1)}, u32[]{:S(2)}, u32[]{:S(2)}) collective-permute-start(bf16[256,1536]{1,0:T(8,128)(2,1)S(1)} %get-tuple-element.114), channel_id=1, source_target_pairs={{0,16},{4,20},{8,24},{12,28},{16,0},{20,4},{24,8},{28,12},{1,17},{... | collective-permute-start | bytes 2359304 | tf_op jit(solution)/shard_map/ppermute | solution.py:30
  244.3 43.5 %collective-permute-start.8 = (bf16[256,1536]{1,0:T(8,128)(2,1)S(1)}, bf16[256,1536]{1,0:T(8,128)(2,1)S(1)}, u32[]{:S(2)}, u32[]{:S(2)}) collective-permute-start(bf16[256,1536]{1,0:T(8,128)(2,1)S(1)} %get-tuple-element.114), channel_id=1, source_target_pairs={{0,8},{4,12},{8,0},{12,4},{16,24},{20,28},{24,16},{28,20},{1,9},{5... | collective-permute-start | bytes 2359304 | tf_op jit(solution)/shard_map/ppermute | solution.py:30
  289.9 283.5 %reduce-scatter.9.cloned.1.call-start = ((), (), s32[]{:S(2)}) async-start(), calls=%async_computation.11 | async-start | bytes 3932160 | tf_op jit(solution)/shard_map/reduce_scatter | solution.py:77
  366.5 222.3 %reduce-scatter.11.cloned.1.call-start = ((), (), s32[]{:S(2)}) async-start(), calls=%async_computation.12 | async-start | bytes 1966080 | tf_op jit(solution)/shard_map/reduce_scatter | solution.py:388
  372.4 36.7 %collective-permute-start.23 = (bf16[256,1536]{1,0:T(8,128)(2,1)S(1)}, bf16[256,1536]{1,0:T(8,128)(2,1)S(1)}, u32[]{:S(2)}, u32[]{:S(2)}) collective-permute-start(bf16[256,1536]{1,0:T(8,128)(2,1)S(1)} %get-tuple-element.132), channel_id=1, source_target_pairs={{0,24},{4,28},{8,16},{12,20},{16,8},{20,12},{24,0},{28,4},{1,25},{... | collective-permute-start | bytes 2359304 | tf_op jit(solution)/shard_map/ppermute | solution.py:30
  373.9 37.1 %collective-permute-start.22 = (bf16[256,1536]{1,0:T(8,128)(2,1)S(1)}, bf16[256,1536]{1,0:T(8,128)(2,1)S(1)}, u32[]{:S(2)}, u32[]{:S(2)}) collective-permute-start(bf16[256,1536]{1,0:T(8,128)(2,1)S(1)} %get-tuple-element.133), channel_id=1, source_target_pairs={{0,16},{4,20},{8,24},{12,28},{16,0},{20,4},{24,8},{28,12},{1,17},{... | collective-permute-start | bytes 2359304 | tf_op jit(solution)/shard_map/ppermute | solution.py:30
  378.8 46.3 %collective-permute-start.13 = (bf16[256,1536]{1,0:T(8,128)(2,1)S(1)}, bf16[256,1536]{1,0:T(8,128)(2,1)S(1)}, u32[]{:S(2)}, u32[]{:S(2)}) collective-permute-start(bf16[256,1536]{1,0:T(8,128)(2,1)S(1)} %get-tuple-element.134), channel_id=1, source_target_pairs={{0,8},{4,12},{8,0},{12,4},{16,24},{20,28},{24,16},{28,20},{1,9},{5... | collective-permute-start | bytes 2359304 | tf_op jit(solution)/shard_map/ppermute | solution.py:30
  380.3 61.8 %collective-permute-start.15 = (bf16[256,1536]{1,0:T(8,128)(2,1)S(1)}, bf16[256,1536]{1,0:T(8,128)(2,1)S(1)}, u32[]{:S(2)}, u32[]{:S(2)}) collective-permute-start(bf16[256,1536]{1,0:T(8,128)(2,1)S(1)} %get-tuple-element.135), channel_id=1, source_target_pairs={{0,24},{4,28},{8,16},{12,20},{16,8},{20,12},{24,0},{28,4},{1,25},{... | collective-permute-start | bytes 2359304 | tf_op jit(solution)/shard_map/ppermute | solution.py:30
  391.3 52.0 %collective-permute-start.14 = (bf16[256,1536]{1,0:T(8,128)(2,1)S(1)}, bf16[256,1536]{1,0:T(8,128)(2,1)S(1)}, u32[]{:S(2)}, u32[]{:S(2)}) collective-permute-start(bf16[256,1536]{1,0:T(8,128)(2,1)S(1)} %get-tuple-element.136), channel_id=1, source_target_pairs={{0,16},{4,20},{8,24},{12,28},{16,0},{20,4},{24,8},{28,12},{1,17},{... | collective-permute-start | bytes 2359304 | tf_op jit(solution)/shard_map/ppermute | solution.py:30
  449.1 33.6 %collective-permute-start.25 = (bf16[256,1536]{1,0:T(8,128)(2,1)S(1)}, bf16[256,1536]{1,0:T(8,128)(2,1)S(1)}, u32[]{:S(2)}, u32[]{:S(2)}) collective-permute-start(bf16[256,1536]{1,0:T(8,128)(2,1)S(1)} %get-tuple-element.111), channel_id=1, source_target_pairs={{0,16},{4,20},{8,24},{12,28},{16,0},{20,4},{24,8},{28,12},{1,17},{... | collective-permute-start | bytes 2359304 | tf_op jit(solution)/shard_map/ppermute | solution.py:30
  489.6 105.7 %reduce-scatter.7.cloned.1.call-start = ((), (), s32[]{:S(2)}) async-start(), calls=%async_computation.10 | async-start | bytes 737280 | tf_op jit(solution)/shard_map/reduce_scatter | solution.py:395
  556.3 76.1 %reduce-scatter.5.cloned.1.call-start = ((), (), s32[]{:S(2)}) async-start(), calls=%async_computation.9 | async-start | bytes 3440640 | tf_op jit(solution)/shard_map/reduce_scatter | solution.py:77
  587.2 36.3 %collective-permute-start.31 = (bf16[256,1536]{1,0:T(8,128)(2,1)}, bf16[256,1536]{1,0:T(8,128)(2,1)}, u32[]{:S(2)}, u32[]{:S(2)}) collective-permute-start(bf16[256,1536]{1,0:T(8,128)(2,1)} %get-tuple-element.129), channel_id=1, source_target_pairs={{0,24},{4,28},{8,16},{12,20},{16,8},{20,12},{24,0},{28,4},{1,25},{... | collective-permute-start | bytes 2359304 | tf_op jit(solution)/shard_map/ppermute | solution.py:30
  588.7 36.2 %collective-permute-start.30 = (bf16[256,1536]{1,0:T(8,128)(2,1)}, bf16[256,1536]{1,0:T(8,128)(2,1)}, u32[]{:S(2)}, u32[]{:S(2)}) collective-permute-start(bf16[256,1536]{1,0:T(8,128)(2,1)} %get-tuple-element.130), channel_id=1, source_target_pairs={{0,16},{4,20},{8,24},{12,28},{16,0},{20,4},{24,8},{28,12},{1,17},{... | collective-permute-start | bytes 2359304 | tf_op jit(solution)/shard_map/ppermute | solution.py:30
  (73 other events, 1090.2 us)
Sparse Core Ops, SparseCore 0:
  55.5 60.3 all-gather.7
  178.4 61.9 all-gather.9
  290.1 36.5 all-gather.5
  366.6 59.1 reduce-scatter.8
  489.7 34.3 reduce-scatter.10
  556.4 21.0 reduce-scatter.6
  579.8 52.5 reduce-scatter.4

commit v2 on v1

v2 whole, which is shorter than its diff:
```python
import jax
import jax.numpy as jnp
import numpy as np
from jax import lax
from jax.experimental import pallas as pl
from jax.experimental.pallas import tpu as pltpu
from jax.sharding import Mesh
from jax.sharding import PartitionSpec as P

HEADS = 24
HEAD_DIM = 64
EPS = 1e-06
NEG = -1e30
TP = 8
OWN = HEADS // TP
BLOCK = OWN * HEAD_DIM
CORE = 4 * BLOCK
EXTRA = 128
WIDE = CORE + EXTRA
RATES = 3 * OWN
GAIN_AT = RATES
LENS_AT = RATES + 4
OFFSETS = (0, 2, 4, 6, 1, 3, 5, 7)
F32 = jnp.float32
BF16 = jnp.bfloat16


def flip(array, offset):
    return lax.ppermute(array, "tp", [(i, i ^ offset) for i in range(TP)])


def sides(own):
    return flip(own, 2), flip(own, 4)


def diagonal(two, four):
    cut = two.shape[0] // 2
    return flip(two[:cut], 4), flip(four[cut:], 2)


def others(own):
    return [flip(own, d) for d in (2, 4, 6)]


def both_cores(near, far_flipped):
    rows = near.shape[0] // 4
    sums = [near[i * rows : (i + 1) * rows].astype(F32) + far_flipped[i * rows : (i + 1) * rows].astype(F32) for i in range(4)]
    return sums[0], [x.astype(BF16) for x in sums[1:]]


def send(blocks):
    return [flip(x, d) for x, d in zip(blocks, (2, 4, 6))]


def relay_six(blocks):
    two, four, six = blocks
    cut = six.shape[0] // 2
    return two, four, flip(six[:cut], 2), flip(six[cut:], 4)


def add_six(blocks):
    two, four, over_two, over_four = blocks
    cut = over_two.shape[0]
    two = jnp.concatenate([two[:cut], (two[cut:].astype(F32) + over_four.astype(F32)).astype(BF16)], axis=0)
    four = jnp.concatenate([(four[:cut].astype(F32) + over_two.astype(F32)).astype(BF16), four[cut:]], axis=0)
    return two, four


def gather_shares(own):
    share = lax.axis_size("sh")
    return [own] + [lax.ppermute(own, "sh", [(i, (i + k) % share) for i in range(share)]) for k in range(1, share)]


def in_order(pieces):
    here = lax.axis_index("sh")
    share = len(pieces)
    out = jnp.zeros((share,) + pieces[0].shape, pieces[0].dtype)
    for k, piece in enumerate(pieces):
        out = lax.dynamic_update_index_in_dim(out, piece, (here - k) % share, 0)
    return out.reshape((-1,) + pieces[0].shape[1:])


def to_shares(part):
    share = lax.axis_size("sh")
    here = lax.axis_index("sh")
    blocks = part.reshape(share, -1, part.shape[1])
    picked = [lax.dynamic_index_in_dim(blocks, (here + k) % share, 0, False) for k in range(share)]
    return picked[:1] + [
        lax.ppermute(picked[k], "sh", [(i, (i + k) % share) for i in range(share)]) for k in range(1, share)
    ]


def total_of(parts):
    return sum(term.astype(F32) for term in parts)


def phase(*values):
    return lax.optimization_barrier(values)


def normed(field_in):
    factor = lax.rsqrt(jnp.mean(field_in * field_in, axis=-1, keepdims=True) + EPS)
    return field_in * factor, factor


def norm_back(normal, factor, grad_in):
    return factor * (grad_in - normal * jnp.mean(grad_in * normal, axis=-1, keepdims=True))


def dot(a, b, dims=((1,), (0,)), precision=None):
    return lax.dot_general(a, b, (dims, ((), ())), precision=precision, preferred_element_type=F32)


def iota(shape, dim):
    return lax.broadcasted_iota(jnp.int32, shape, dim)


def settings(us, mib):
    cost = pl.CostEstimate(flops=int(us * 1e7), bytes_accessed=int(us * 1e4), transcendentals=0)
    return dict(compiler_params=pltpu.CompilerParams(vmem_limit_bytes=mib * 2**20), cost_estimate=cost)


SMEM = pl.BlockSpec(memory_space=pltpu.SMEM)
VMEM = pl.BlockSpec(memory_space=pltpu.VMEM)


def shape(dims, dtype):
    return jax.ShapeDtypeStruct(dims, dtype)


def rate_picks(t, rows, columns, flipped=False):
    whole, own = iota((rows, columns), 1 if flipped else 0), iota((rows, columns), 0 if flipped else 1)
    kind, head = own // OWN, own % OWN
    return ((own < RATES) & (whole == kind * HEADS + t * OWN + head)).astype(BF16)


def pack_in_kernel(lens_ref, w_ref, rates_ref, gains_ref, out_ref):
    rows, width = w_ref.shape[0], w_ref.shape[1] // 4
    picks = (iota((4, EXTRA), 1) == GAIN_AT + iota((4, EXTRA), 0)).astype(BF16)
    beside = dot(gains_ref[...], picks, ((0,), (0,)))
    lane, row = iota((rows, EXTRA), 1), iota((rows, EXTRA), 0)
    for j in range(lens_ref.shape[0]):
        beside = jnp.where((lane == LENS_AT + j) & (row == 0), lens_ref[j].astype(F32), beside)
    for t in range(TP):
        for b in range(4):
            at = b * width + t * BLOCK
            out_ref[t, :, b * BLOCK : (b + 1) * BLOCK] = w_ref[:, at : at + BLOCK]
        rates = dot(rates_ref[...], rate_picks(t, rates_ref.shape[1], EXTRA))
        out_ref[t, :, CORE:WIDE] = (rates + beside).astype(BF16)


def pack_in(lens, w, rates, gains):
    return pl.pallas_call(
        pack_in_kernel,
        in_specs=[SMEM, VMEM, VMEM, VMEM],
        out_specs=VMEM,
        out_shape=shape((TP, w.shape[0], WIDE), BF16),
        **settings(3, 16),
        name="pack_in",
    )(lens, w, rates, gains)


def pack_gu_kernel(w_ref, out_ref):
    ff = w_ref.shape[1] // 2
    own = ff // TP
    for t in range(TP):
        out_ref[t, :, :own] = w_ref[:, t * own : (t + 1) * own]
        out_ref[t, :, own:] = w_ref[:, ff + t * own : ff + (t + 1) * own]


def pack_gu(w):
    return pl.pallas_call(
        pack_gu_kernel,
        in_specs=[VMEM],
        out_specs=VMEM,
        out_shape=shape((TP, w.shape[0], w.shape[1] // TP), BF16),
        **settings(2, 16),
        name="pack_gu",
    )(w)


def join_ffn(got, down):
    columns = got.shape[2]
    top, rows = got.shape[0] * got.shape[1], down.shape[0]
    half = rows // 2

    def kernel(got_ref, down_ref, out_ref):
        for t in range(TP):
            out_ref[t * got.shape[1] : (t + 1) * got.shape[1], :] = got_ref[t]
        out_ref[top : top + rows, :] = down_ref[:, :columns]
        out_ref[top + rows :, : columns // 2] = down_ref[:half, columns:]
        out_ref[top + rows :, columns // 2 :] = down_ref[half:, columns:]

    return pl.pallas_call(
        kernel,
        in_specs=[VMEM, VMEM],
        out_specs=VMEM,
        out_shape=shape((top + rows + half, columns), BF16),
        **settings(2, 16),
        name="join_ffn",
    )(got, down)


def open_ffn(joined, down_rows, width):
    share, _, columns = joined.shape
    own_rows = width // (TP * share)
    top = TP * own_rows
    half = down_rows // 2

    def kernel(in_ref, gu_ref, down_ref):
        for z in range(share):
            for t in range(TP):
                at = (t * share + z) * own_rows
                gu_ref[at : at + own_rows, :] = in_ref[z, t * own_rows : (t + 1) * own_rows, :]
            at = z * down_rows
            down_ref[at : at + down_rows, :columns] = in_ref[z, top : top + down_rows, :]
            down_ref[at : at + half, columns:] = in_ref[z, top + down_rows :, : columns // 2]
            down_ref[at + half : at + down_rows, columns:] = in_ref[z, top + down_rows :, columns // 2 :]

    return pl.pallas_call(
        kernel,
        in_specs=[VMEM],
        out_specs=[VMEM, VMEM],
        out_shape=[shape((width, columns), BF16), shape((share * down_rows, width), BF16)],
        **settings(4, 16),
        name="open_ffn",
    )(joined)


def join_rows(*pieces):
    pieces = [x if isinstance(x, tuple) else (x, 0) for x in pieces]
    total = sum(x.shape[0] - first for x, first in pieces)

    def kernel(*refs):
        at = 0
        for ref, (x, first) in zip(refs, pieces):
            more = x.shape[0] - first
            refs[-1][at : at + more, :] = ref[first:, :]
            at += more

    return pl.pallas_call(
        kernel,
        in_specs=[VMEM] * len(pieces),
        out_specs=VMEM,
        out_shape=shape((total, pieces[0][0].shape[1]), pieces[0][0].dtype),
        **settings(2, 24),
        name="join_rows",
    )(*[x for x, _ in pieces])


def unpack_in_kernel(got_ref, w_ref, rates_ref, gain_ref, dw_ref, drates_ref, small_ref):
    rows, width = w_ref.shape[0], w_ref.shape[1] // 4
    along = jnp.zeros((rows, 1), F32)
    drates = jnp.zeros((rows, EXTRA), F32)
    sums = jnp.zeros((rows, EXTRA), F32)
    bias = jnp.zeros((rows, EXTRA), F32)
    lane, row = iota((rows, EXTRA), 1), iota((rows, EXTRA), 0)
    for t in range(TP):
        for b in range(4):
            at = b * width + t * BLOCK
            piece = got_ref[t, :, b * BLOCK : (b + 1) * BLOCK].astype(F32)
            dw_ref[:, at : at + BLOCK] = piece
            along = along + jnp.sum(piece * w_ref[:, at : at + BLOCK].astype(F32), axis=1, keepdims=True)
        extra = got_ref[t, :, CORE:WIDE]
        drates = drates + dot(extra, rate_picks(t, EXTRA, EXTRA, True))
        extra = extra.astype(F32)
        sums = sums + extra
        spot = (row // OWN) * HEADS + t * OWN + row % OWN
        bias = bias + jnp.where((lane == spot) & (row < RATES), extra[:, RATES + 2 : RATES + 3], 0.0)
    columns = rates_ref.shape[1]
    drates_ref[...] = drates[:, :columns]
    along = along + jnp.sum(drates[:, :columns] * rates_ref[...].astype(F32), axis=1, keepdims=True)
    turned = jnp.where(lane == 0, along, 0.0) + jnp.where(lane == 1, sums[:, RATES : RATES + 1], 0.0)
    turned = turned + jnp.where(lane == 2, sums[:, RATES + 1 : RATES + 2], 0.0)
    pick = (iota((rows, EXTRA), 0) == iota((rows, EXTRA), 1)).astype(F32)
    turned = dot(turned, pick, ((0,), (0,)), lax.Precision.HIGHEST)
    small_ref[0:1, :] = turned[0:1, :] / gain_ref[...]
    small_ref[1:3, :] = turned[1:3, :]
    small_ref[3:4, :] = jnp.sum(bias, axis=0, keepdims=True)
    small_ref[4:8, :] = jnp.zeros((4, EXTRA), F32)


def unpack_in(got, w, rates, gain):
    rows = w.shape[0]
    gain = jnp.pad(gain.astype(F32)[None], ((0, 0), (0, EXTRA - rows)), constant_values=1.0)
    return pl.pallas_call(
        unpack_in_kernel,
        in_specs=[VMEM] * 4,
        out_specs=[VMEM] * 3,
        out_shape=[shape(w.shape, F32), shape(rates.shape, F32), shape((8, EXTRA), F32)],
        **settings(5, 16),
        name="unpack_in",
    )(got, w, rates, gain)


def unpack_gu_kernel(got_ref, w_ref, gain_ref, dw_ref, small_ref):
    rows, ff = w_ref.shape[0], w_ref.shape[1] // 2
    own = ff // TP
    along = jnp.zeros((rows, 1), F32)
    for t in range(TP):
        for half in range(2):
            at = half * ff + t * own
            piece = got_ref[t, :, half * own : (half + 1) * own].astype(F32)
            dw_ref[:, at : at + own] = piece
            along = along + jnp.sum(piece * w_ref[:, at : at + own].astype(F32), axis=1, keepdims=True)
    lane = iota((rows, EXTRA), 1)
    pick = (iota((rows, EXTRA), 0) == lane).astype(F32)
    turned = dot(jnp.where(lane == 0, along, 0.0), pick, ((0,), (0,)), lax.Precision.HIGHEST)
    small_ref[...] = turned[0:8, :] / gain_ref[...]


def unpack_gu(got, w, gain):
    rows = w.shape[0]
    gain = jnp.pad(gain.astype(F32)[None], ((0, 0), (0, EXTRA - rows)), constant_values=1.0)
    return pl.pallas_call(
        unpack_gu_kernel,
        in_specs=[VMEM] * 3,
        out_specs=[VMEM] * 2,
        out_shape=[shape(w.shape, F32), shape((8, EXTRA), F32)],
        **settings(3, 16),
        name="unpack_gu",
    )(got, w, gain)


def fold(block):
    cut = block.shape[0] // 2
    tail = jnp.concatenate([block[:cut, EXTRA:], block[cut:, EXTRA:]], axis=1)
    return jnp.concatenate([block[:, :EXTRA], tail], axis=0)


def unfold(block):
    rows = 2 * block.shape[0] // 3
    tail = block[rows:]
    tail = jnp.concatenate([tail[:, : BLOCK - EXTRA], tail[:, BLOCK - EXTRA :]], axis=0)
    return jnp.concatenate([block[:rows], tail], axis=1)


def split(field_in, count):
    terms = []
    for _ in range(count):
        terms.append(field_in.astype(BF16))
        field_in = field_in - terms[-1].astype(F32)
    return terms


def dot_split(field_in, picks, count):
    return sum(dot(term, picks) for term in split(field_in, count))


TAIL = 64
SPAN = BLOCK + TAIL
TERMS = 3


def tail_lane(h, term):
    return 8 * h + term


def constants():
    head = np.arange(BLOCK) // HEAD_DIM
    same = head[:, None] == head[None, :]
    extra = np.arange(EXTRA)
    key_lanes = extra[:, None] == OWN + head[None, :]
    value_lanes = extra[:, None] == 2 * OWN + head[None, :]
    to_query = np.zeros((TERMS, EXTRA, TAIL))
    to_key = np.zeros((TERMS, EXTRA, TAIL))
    from_tail = np.zeros((TAIL, EXTRA))
    for h in range(OWN):
        for term in range(TERMS):
            to_query[term, h, tail_lane(h, term)] = 1
            to_key[term, h, tail_lane(h, TERMS + term)] = -1
        from_tail[tail_lane(h, TERMS), h] = 1
    wide = np.concatenate([same, key_lanes, value_lanes], axis=0)
    tails = np.concatenate([to_query.reshape(-1, TAIL), to_key.reshape(-1, TAIL)], axis=0)
    backs = np.concatenate([key_lanes.T, value_lanes.T, from_tail], axis=0)
    return tuple(jnp.asarray(x, BF16) for x in (wide, tails, backs))


def places_of(lens_ref, bucket, rows):
    ends = []
    total = jnp.int32(0)
    for j in range(lens_ref.shape[1]):
        total = total + lens_ref[bucket, j]
        ends.append(total)

    def segment(place):
        seg = jnp.zeros(place.shape, jnp.int32)
        for end in ends:
            seg = seg + (end <= place).astype(jnp.int32)
        return seg

    col = iota((rows, 1), 0)
    row = iota((1, rows), 1)
    seg_col = segment(col)
    allowed = (col <= row) & (segment(row) == seg_col)
    live = (col < total).astype(F32)
    same_prev = ((col > 0) & (seg_col == segment(col - 1))).astype(F32)
    return allowed, live, same_prev


def front(lens_ref, proj, bias_ref, gains_ref, wide_ref, tails_ref, bucket):
    rows = proj.shape[0]
    allowed, live, same_prev = places_of(lens_ref, bucket, rows)
    q = proj[:, 0:BLOCK]
    k = proj[:, BLOCK : 2 * BLOCK]
    v = proj[:, 2 * BLOCK : 3 * BLOCK]
    og = proj[:, 3 * BLOCK : CORE]
    rate = proj[:, CORE:WIDE] + bias_ref[0:1, :]
    sig = jax.nn.sigmoid(rate)
    log_keep = jnp.minimum(rate, 0.0) - jnp.log1p(jnp.exp(-jnp.abs(rate)))
    upto = (iota((rows, rows), 1) <= iota((rows, rows), 0)).astype(BF16)
    decay = sum(dot(upto, term) for term in split(log_keep, TERMS))
    same_head = wide_ref[0:BLOCK]
    ak = dot_split(sig, wide_ref[BLOCK : BLOCK + EXTRA], 2)
    av = dot_split(sig, wide_ref[BLOCK + EXTRA :], 2)
    k_prev = pltpu.roll(k, 1, 0) * same_prev
    v_prev = pltpu.roll(v, 1, 0) * same_prev
    ks = ak * k_prev + (1.0 - ak) * k
    vs = av * v_prev + (1.0 - av) * v

    def head_norm(u):
        factor = lax.rsqrt(dot_split(u * u, same_head, 2) * (1.0 / HEAD_DIM) + EPS)
        return u * factor, factor

    qn, rq = head_norm(q)
    kn, rk = head_norm(ks)
    q_gain, k_gain = gains_ref[0:1, 0:BLOCK], gains_ref[1:2, 0:BLOCK]
    qb = (qn * q_gain).astype(BF16) * jnp.asarray(HEAD_DIM**-0.5, BF16)
    kb = (kn * k_gain).astype(BF16)

    terms = split(decay, TERMS)
    lane = iota((1, TAIL), 1)
    ones_q = ((lane % 8 >= TERMS) & (lane % 8 < 2 * TERMS)).astype(F32)
    ones_k = (lane % 8 < TERMS).astype(F32)
    q_tail = ones_q + sum(dot(terms[t], tails_ref[t * EXTRA : (t + 1) * EXTRA]) for t in range(TERMS))
    k_tail = ones_k + sum(
        dot(terms[t], tails_ref[(TERMS + t) * EXTRA : (TERMS + t + 1) * EXTRA]) for t in range(TERMS)
    )
    qx = jnp.concatenate([qb, q_tail.astype(BF16)], axis=1)
    kx = jnp.concatenate([kb, k_tail.astype(BF16)], axis=1)
    span = iota((rows, SPAN), 1)
    masks = []
    for h in range(OWN):
        feature = (span >= h * HEAD_DIM) & (span < (h + 1) * HEAD_DIM)
        masks.append(feature | ((span >= BLOCK + 8 * h) & (span < BLOCK + 8 * (h + 1))))
    return dict(
        rows=rows, allowed=allowed, live=live, same_prev=same_prev, k=k, v=v, og=og, sig=sig, masks=masks,
        same_head=same_head, ak=ak, av=av, k_prev=k_prev, v_prev=v_prev, qn=qn, rq=rq, kn=kn, rk=rk,
        q_gain=q_gain, k_gain=k_gain, qx=qx, kx=kx, ks_low=kb, vs=vs,
    )


def scores_of(f, h):
    qh = jnp.where(f["masks"][h], f["qx"], jnp.zeros_like(f["qx"]))
    return jnp.where(f["allowed"], dot(f["kx"], qh, ((1,), (1,))), NEG), qh


def head_rows(h):
    return slice(h * HEAD_DIM, (h + 1) * HEAD_DIM)


def attn_fwd_kernel(
    lens_ref, spots_ref, near_ref, far_ref, w_ref, bias_ref, wide_ref, tails_ref,
    h1_ref, proj_ref, mixed_ref, att_ref, lse_ref, gains_ref, heads_ref,
):
    picks = (iota((8, EXTRA), 1) == GAIN_AT + iota((8, EXTRA), 0)) & (iota((8, EXTRA), 0) < 4)
    picks = picks.astype(BF16)
    gains = dot(picks, w_ref[:, CORE:WIDE], ((1,), (1,)))
    gains_ref[...] = gains
    at = pl.multiple_of(spots_ref[0] * BLOCK, BLOCK)
    heads = dot(picks, w_ref[pl.ds(at, BLOCK), CORE:WIDE], ((1,), (1,)))
    heads_ref[0:1, 0:BLOCK] = heads[1:2]
    heads_ref[1:2, 0:BLOCK] = heads[2:3]
    tok = jnp.where(pl.program_id(0) < 4, near_ref[...], far_ref[...]).astype(F32)
    h1 = (normed(tok)[0] * gains[0:1]).astype(BF16)
    h1_ref[...] = h1
    proj_ref[...] = dot(h1, w_ref[...])
    f = front(lens_ref, proj_ref, bias_ref, heads_ref, wide_ref, tails_ref, pl.program_id(0))
    vt = f["vs"].T.astype(BF16)
    att = []
    for h in range(OWN):
        s, _ = scores_of(f, h)
        top = jnp.max(s, axis=0, keepdims=True)
        e = jnp.exp(s - top)
        total = jnp.sum(e, axis=0, keepdims=True)
        prob = (e * (1.0 / total)).astype(BF16)
        att.append(dot(vt[head_rows(h)], prob))
        lse_ref[h : h + 1, :] = top + jnp.log(total)
    att = jnp.concatenate(att, axis=0).T
    att_ref[...] = att
    mixed_ref[0] = fold(att * jax.nn.sigmoid(f["og"]) * f["live"]).astype(BF16)


def attn_bwd_kernel(
    lens_ref, spots_ref, proj_ref, bias_ref, gains_ref, wide_ref, tails_ref, backs_ref, w_ref,
    att_ref, lse_ref, dm_ref, dp_ref, sums_ref, near_ref, far_ref,
):
    bucket = pl.program_id(0)
    f = front(lens_ref, proj_ref, bias_ref, gains_ref, wide_ref, tails_ref, bucket)
    rows, same_head = f["rows"], f["same_head"]
    dm = unfold(dm_ref[0].astype(F32)) * f["live"]
    g = jax.nn.sigmoid(f["og"])
    dab = (dm * g).astype(BF16)
    dog = dm * att_ref[...] * g * (1.0 - g)
    vb = f["vs"].astype(BF16)
    kt = f["kx"][:, :BLOCK].astype(F32).T.astype(BF16)
    zero = jnp.zeros((rows, BLOCK), BF16)
    dkx = jnp.zeros((rows, SPAN), F32)
    dvb = jnp.zeros((rows, BLOCK), F32)
    tail = jnp.zeros((TAIL, rows), F32)
    dqt = []
    for h in range(OWN):
        s, qh = scores_of(f, h)
        p = jnp.exp(s - lse_ref[h : h + 1, :])
        dab_h = jnp.where(f["masks"][h][:, :BLOCK], dab, zero)
        dvb = dvb + dot(p.astype(BF16), dab_h)
        dp = dot(vb, dab_h, ((1,), (1,)))
        ds = p * (dp - jnp.sum(p * dp, axis=0, keepdims=True))
        dsb = ds.astype(BF16)
        dqt.append(dot(kt[head_rows(h)], dsb))
        dkx = dkx + dot(dsb, qh)
        along = jnp.sum(dsb.astype(F32), axis=0, keepdims=True)
        tail = jnp.where(iota((TAIL, rows), 0) == tail_lane(h, TERMS), along, tail)
    dqx = jnp.concatenate(dqt + [tail], axis=0).T
    dqb = dqx[:, :BLOCK] * HEAD_DIM**-0.5
    dkb = dkx[:, :BLOCK]

    def back(n, r, e):
        return r * (e - n * (dot_split(e * n, same_head, 2) * (1.0 / HEAD_DIM)))

    dq = back(f["qn"], f["rq"], dqb * f["q_gain"])
    dks = back(f["kn"], f["rk"], dkb * f["k_gain"])
    last = iota((rows, 1), 0) == rows - 1

    def mix_back(grad, rate, cur, prev):
        ahead = pltpu.roll(rate * grad * f["same_prev"], rows - 1, 0)
        return (1.0 - rate) * grad + jnp.where(last, 0.0, ahead), grad * (prev - cur)

    dk, dak = mix_back(dks, f["ak"], f["k"], f["k_prev"])
    dv, dav = mix_back(dvb, f["av"], f["v"], f["v_prev"])

    onward = (iota((rows, rows), 1) >= iota((rows, rows), 0)).astype(BF16)
    keep = sum(dot(onward, term) for term in split(dqx[:, BLOCK:] - dkx[:, BLOCK:], TERMS))
    sig = f["sig"]
    drate = (
        dot_split(dak, backs_ref[0:BLOCK], 2)
        + dot_split(dav, backs_ref[BLOCK : 2 * BLOCK], 2)
        + dot_split(keep, backs_ref[2 * BLOCK :], 2)
    )
    lane = iota((rows, EXTRA), 1)
    drate = drate * (1.0 - sig) * jnp.where(lane < OWN, 1.0, sig)
    drate = jnp.where(lane < RATES, drate, 0.0)
    grads = jnp.concatenate([dq, dk, dv, dog, drate], axis=1).astype(BF16)
    dp_ref[...] = grads
    dh1 = dot(grads, w_ref[...], ((1,), (1,))).astype(BF16)

    @pl.when(bucket < 4)
    def _():
        near_ref[...] = dh1

    @pl.when(bucket >= 4)
    def _():
        far_ref[...] = dh1

    @pl.when(bucket == 0)
    def _():
        sums_ref[...] = jnp.zeros_like(sums_ref)

    sums_ref[0:1, 0:BLOCK] += jnp.sum(dqb * f["qn"], axis=0, keepdims=True)
    sums_ref[1:2, 0:BLOCK] += jnp.sum(dkb * f["kn"], axis=0, keepdims=True)
    sums_ref[2:3, 0:EXTRA] += jnp.sum(drate, axis=0, keepdims=True)


def rows_spec(rows, width):
    return pl.BlockSpec((rows, width), lambda i, lens, spots: (i, 0))


def whole_spec(dims):
    return pl.BlockSpec(dims, lambda i, lens, spots: (0,) * len(dims))


def spot_spec(rows):
    return pl.BlockSpec((1, rows * 3 // 2, EXTRA), lambda i, lens, spots: (spots[i], 0, 0))


def attn_fwd(lens, spots, near, far, w, bias, wide, tails):
    buckets = lens.shape[0]
    width = near.shape[1]
    total = 2 * near.shape[0]
    rows = total // buckets
    return pl.pallas_call(
        attn_fwd_kernel,
        grid_spec=pltpu.PrefetchScalarGridSpec(
            num_scalar_prefetch=2,
            grid=(buckets,),
            in_specs=[
                near_spec(rows, width),
                far_spec(rows, width),
                whole_spec(w.shape),
                whole_spec(bias.shape),
                whole_spec(wide.shape),
                whole_spec(tails.shape),
            ],
            out_specs=[
                rows_spec(rows, width),
                rows_spec(rows, WIDE),
                spot_spec(rows),
                rows_spec(rows, BLOCK),
                rows_spec(8, rows),
                whole_spec((8, width)),
                whole_spec((8, 2 * EXTRA)),
            ],
        ),
        out_shape=[
            shape((total, width), BF16),
            shape((total, WIDE), F32),
            shape((buckets, rows * 3 // 2, EXTRA), BF16),
            shape((total, BLOCK), F32),
            shape((8 * buckets, rows), F32),
            shape((8, width), F32),
            shape((8, 2 * EXTRA), F32),
        ],
        **settings(20, 60),
        name="attn_fwd",
    )(lens, spots, near, far, w, bias, wide, tails)


def near_spec(rows, width):
    return pl.BlockSpec((rows, width), lambda i, lens, spots: (jnp.minimum(i, 3), 0))


def far_spec(rows, width):
    return pl.BlockSpec((rows, width), lambda i, lens, spots: (jnp.maximum(i - 4, 0), 0))


def attn_bwd(lens, spots, proj, bias, gains, wide, tails, backs, w, att, lse, dm):
    buckets = lens.shape[0]
    total = proj.shape[0]
    width = w.shape[0]
    rows = total // buckets
    return pl.pallas_call(
        attn_bwd_kernel,
        grid_spec=pltpu.PrefetchScalarGridSpec(
            num_scalar_prefetch=2,
            grid=(buckets,),
            in_specs=[rows_spec(rows, WIDE)]
            + [whole_spec(x.shape) for x in (bias, gains, wide, tails, backs, w)]
            + [rows_spec(rows, BLOCK), rows_spec(8, rows), spot_spec(rows)],
            out_specs=[
                rows_spec(rows, WIDE),
                whole_spec((8, 2 * EXTRA)),
                near_spec(rows, width),
                far_spec(rows, width),
            ],
        ),
        out_shape=[shape((total, WIDE), BF16), shape((8, 2 * EXTRA), F32)]
        + [shape((total // 2, width), BF16)] * 2,
        **settings(24, 60),
        name="attn_bwd",
    )(lens, spots, proj, bias, gains, wide, tails, backs, w, att, lse, dm)


def mid_fwd_kernel(spots_ref, got_ref, tok_ref, gain_ref, *refs):
    x2_ref, h2_ref = refs[TP:]
    acc = tok_ref[...].astype(F32)
    for i in range(TP):
        acc = acc + dot(unfold(got_ref[spots_ref[i]]), refs[i][0:BLOCK, :])
    x2_ref[...] = acc
    h2_ref[...] = (normed(acc)[0] * gain_ref[...]).astype(BF16)


def mid_fwd(spots, got, w, tok, gain):
    return pl.pallas_call(
        mid_fwd_kernel,
        in_specs=[SMEM] + [VMEM] * (3 + TP),
        out_specs=[VMEM, VMEM],
        out_shape=[shape(tok.shape, F32), shape(tok.shape, BF16)],
        **settings(6, 40),
        name="mid_fwd",
    )(spots, got, tok, gain, *w)


def mid_bwd_kernel(
    spots_ref, a_ref, b_ref, c_ref, d_ref, x2_ref, cot_ref, gain_ref, *refs
):
    dx2_ref, dxb_ref, dm_ref = refs[TP:]
    dh2 = a_ref[...] + b_ref[...].astype(F32) + c_ref[...].astype(F32) + d_ref[...].astype(F32)
    n2, r2 = normed(x2_ref[...])
    dx2 = cot_ref[...].astype(F32) + norm_back(n2, r2, dh2 * gain_ref[...])
    dx2_ref[...] = dx2
    dxb = dx2.astype(BF16)
    dxb_ref[...] = dxb
    for i in range(TP):
        dm = dot(dxb, refs[i][0:BLOCK, :], ((1,), (1,)))
        dm_ref[spots_ref[i]] = fold(dm).astype(BF16)


def mid_bwd(spots, parts, x2, cot, gain, w):
    rows, width = x2.shape
    return pl.pallas_call(
        mid_bwd_kernel,
        in_specs=[SMEM] + [VMEM] * (7 + TP),
        out_specs=[VMEM] * 3,
        out_shape=[shape((rows, width), F32), shape((rows, width), BF16), shape((TP, rows * 3 // 2, EXTRA), BF16)],
        **settings(8, 40),
        name="mid_bwd",
    )(spots, *parts, x2, cot, gain, *w)


def grad_mix_kernel(spots_ref, got_ref, dxb_ref, near_ref, far_ref):
    for i in range(TP):
        out_ref = near_ref if i < 4 else far_ref
        piece = dot(unfold(got_ref[spots_ref[i]]), dxb_ref[...], ((0,), (0,)))
        out_ref[(i % 4) * BLOCK : (i % 4 + 1) * BLOCK, :] = piece.astype(BF16)


def grad_mix(spots, got, dxb):
    width = dxb.shape[1]
    return pl.pallas_call(
        grad_mix_kernel,
        in_specs=[SMEM, VMEM, VMEM],
        out_specs=[VMEM, VMEM],
        out_shape=[shape((4 * BLOCK, width), BF16)] * 2,
        **settings(4, 40),
        name="grad_mix",
    )(spots, got, dxb)


def ffn_kernel(lens_ref, h2_ref, cot_ref, gu_ref, dn_ref, ab_ref, dgu_ref, out_ref, dh2_ref):
    rows, ff = h2_ref.shape[0], dn_ref.shape[0]
    total = jnp.int32(0)
    for j in range(lens_ref.shape[1]):
        total = total + lens_ref[pl.program_id(0), j]
    live = (iota((rows, 1), 0) < total).astype(F32)
    gu = dot(h2_ref[...], gu_ref[...])
    da = dot(cot_ref[...], dn_ref[...], ((1,), (1,))) * live
    gate, up = gu[:, :ff], gu[:, ff:]
    sg = jax.nn.sigmoid(gate)
    act = gate * sg
    ab = (act * up * live).astype(BF16)
    dgate = (da * up * sg * (1.0 + gate * (1.0 - sg))).astype(BF16)
    dup = (da * act).astype(BF16)
    ab_ref[...] = ab
    dgu_ref[:, :ff] = dgate
    dgu_ref[:, ff:] = dup
    dh2 = dot(dgate, gu_ref[:, :ff], ((1,), (1,))) + dot(dup, gu_ref[:, ff:], ((1,), (1,)))
    dh2_ref[...] = dh2.astype(BF16)
    out_ref[...] = dot(ab, dn_ref[...]).astype(BF16)


def ffn(lens, h2, cot, gu, dn):
    buckets = lens.shape[0]
    total, width = h2.shape
    rows = total // buckets
    ff = dn.shape[0]

    def block(columns):
        return pl.BlockSpec((rows, columns), lambda i: (i, 0))

    def whole(dims):
        return pl.BlockSpec(dims, lambda i: (0, 0))

    outs = (ff, 2 * ff, width, width)
    return pl.pallas_call(
        ffn_kernel,
        grid=(buckets,),
        in_specs=[SMEM, block(width), block(width), whole(gu.shape), whole(dn.shape)],
        out_specs=[block(c) for c in outs],
        out_shape=[shape((total, c), BF16) for c in outs],
        **settings(4 * buckets, 40),
        name="ffn",
    )(lens, h2, cot, gu, dn)


def grad_down(ab, cot):
    ff, width = ab[0].shape[1], cot[0].shape[1]
    steps = 4
    columns = width // steps

    def kernel(ab0_ref, ab1_ref, cot0_ref, cot1_ref, out_ref):
        res = dot(ab0_ref[...], cot0_ref[...], ((0,), (0,))) + dot(ab1_ref[...], cot1_ref[...], ((0,), (0,)))
        out_ref[...] = res.astype(BF16)

    return pl.pallas_call(
        kernel,
        grid=(steps,),
        in_specs=[pl.BlockSpec(x.shape, lambda i: (0, 0)) for x in ab]
        + [pl.BlockSpec((x.shape[0], columns), lambda i: (0, i)) for x in cot],
        out_specs=pl.BlockSpec((ff, columns), lambda i: (0, i)),
        out_shape=shape((ff, width), BF16),
        **settings(6, 60),
        name="grad_down",
    )(*ab, *cot)


def grad_gu(h2, dgu, share):
    rows, width = h2[0].shape
    own_rows = width // (TP * share)
    columns = dgu[0].shape[1]
    steps = TP // 2

    def kernel(left0_ref, left1_ref, right0_ref, right1_ref, out_ref):
        res = dot(left0_ref[...], right0_ref[...], ((0,), (0,)))
        res = res + dot(left1_ref[...], right1_ref[...], ((0,), (0,)))
        for k in range(2):
            for z in range(share):
                at = (k * share + z) * own_rows
                out_ref[z, k] = res[at : at + own_rows].astype(BF16)

    return pl.pallas_call(
        kernel,
        grid=(steps,),
        in_specs=[pl.BlockSpec((rows, width // steps), lambda i: (0, i))] * 2
        + [pl.BlockSpec((rows, columns), lambda i: (0, 0))] * 2,
        out_specs=pl.BlockSpec((share, 2, own_rows, columns), lambda i: (0, i, 0, 0)),
        out_shape=shape((share, TP, own_rows, columns), BF16),
        **settings(11, 60),
        name="grad_gu",
    )(*h2, *dgu)


def grad_in(place, sums, left, right, share):
    own_rows = left.shape[1] // (TP * share)
    columns = right.shape[1]
    steps = TP // 2

    def kernel(place_ref, sums_ref, left_ref, right_ref, out_ref):
        res = dot(left_ref[...], right_ref[...], ((0,), (0,)))
        lane, row = iota((BLOCK, EXTRA), 1), iota((BLOCK, EXTRA), 0)
        turned = sums_ref[...].T[0:BLOCK]
        bias = jnp.where((lane == row % own_rows) & (lane < RATES), sums_ref[2:3, 0:EXTRA], 0.0)
        bias = jnp.sum(bias, axis=1, keepdims=True)
        for k in range(2):
            mine = (pl.program_id(0) * 2 + k == place_ref[0]).astype(F32)
            extra = res[k * BLOCK : (k + 1) * BLOCK, CORE:WIDE]
            extra = jnp.where(lane == RATES, turned[:, 0:1] * mine, extra)
            extra = jnp.where(lane == RATES + 1, turned[:, 1:2] * mine, extra)
            extra = jnp.where(lane == RATES + 2, bias, extra)
            for z in range(share):
                at = z * own_rows
                rest = k * BLOCK + at
                out_ref[z, k, :, :CORE] = res[rest : rest + own_rows, :CORE].astype(BF16)
                out_ref[z, k, :, CORE:] = extra[at : at + own_rows].astype(BF16)

    return pl.pallas_call(
        kernel,
        grid=(steps,),
        in_specs=[
            SMEM,
            pl.BlockSpec(sums.shape, lambda i: (0, 0)),
            pl.BlockSpec((left.shape[0], left.shape[1] // steps), lambda i: (0, i)),
            pl.BlockSpec(right.shape, lambda i: (0, 0)),
        ],
        out_specs=pl.BlockSpec((share, 2, own_rows, columns), lambda i: (0, i, 0, 0)),
        out_shape=shape((share, TP, own_rows, columns), BF16),
        **settings(11, 60),
        name="grad_in",
    )(place, sums, left, right)


def own_share(part):
    columns = part.shape[-1]
    summed = lax.psum_scatter(part.reshape(-1, columns), "sh", scatter_dimension=0, tiled=True)
    return summed.reshape(TP, -1, columns)


def swap(blocks):
    return lax.all_to_all(blocks, "tp", 0, 0, tiled=True)


def body(
    tokens,
    doc_lengths,
    norm_gain,
    w_attn_in,
    w_rates,
    rate_bias,
    q_gain,
    k_gain,
    w_out,
    ffn_gain,
    w_gate_up,
    w_down,
    cotangent,
):
    place = lax.axis_index("tp")
    share = lax.axis_size("sh")
    width = tokens.shape[1]
    own_rows = w_attn_in.shape[0]
    spots = place ^ jnp.array(OFFSETS, jnp.int32)

    gains = jnp.stack([norm_gain, q_gain, k_gain, ffn_gain])
    packed, w_mix = phase(pack_in(doc_lengths, w_attn_in, w_rates, gains), w_out)
    got_in, w_mix = phase(swap(packed), gather_shares(w_mix))
    w_in = lax.all_gather(got_in, "sh", axis=1).reshape(width, WIDE)
    lens_all = got_in[:, 0, CORE + LENS_AT : CORE + LENS_AT + doc_lengths.shape[0]].astype(jnp.int32)
    lens = lens_all[spots]
    bias = lax.dynamic_index_in_dim(rate_bias.reshape(3, TP, OWN), place, 1, False).reshape(1, RATES)
    bias = jnp.pad(bias, ((0, 7), (0, EXTRA - RATES)))

    tok, w_gu, _ = phase(tokens, w_gate_up, got_in)
    two_four = sides(tok)
    tok = join_rows(tok, *two_four, *diagonal(*two_four))
    tok, packed = phase(tok, pack_gu(w_gu))
    joined = join_ffn(swap(packed), w_down)
    far = flip(tok, 1)
    w_gu, w_dn = open_ffn(lax.all_gather(joined, "sh", axis=0), w_down.shape[0], width)

    wide, tails, backs = constants()
    beside = phase(join_rows(in_order(w_mix), cotangent), joined)[0]
    two_four = sides(beside)
    h1, proj, mixed, att, lse, gains, gain_heads = attn_fwd(lens, spots, tok, far, w_in, bias, wide, tails)
    gain_one, gain_two = gains[0:1], gains[3:4]
    mixed, two_four = phase(mixed, two_four)
    near = [beside, *two_four]
    six = diagonal(*two_four)
    got_mixed, six, far = phase(swap(mixed), six, [flip(x, 1) for x in near])
    far = [*far, *[flip(x, 1) for x in six]]
    near = [*near, *six]
    x2, h2 = mid_fwd(spots, got_mixed, near[:4] + far[:4], tokens, gain_two)

    h2, near, far = phase(h2, near, far)
    w_mix = near[:4] + far[:4]
    two_four = sides(h2)
    cot = [join_rows(*[(x, BLOCK) for x in half[:4]], half[4]) for half in (near, far)]
    two_four, cot = phase(two_four, cot)
    h2 = join_rows(h2, *two_four, *diagonal(*two_four))
    h2_far, found_near = phase(flip(h2, 1), ffn(lens[:4], h2, cot[0], w_gu, w_dn))
    h2 = h2, h2_far
    found_far = ffn(lens[4:], h2_far, cot[1], w_gu, w_dn)
    ab, dgu, out, dh2 = phase(*zip(found_near, found_far))
    dh2_far, dw_dn, out_far = phase(flip(dh2[1], 1), grad_down(ab, cot), flip(out[1], 1))
    own, low = both_cores(dh2[0], dh2_far)
    dw_dn = lax.psum_scatter(dw_dn, "sh", scatter_dimension=0, tiled=True)
    own, low, dgu, out_far = phase(own, low, dgu, out_far)
    layer_own, layer_low = both_cores(out[0], out_far)
    dh2, dw_gu, dw_dn, own, layer_low = phase(send(low), grad_gu(h2, dgu, share), dw_dn, own, layer_low)
    dw_gu = own_share(dw_gu)

    dx2, dxb, dm = mid_bwd(spots, [own] + dh2, x2, cotangent, gain_two, w_mix)
    dxb, dm = phase(dxb, dm)
    got_dm, mix, layer_low = phase(swap(dm), grad_mix(spots, got_mixed, dxb), layer_low)
    layer, mix_far, found, dw_gu = phase(
        send(layer_low),
        flip(mix[1], 1),
        attn_bwd(lens, spots, proj, bias, gain_heads, wide, tails, backs, w_in, att, lse, got_dm),
        dw_gu,
    )
    dp, sums, dh1_near, dh1_far = found
    layer_out = (x2 + total_of([layer_own] + layer)).astype(BF16)

    mix_own, low = both_cores(mix[0], mix_far)
    dh1_far, low, dw_in, got_gu = phase(
        flip(dh1_far, 1), relay_six(low), grad_in(place.reshape(1), sums, h1, dp, share), swap(dw_gu)
    )
    dw_in = own_share(dw_in)
    low = add_six(low)
    dh1_own, dh1_low = both_cores(dh1_near, dh1_far)
    low, dh1_low = phase(low, dh1_low)
    dh1, mix, dw_in = phase(send(dh1_low), (flip(low[0], 2), flip(low[1], 4)), dw_in)
    got_in_grad, mix = phase(swap(dw_in), to_shares(total_of((mix_own, *mix)).astype(BF16)))
    n1, r1 = normed(tokens.astype(F32))
    d_tokens = dx2 + norm_back(n1, r1, total_of([dh1_own] + dh1) * gain_one)

    d_w_attn_in, d_w_rates, small = unpack_in(got_in_grad, w_attn_in, w_rates, norm_gain)
    d_w_gate_up, small_gu = unpack_gu(got_gu, w_gate_up, ffn_gain)
    d_ffn_gain = small_gu[0, :own_rows]
    d_w_out = total_of(mix)
    return (
        layer_out,
        d_tokens,
        small[0, :own_rows],
        d_w_attn_in,
        d_w_rates,
        small[3, : w_rates.shape[1]],
        small[1, :own_rows],
        small[2, :own_rows],
        d_w_out,
        d_ffn_gain,
        d_w_gate_up,
        dw_dn.astype(F32),
    )


def solution(mesh):
    devices = mesh.devices.reshape(TP, -1)
    grid = Mesh(devices, ("tp", "sh"))
    rows = P(("tp", "sh"), None)
    flat = P(("tp", "sh"))
    in_specs = (rows, flat, flat, rows, rows, P(), flat, flat, rows, flat, rows, rows, rows)
    out_specs = (rows, rows, flat, rows, rows, P(), flat, flat, rows, flat, rows, rows)
    return jax.shard_map(body, mesh=grid, in_specs=in_specs, out_specs=out_specs, check_vma=False)
```

time: 668 us -> 480 us (0.72)
  waiting for transfers between devices: 276 us -> 160 us
  Pallas kernels: 53.3 us -> 153 us
  matrix products: 79.1 us -> 0 us
  local copies, waits for them, and re-layouts: 99.4 us -> 49.8 us
  blocking collectives: 38.2 us -> 0 us
  other arithmetic: 59.9 us -> 30.1 us
  starting transfers between devices: 42.8 us -> 70.4 us
    ppermute x32 -> x36, waiting for transfers between devices: 229 us -> 117 us  [flip(): return lax.ppermute(array, 'tp', [(i, i ^ offset) for i in range(TP)])]
    pallas_call x2 -> x21, Pallas kernels: 53.3 us -> 153 us  [the longest x1 34.3 us: attn_bwd(): pl.pallas_call(attn_bwd_kernel, grid_spec=pltpu.PrefetchScalarGridSpec(nu...]
    dot_general x11 -> x0, matrix products: 79.1 us -> none  [dot(): lax.dot_general(a, b, (dims, ((), ())), precision=precision, preferred_el...]
    all_gather x1, waiting for transfers between devices: 24.4 us -> 0.01 us  [body(): w_in = lax.all_gather(got_in, 'sh', axis=1).reshape(width, WIDE)]
    all_gather x1 -> x0, blocking collectives: 21.4 us -> none  [body(): w_mix = lax.all_gather(w_out, 'sh', axis=0, tiled=True)]
    all_to_all x3 -> x6, waiting for transfers between devices: 10.1 us -> 29.8 us  [swap(): return lax.all_to_all(blocks, 'tp', 0, 0, tiled=True)]
    concatenate x8 -> x0, local copies, waits for them, and re-layouts: 18.6 us -> none  [the longest x4 15.5 us: gather_rows(): return jnp.concatenate([half, flip(half, 1)], axis=0)]
    all_to_all x1 -> x0, blocking collectives: 16.8 us -> none  [body(): got_gu = lax.all_to_all(columns_out(w_gate_up, 2), 'tp', 0, 0, tiled=True)]
  transfers between devices with their start and end apart: 42 -> 53, of which waited for: 25 -> 22; matrix products, arithmetic and copies ran while one was open for 28% -> 8% of each run, Pallas kernels for 5% -> 28%
where the time goes in v2:
time: 480 us; the launch traced here: 477 us
  waiting for transfers between devices  160 us (33%)
  Pallas kernels  153 us (32%)
  starting transfers between devices  70.4 us (15%)
  local copies, waits for them, and re-layouts  49.8 us (10%)
  other arithmetic  30.1 us (6%)
  between operations  14.6 us (3%)
    ppermute x36, waiting for transfers between devices, flip(): return lax.ppermute(array, 'tp', [(i, i ^ offset) for i in range(TP)])  117 us
    unnamed x128, local copies, waits for them, and re-layouts  38.4 us
    pallas_call x1, Pallas kernels, attn_bwd(): pl.pallas_call(attn_bwd_kernel, grid_spec=pltpu.PrefetchScalarGridSpec(nu...  34.3 us
    ppermute x36, starting transfers between devices, flip(): return lax.ppermute(array, 'tp', [(i, i ^ offset) for i in range(TP)])  32.3 us
    all_to_all x6, waiting for transfers between devices, swap(): return lax.all_to_all(blocks, 'tp', 0, 0, tiled=True)  29.8 us
    pallas_call x1, Pallas kernels, attn_fwd(): pl.pallas_call(attn_fwd_kernel, grid_spec=pltpu.PrefetchScalarGridSpec(nu...  28.6 us
    pallas_call x2, Pallas kernels, ffn(): pl.pallas_call(ffn_kernel, grid=(buckets,), in_specs=[SMEM, block(width),...  28.2 us
    all_to_all x6, starting transfers between devices, swap(): return lax.all_to_all(blocks, 'tp', 0, 0, tiled=True)  25.3 us
  transfers between devices with their start and end apart: 53, of which 22 were waited for; matrix products, arithmetic and copies ran while one was open for 8% of the time, Pallas kernels for 28%

profile of v2, /device:TPU:0, one launch (start us, length us, event | category | flops | bytes accessed | tf_op | source)
XLA Modules:
  0.0 477.5 jit_solution(12687006626730956542)
XLA Ops:
  12.0 5.3 %all-to-all-start = ((bf16[8,48,896]{2,1,0:T(8,128)(2,1)}), bf16[8,48,896]{2,1,0:T(8,128)(2,1)S(1)}, u32[]{:S(2)}, u32[]{:S(2)}) async-start(bf16[8,48,896]{2,1,0:T(8,128)(2,1)} %pack_in.1), calls=%async_computation | async-start | bytes 1376256 | tf_op jit(solution)/shard_map/all_to_all | solution.py:868
  25.9 5.9 %collective-permute-done.1 = bf16[48,1536]{1,0:T(8,128)(2,1)S(1)} collective-permute-done((bf16[48,1536]{1,0:T(8,128)(2,1)S(1)}, bf16[48,1536]{1,0:T(8,128)(2,1)S(1)}, u32[]{:S(2)}, u32[]{:S(2)}) %collective-permute-start.1) | collective-permute-done | bytes 147488 | tf_op jit(solution)/shard_map/ppermute | solution.py:71
  36.6 16.3 %collective-permute-done.3.refs_1_ = bf16[256,1536]{1,0:T(8,128)(2,1)S(1)} collective-permute-done((bf16[256,1536]{1,0:T(8,128)(2,1)S(1)}, bf16[256,1536]{1,0:T(8,128)(2,1)S(1)}, u32[]{:S(2)}, u32[]{:S(2)}) %collective-permute-start.3) | collective-permute-done | bytes 786464 | tf_op jit(solution)/shard_map/ppermute | solution.py:29
  58.5 5.6 %collective-permute-done.5.refs_3_ = bf16[128,1536]{1,0:T(8,128)(2,1)S(1)} collective-permute-done((bf16[128,1536]{1,0:T(8,128)(2,1)}, bf16[128,1536]{1,0:T(8,128)(2,1)S(1)}, u32[]{:S(2)}, u32[]{:S(2)}) %collective-permute-start.5) | collective-permute-done | bytes 393248 | tf_op jit(solution)/shard_map/ppermute | solution.py:29
  69.3 4.4 all-to-all-start.1
  74.8 11.5 %all-to-all-done.1.got_ref = bf16[8,48,1024]{2,1,0:T(8,128)(2,1)} async-done(((bf16[8,48,1024]{2,1,0:T(8,128)(2,1)}), bf16[8,48,1024]{2,1,0:T(8,128)(2,1)}, u32[]{:S(2)}, u32[]{:S(2)}) %all-to-all-start.1) | async-done | bytes 786464 | tf_op jit(solution)/shard_map/all_to_all | solution.py:868
  94.6 28.6 %attn_fwd.1 = (bf16[2048,1536]{1,0:T(8,128)(2,1)}, f32[2048,896]{1,0:T(8,128)}, bf16[8,384,128]{2,1,0:T(8,128)(2,1)}, f32[2048,192]{1,0:T(8,128)}, f32[64,256]{1...) custom-call(s32[8,4]{1,0:T(8,128)} %gather_fusion, s32[8]{0:T(128)} %get-tuple-element.321.spots_ref, ...), custom_call_target="tpu_custom_call" | custom-call | flops 200000000 | bytes 200000 | tf_op jit(solution)/shard_map/attn_fwd/pallas_call | solution.py:591
  134.4 9.7 %all-to-all-done.2.got_ref = bf16[8,384,128]{2,1,0:T(8,128)(2,1)} async-done(((bf16[8,384,128]{2,1,0:T(8,128)(2,1)}), bf16[8,384,128]{2,1,0:T(8,128)(2,1)}, u32[]{:S(2)}, u32[]{:S(2)}) %all-to-all-start.2) | async-done | bytes 786464 | tf_op jit(solution)/shard_map/all_to_all | solution.py:868
  144.2 13.3 %collective-permute-done.10.refs_3_ = bf16[224,1536]{1,0:T(8,128)(2,1)} collective-permute-done((bf16[224,1536]{1,0:T(8,128)(2,1)}, bf16[224,1536]{1,0:T(8,128)(2,1)}, u32[]{:S(2)}, u32[]{:S(2)}) %collective-permute-start.10) | collective-permute-done | bytes 688160 | tf_op jit(solution)/shard_map/ppermute | solution.py:29
  159.9 5.2 %mid_fwd.1 = (f32[256,1536]{1,0:T(8,128)S(1)}, bf16[256,1536]{1,0:T(8,128)(2,1)S(1)}) custom-call(s32[8]{0:T(128)S(1)} %copy-done.42, bf16[8,384,128]{2,1,0:T(8,128)(2,1)} %all-to-all-done.2.got_ref, bf16[256,1536]{1,0:T(8,128)(2,1)S(1)} %copy-done.5, f32[1,1536]{1,0:T(1,128)S(1)} %get-tuple-element.314.gain_ref, bf16[448,1536]{1,0:T(8,128)(2,1)S(1)} %join_rows.6.refs_0_, ...), custom_call_target="tpu_custom_call" | custom-call | flops 60000000 | bytes 60000 | tf_op jit(solution)/shard_map/mid_fwd/pallas_call | solution.py:673
  174.9 9.9 %collective-permute-done.17.refs_1_ = bf16[256,1536]{1,0:T(8,128)(2,1)S(1)} collective-permute-done((bf16[256,1536]{1,0:T(8,128)(2,1)S(1)}, bf16[256,1536]{1,0:T(8,128)(2,1)S(1)}, u32[]{:S(2)}, u32[]{:S(2)}) %collective-permute-start.17) | collective-permute-done | bytes 786464 | tf_op jit(solution)/shard_map/ppermute | solution.py:29
  188.2 7.8 %collective-permute-done.19.refs_3_ = bf16[128,1536]{1,0:T(8,128)(2,1)S(1)} collective-permute-done((bf16[128,1536]{1,0:T(8,128)(2,1)S(1)}, bf16[128,1536]{1,0:T(8,128)(2,1)S(1)}, u32[]{:S(2)}, u32[]{:S(2)}) %collective-permute-start.19) | collective-permute-done | bytes 393248 | tf_op jit(solution)/shard_map/ppermute | solution.py:29
  202.3 13.6 %ffn.2 = (bf16[1024,512]{1,0:T(8,128)(2,1)S(1)}, bf16[1024,1024]{1,0:T(8,128)(2,1)S(1)}, bf16[1024,1536]{1,0:T(8,128)(2,1)S(1)}, bf16[1024,1536]{1,0:T(8,128)(2,1)S(1)}) custom-call(s32[4,4]{1,0:T(4,128)S(1)} %get-tuple-element.319.lens_ref, bf16[1024,1536]{1,0:T(8,128)(2,1)S(1)} %join_rows.9.h2_ref.left0_ref, bf16[1024,1536]{1,0:T(8,128)(2,1)} %copy-done, ...), custom_call_target="tpu_custom_call" | custom-call | flops 160000000 | bytes 160000 | tf_op jit(solution)/shard_map/ffn/pallas_call | solution.py:764
  221.5 14.7 %ffn.3 = (bf16[1024,512]{1,0:T(8,128)(2,1)S(1)}, bf16[1024,1024]{1,0:T(8,128)(2,1)S(1)}, bf16[1024,1536]{1,0:T(8,128)(2,1)}, bf16[1024,1536]{1,0:T(8,128)(2,1)}) custom-call(s32[4,4]{1,0:T(4,128)S(1)} %get-tuple-element.318.lens_ref, bf16[1024,1536]{1,0:T(8,128)(2,1)} %collective-permute-done.21.h2_ref.left1_ref, bf16[1024,1536]{1,0:T(8,128)(2,1)} %copy-done.1, ...), custom_call_target="tpu_custom_call" | custom-call | flops 160000000 | bytes 160000 | tf_op jit(solution)/shard_map/ffn/pallas_call | solution.py:764
  239.0 8.4 %grad_down.1 = bf16[512,1536]{1,0:T(8,128)(2,1)} custom-call(bf16[1024,512]{1,0:T(8,128)(2,1)} %copy-done.28, bf16[1024,512]{1,0:T(8,128)(2,1)} %copy-done.29, bf16[1024,1536]{1,0:T(8,128)(2,1)} %copy-done, bf16[1024,1536]{1,0:T(8,128)(2,1)} %copy-done.1), custom_call_target="tpu_custom_call" | custom-call | flops 60000000 | bytes 60000 | tf_op jit(solution)/shard_map/grad_down/pallas_call | solution.py:784
  249.3 4.3 add_convert_fusion.7
  257.1 11.0 %grad_gu.1 = bf16[4,8,48,1024]{3,2,1,0:T(8,128)(2,1)} custom-call(bf16[1024,1536]{1,0:T(8,128)(2,1)} %copy-done.2, bf16[1024,1536]{1,0:T(8,128)(2,1)} %collective-permute-done.21.h2_ref.left1_ref, bf16[1024,1024]{1,0:T(8,128)(2,1)} %copy-done.26, bf16[1024,1024]{1,0:T(8,128)(2,1)} %copy-done.27), custom_call_target="tpu_custom_call" | custom-call | flops 110000000 | bytes 110000 | tf_op jit(solution)/shard_map/grad_gu/pallas_call | solution.py:810
  275.1 16.3 %collective-permute-done.25.c_ref = bf16[256,1536]{1,0:T(8,128)(2,1)S(1)} collective-permute-done((bf16[256,1536]{1,0:T(8,128)(2,1)}, bf16[256,1536]{1,0:T(8,128)(2,1)S(1)}, u32[]{:S(2)}, u32[]{:S(2)}) %collective-permute-start.25) | collective-permute-done | bytes 786464 | tf_op jit(solution)/shard_map/ppermute | solution.py:29
  299.6 7.1 %mid_bwd.1 = (f32[256,1536]{1,0:T(8,128)}, bf16[256,1536]{1,0:T(8,128)(2,1)S(1)}, bf16[8,384,128]{2,1,0:T(8,128)(2,1)S(1)}) custom-call(s32[8]{0:T(128)S(1)} %copy-done.42, f32[256,1536]{1,0:T(8,128)} %get-tuple-element.226.a_ref, bf16[256,1536]{1,0:T(8,128)(2,1)S(1)} %copy-done.31, bf16[256,1536]{1,0:T(8,128)(2,1)S(1)} %copy-done.33, ...), custom_call_target="tpu_custom_call" | custom-call | flops 80000000 | bytes 80000 | tf_op jit(solution)/shard_map/mid_bwd/pallas_call | solution.py:700
  308.6 4.3 all-to-all-start.3
  316.9 8.6 %all-to-all-done.3.dm_ref = bf16[8,384,128]{2,1,0:T(8,128)(2,1)} async-done(((bf16[8,384,128]{2,1,0:T(8,128)(2,1)}), bf16[8,384,128]{2,1,0:T(8,128)(2,1)}, u32[]{:S(2)}, u32[]{:S(2)}) %all-to-all-start.3) | async-done | bytes 786464 | tf_op jit(solution)/shard_map/all_to_all | solution.py:868
  329.0 34.3 %attn_bwd.1 = (bf16[2048,896]{1,0:T(8,128)(2,1)}, f32[8,256]{1,0:T(8,128)}, bf16[1024,1536]{1,0:T(8,128)(2,1)}, bf16[1024,1536]{1,0:T(8,128)(2,1)}) custom-call(s32[8,4]{1,0:T(8,128)} %gather_fusion, s32[8]{0:T(128)} %get-tuple-element.321.spots_ref, f32[2048,896]{1,0:T(8,128)} %get-tuple-element.243.proj_ref, f32[8,128]{1,0:T(8,128)} %pad.15.bias_ref, ...), custom_call_target="tpu_custom_call" | custom-call | flops 240000000 | bytes 240000 | tf_op jit(solution)/shard_map/attn_bwd/pallas_call | solution.py:641
  373.6 10.9 %grad_in.1 = bf16[4,8,48,896]{3,2,1,0:T(8,128)(2,1)} custom-call(s32[1]{0:T(128)} %bitcast.14.place_ref, f32[8,256]{1,0:T(8,128)} %get-tuple-element.261.sums_ref, bf16[2048,1536]{1,0:T(8,128)(2,1)} %get-tuple-element.262.left_ref, bf16[2048,896]{1,0:T(8,128)(2,1)} %get-tuple-element.263.right_ref), custom_call_target="tpu_custom_call" | custom-call | flops 110000000 | bytes 110000 | tf_op jit(solution)/shard_map/grad_in/pallas_call | solution.py:845
  403.1 37.7 %collective-permute-done.37 = bf16[192,1536]{1,0:T(8,128)(2,1)S(1)} collective-permute-done((bf16[192,1536]{1,0:T(8,128)(2,1)S(1)}, bf16[192,1536]{1,0:T(8,128)(2,1)S(1)}, u32[]{:S(2)}, u32[]{:S(2)}) %collective-permute-start.37) | collective-permute-done | bytes 589856 | tf_op jit(solution)/shard_map/ppermute | solution.py:29
  (283 shorter events, 168.2 us)
Async XLA Ops:
  17.3 77.3 %all-gather.5.cloned.1.call-start = ((), (), s32[]{:S(2)}) async-start(), calls=%async_computation.12 | async-start | bytes 3440640 | tf_op jit(solution)/shard_map/all_gather | solution.py:895
  69.2 25.4 %collective-permute-start.7 = (bf16[1024,1536]{1,0:T(8,128)(2,1)}, bf16[1024,1536]{1,0:T(8,128)(2,1)}, u32[]{:S(2)}, u32[]{:S(2)}) collective-permute-start(bf16[1024,1536]{1,0:T(8,128)(2,1)} %join_rows.5.near_ref), channel_id=1, source_target_pairs={{0,4},{4,0},{8,12},{12,8},{16,20},{20,16},{24,28},{28,24},{1,5},{5... | collective-permute-start | bytes 9437192 | tf_op jit(solution)/shard_map/ppermute | solution.py:29
  73.7 123.2 %all-gather.7.cloned.1.call-start = ((), (), s32[]{:S(2)}) async-start(), calls=%async_computation.13 | async-start | bytes 5898240 | tf_op jit(solution)/shard_map/all_gather | solution.py:907
  89.5 33.7 %collective-permute-start.8 = (bf16[448,1536]{1,0:T(8,128)(2,1)S(1)}, bf16[448,1536]{1,0:T(8,128)(2,1)S(1)}, u32[]{:S(2)}, u32[]{:S(2)}) collective-permute-start(bf16[448,1536]{1,0:T(8,128)(2,1)S(1)} %join_rows.6.refs_0_), channel_id=1, source_target_pairs={{0,8},{4,12},{8,0},{12,4},{16,24},{20,28},{24,16},{28,20},{1,9},{5... | collective-permute-start | bytes 4128776 | tf_op jit(solution)/shard_map/ppermute | solution.py:29
  90.0 33.2 %collective-permute-start.9 = (bf16[448,1536]{1,0:T(8,128)(2,1)S(1)}, bf16[448,1536]{1,0:T(8,128)(2,1)}, u32[]{:S(2)}, u32[]{:S(2)}) collective-permute-start(bf16[448,1536]{1,0:T(8,128)(2,1)S(1)} %join_rows.6.refs_0_), channel_id=1, source_target_pairs={{0,16},{4,20},{8,24},{12,28},{16,0},{20,4},{24,8},{28,12},{1,17},{... | collective-permute-start | bytes 4128776 | tf_op jit(solution)/shard_map/ppermute | solution.py:29
  94.6 39.8 %collective-permute-start.12 = (bf16[448,1536]{1,0:T(8,128)(2,1)S(1)}, bf16[448,1536]{1,0:T(8,128)(2,1)}, u32[]{:S(2)}, u32[]{:S(2)}) collective-permute-start(bf16[448,1536]{1,0:T(8,128)(2,1)S(1)} %join_rows.6.refs_0_), channel_id=1, source_target_pairs={{0,4},{4,0},{8,12},{12,8},{16,20},{20,16},{24,28},{28,24},{1,5},{5... | collective-permute-start | bytes 4128776 | tf_op jit(solution)/shard_map/ppermute | solution.py:29
  123.3 34.2 %collective-permute-start.13 = (bf16[448,1536]{1,0:T(8,128)(2,1)S(1)}, bf16[448,1536]{1,0:T(8,128)(2,1)}, u32[]{:S(2)}, u32[]{:S(2)}) collective-permute-start(bf16[448,1536]{1,0:T(8,128)(2,1)S(1)} %collective-permute-done.8.refs_1_), channel_id=1, source_target_pairs={{0,4},{4,0},{8,12},{12,8},{16,20},{20,16},{24,28},{28,24},{1,5},{5... | collective-permute-start | bytes 4128776 | tf_op jit(solution)/shard_map/ppermute | solution.py:29
  123.8 33.7 %collective-permute-start.14 = (bf16[448,1536]{1,0:T(8,128)(2,1)}, bf16[448,1536]{1,0:T(8,128)(2,1)}, u32[]{:S(2)}, u32[]{:S(2)}) collective-permute-start(bf16[448,1536]{1,0:T(8,128)(2,1)} %collective-permute-done.9.refs_2_), channel_id=1, source_target_pairs={{0,4},{4,0},{8,12},{12,8},{16,20},{20,16},{24,28},{28,24},{1,5},{5... | collective-permute-start | bytes 4128776 | tf_op jit(solution)/shard_map/ppermute | solution.py:29
  131.0 162.2 %reduce-scatter.4.cloned.1.call-start = ((), (), s32[]{:S(2)}) async-start(), calls=%async_computation.9 | async-start | bytes 1966080 | tf_op jit(solution)/shard_map/reduce_scatter | solution.py:934
  131.3 26.2 %collective-permute-start.10 = (bf16[224,1536]{1,0:T(8,128)(2,1)}, bf16[224,1536]{1,0:T(8,128)(2,1)}, u32[]{:S(2)}, u32[]{:S(2)}) collective-permute-start(bf16[224,1536]{1,0:T(8,128)(2,1)} %slice.165), channel_id=1, source_target_pairs={{0,16},{4,20},{8,24},{12,28},{16,0},{20,4},{24,8},{28,12},{1,17},{... | collective-permute-start | bytes 2064392 | tf_op jit(solution)/shard_map/ppermute | solution.py:29
  196.8 24.8 %collective-permute-start.21 = (bf16[1024,1536]{1,0:T(8,128)(2,1)S(1)}, bf16[1024,1536]{1,0:T(8,128)(2,1)}, u32[]{:S(2)}, u32[]{:S(2)}) collective-permute-start(bf16[1024,1536]{1,0:T(8,128)(2,1)S(1)} %join_rows.9.h2_ref.left0_ref), channel_id=1, source_target_pairs={{0,4},{4,0},{8,12},{12,8},{16,20},{20,16},{24,28},{28,24},{1,5},{5... | collective-permute-start | bytes 9437192 | tf_op jit(solution)/shard_map/ppermute | solution.py:29
  249.0 114.3 %reduce-scatter.6.cloned.1.call-start = ((), (), s32[]{:S(2)}) async-start(), calls=%async_computation.10 | async-start | bytes 3932160 | tf_op jit(solution)/shard_map/reduce_scatter | solution.py:863
  255.0 36.4 %collective-permute-start.25 = (bf16[256,1536]{1,0:T(8,128)(2,1)}, bf16[256,1536]{1,0:T(8,128)(2,1)S(1)}, u32[]{:S(2)}, u32[]{:S(2)}) collective-permute-start(bf16[256,1536]{1,0:T(8,128)(2,1)} %get-tuple-element.220), channel_id=1, source_target_pairs={{0,16},{4,20},{8,24},{12,28},{16,0},{20,4},{24,8},{28,12},{1,17},{... | collective-permute-start | bytes 2359304 | tf_op jit(solution)/shard_map/ppermute | solution.py:29
  255.6 36.7 %collective-permute-start.26 = (bf16[256,1536]{1,0:T(8,128)(2,1)}, bf16[256,1536]{1,0:T(8,128)(2,1)S(1)}, u32[]{:S(2)}, u32[]{:S(2)}) collective-permute-start(bf16[256,1536]{1,0:T(8,128)(2,1)} %get-tuple-element.221), channel_id=1, source_target_pairs={{0,24},{4,28},{8,16},{12,20},{16,8},{20,12},{24,0},{28,4},{1,25},{... | collective-permute-start | bytes 2359304 | tf_op jit(solution)/shard_map/ppermute | solution.py:29
  325.5 37.8 %collective-permute-start.30 = (bf16[768,1536]{1,0:T(8,128)(2,1)S(1)}, bf16[768,1536]{1,0:T(8,128)(2,1)}, u32[]{:S(2)}, u32[]{:S(2)}) collective-permute-start(bf16[768,1536]{1,0:T(8,128)(2,1)S(1)} %get-tuple-element.242), channel_id=1, source_target_pairs={{0,4},{4,0},{8,12},{12,8},{16,20},{20,16},{24,28},{28,24},{1,5},{5... | collective-permute-start | bytes 7077896 | tf_op jit(solution)/shard_map/ppermute | solution.py:29
  325.5 37.8 %collective-permute-start.27 = (bf16[256,1536]{1,0:T(8,128)(2,1)}, bf16[256,1536]{1,0:T(8,128)(2,1)}, u32[]{:S(2)}, u32[]{:S(2)}) collective-permute-start(bf16[256,1536]{1,0:T(8,128)(2,1)} %get-tuple-element.239), channel_id=1, source_target_pairs={{0,8},{4,12},{8,0},{12,4},{16,24},{20,28},{24,16},{28,20},{1,9},{5... | collective-permute-start | bytes 2359304 | tf_op jit(solution)/shard_map/ppermute | solution.py:29
  326.1 37.2 %collective-permute-start.28 = (bf16[256,1536]{1,0:T(8,128)(2,1)}, bf16[256,1536]{1,0:T(8,128)(2,1)}, u32[]{:S(2)}, u32[]{:S(2)}) collective-permute-start(bf16[256,1536]{1,0:T(8,128)(2,1)} %get-tuple-element.240), channel_id=1, source_target_pairs={{0,16},{4,20},{8,24},{12,28},{16,0},{20,4},{24,8},{28,12},{1,17},{... | collective-permute-start | bytes 2359304 | tf_op jit(solution)/shard_map/ppermute | solution.py:29
  326.7 36.6 %collective-permute-start.29 = (bf16[256,1536]{1,0:T(8,128)(2,1)}, bf16[256,1536]{1,0:T(8,128)(2,1)}, u32[]{:S(2)}, u32[]{:S(2)}) collective-permute-start(bf16[256,1536]{1,0:T(8,128)(2,1)} %get-tuple-element.241), channel_id=1, source_target_pairs={{0,24},{4,28},{8,16},{12,20},{16,8},{20,12},{24,0},{28,4},{1,25},{... | collective-permute-start | bytes 2359304 | tf_op jit(solution)/shard_map/ppermute | solution.py:29
  367.0 76.0 %reduce-scatter.8.cloned.1.call-start = ((), (), s32[]{:S(2)}) async-start(), calls=%async_computation.11 | async-start | bytes 3440640 | tf_op jit(solution)/shard_map/reduce_scatter | solution.py:863
  392.0 50.2 %collective-permute-start.34 = (bf16[256,1536]{1,0:T(8,128)(2,1)S(1)}, bf16[256,1536]{1,0:T(8,128)(2,1)S(1)}, u32[]{:S(2)}, u32[]{:S(2)}) collective-permute-start(bf16[256,1536]{1,0:T(8,128)(2,1)S(1)} %get-tuple-element.270), channel_id=1, source_target_pairs={{0,8},{4,12},{8,0},{12,4},{16,24},{20,28},{24,16},{28,20},{1,9},{5... | collective-permute-start | bytes 2359304 | tf_op jit(solution)/shard_map/ppermute | solution.py:29
  393.4 48.7 %collective-permute-start.35 = (bf16[256,1536]{1,0:T(8,128)(2,1)S(1)}, bf16[256,1536]{1,0:T(8,128)(2,1)}, u32[]{:S(2)}, u32[]{:S(2)}) collective-permute-start(bf16[256,1536]{1,0:T(8,128)(2,1)S(1)} %get-tuple-element.271), channel_id=1, source_target_pairs={{0,16},{4,20},{8,24},{12,28},{16,0},{20,4},{24,8},{28,12},{1,17},{... | collective-permute-start | bytes 2359304 | tf_op jit(solution)/shard_map/ppermute | solution.py:29
  394.1 48.9 %collective-permute-start.36 = (bf16[256,1536]{1,0:T(8,128)(2,1)S(1)}, bf16[256,1536]{1,0:T(8,128)(2,1)}, u32[]{:S(2)}, u32[]{:S(2)}) collective-permute-start(bf16[256,1536]{1,0:T(8,128)(2,1)S(1)} %get-tuple-element.272), channel_id=1, source_target_pairs={{0,24},{4,28},{8,16},{12,20},{16,8},{20,12},{24,0},{28,4},{1,25},{... | collective-permute-start | bytes 2359304 | tf_op jit(solution)/shard_map/ppermute | solution.py:29
  395.5 45.2 %collective-permute-start.37 = (bf16[192,1536]{1,0:T(8,128)(2,1)S(1)}, bf16[192,1536]{1,0:T(8,128)(2,1)S(1)}, u32[]{:S(2)}, u32[]{:S(2)}) collective-permute-start(bf16[192,1536]{1,0:T(8,128)(2,1)S(1)} %pad_maximum_fusion), channel_id=1, source_target_pairs={{0,8},{4,12},{8,0},{12,4},{16,24},{20,28},{24,16},{28,20},{1,9},{5... | collective-permute-start | bytes 1769480 | tf_op jit(solution)/shard_map/ppermute | solution.py:29
  396.9 45.2 %collective-permute-start.38 = (bf16[192,1536]{1,0:T(8,128)(2,1)S(1)}, bf16[192,1536]{1,0:T(8,128)(2,1)S(1)}, u32[]{:S(2)}, u32[]{:S(2)}) collective-permute-start(bf16[192,1536]{1,0:T(8,128)(2,1)S(1)} %pad_maximum_fusion.1), channel_id=1, source_target_pairs={{0,16},{4,20},{8,24},{12,28},{16,0},{20,4},{24,8},{28,12},{1,17},{... | collective-permute-start | bytes 1769480 | tf_op jit(solution)/shard_map/ppermute | solution.py:29
  (93 other events, 970.5 us)
Sparse Core Ops, SparseCore 0:
  33.5 59.4 all-gather.4
  95.1 88.1 all-gather.6
  249.2 35.3 reduce-scatter.3
  293.4 60.3 reduce-scatter.5
  385.8 54.3 reduce-scatter.7

commit v3 on v2

--- a/solution.py
+++ b/solution.py
@@ -42,10 +42,14 @@
     return [flip(own, d) for d in (2, 4, 6)]
 
 
-def both_cores(near, far_flipped):
-    rows = near.shape[0] // 4
-    sums = [near[i * rows : (i + 1) * rows].astype(F32) + far_flipped[i * rows : (i + 1) * rows].astype(F32) for i in range(4)]
+def both_cores(near, far):
+    sums = [x.astype(F32) + y.astype(F32) for x, y in zip(near, far)]
     return sums[0], [x.astype(BF16) for x in sums[1:]]
+
+
+def quarters(array):
+    rows = array.shape[0] // 4
+    return [array[i * rows : (i + 1) * rows] for i in range(4)]
 
 
 def send(blocks):
@@ -398,9 +402,12 @@
     return allowed, live, same_prev
 
 
-def front(lens_ref, proj, bias_ref, gains_ref, wide_ref, tails_ref, bucket):
+KEPT = ("qn", "kn", "rq", "rk", "ak", "av", "k", "v", "g")
+KEPT_LOW = ("qx", "kx", "vb")
+
+
+def front(proj, bias_ref, gains_ref, wide_ref, tails_ref, same_prev):
     rows = proj.shape[0]
-    allowed, live, same_prev = places_of(lens_ref, bucket, rows)
     q = proj[:, 0:BLOCK]
     k = proj[:, BLOCK : 2 * BLOCK]
     v = proj[:, 2 * BLOCK : 3 * BLOCK]
@@ -413,10 +420,8 @@
     same_head = wide_ref[0:BLOCK]
     ak = dot_split(sig, wide_ref[BLOCK : BLOCK + EXTRA], 2)
     av = dot_split(sig, wide_ref[BLOCK + EXTRA :], 2)
-    k_prev = pltpu.roll(k, 1, 0) * same_prev
-    v_prev = pltpu.roll(v, 1, 0) * same_prev
-    ks = ak * k_prev + (1.0 - ak) * k
-    vs = av * v_prev + (1.0 - av) * v
+    ks = ak * shifted(k, same_prev) + (1.0 - ak) * k
+    vs = av * shifted(v, same_prev) + (1.0 - av) * v
 
     def head_norm(u):
         factor = lax.rsqrt(dot_split(u * u, same_head, 2) * (1.0 / HEAD_DIM) + EPS)
@@ -438,21 +443,28 @@
     )
     qx = jnp.concatenate([qb, q_tail.astype(BF16)], axis=1)
     kx = jnp.concatenate([kb, k_tail.astype(BF16)], axis=1)
+    return dict(
+        qn=qn, kn=kn, rq=rq, rk=rk, ak=ak, av=av, k=k, v=v, g=jax.nn.sigmoid(og),
+        qx=qx, kx=kx, vb=vs.astype(BF16), vs=vs, sig=sig,
+    )
+
+
+def shifted(array, same_prev):
+    return pltpu.roll(array, 1, 0) * same_prev
+
+
+def head_masks(rows):
     span = iota((rows, SPAN), 1)
     masks = []
     for h in range(OWN):
         feature = (span >= h * HEAD_DIM) & (span < (h + 1) * HEAD_DIM)
         masks.append(feature | ((span >= BLOCK + 8 * h) & (span < BLOCK + 8 * (h + 1))))
-    return dict(
-        rows=rows, allowed=allowed, live=live, same_prev=same_prev, k=k, v=v, og=og, sig=sig, masks=masks,
-        same_head=same_head, ak=ak, av=av, k_prev=k_prev, v_prev=v_prev, qn=qn, rq=rq, kn=kn, rk=rk,
-        q_gain=q_gain, k_gain=k_gain, qx=qx, kx=kx, ks_low=kb, vs=vs,
-    )
-
-
-def scores_of(f, h):
-    qh = jnp.where(f["masks"][h], f["qx"], jnp.zeros_like(f["qx"]))
-    return jnp.where(f["allowed"], dot(f["kx"], qh, ((1,), (1,))), NEG), qh
+    return masks
+
+
+def scores_of(qx, kx, mask, allowed):
+    qh = jnp.where(mask, qx, jnp.zeros_like(qx))
+    return jnp.where(allowed, dot(kx, qh, ((1,), (1,))), NEG), qh
 
 
 def head_rows(h):
@@ -461,7 +473,7 @@
 
 def attn_fwd_kernel(
     lens_ref, spots_ref, near_ref, far_ref, w_ref, bias_ref, wide_ref, tails_ref,
-    h1_ref, proj_ref, mixed_ref, att_ref, lse_ref, gains_ref, heads_ref,
+    h1_ref, mixed_ref, att_ref, lse_ref, gains_ref, heads_ref, sig_ref, *kept_refs
 ):
     picks = (iota((8, EXTRA), 1) == GAIN_AT + iota((8, EXTRA), 0)) & (iota((8, EXTRA), 0) < 4)
     picks = picks.astype(BF16)
@@ -474,12 +486,16 @@
     tok = jnp.where(pl.program_id(0) < 4, near_ref[...], far_ref[...]).astype(F32)
     h1 = (normed(tok)[0] * gains[0:1]).astype(BF16)
     h1_ref[...] = h1
-    proj_ref[...] = dot(h1, w_ref[...])
-    f = front(lens_ref, proj_ref, bias_ref, heads_ref, wide_ref, tails_ref, pl.program_id(0))
+    rows = h1.shape[0]
+    allowed, live, same_prev = places_of(lens_ref, pl.program_id(0), rows)
+    f = front(dot(h1, w_ref[...]), bias_ref, heads_ref, wide_ref, tails_ref, same_prev)
+    sig_ref[...] = f["sig"]
+    for name, ref in zip(KEPT + KEPT_LOW, kept_refs):
+        ref[...] = f[name]
     vt = f["vs"].T.astype(BF16)
     att = []
-    for h in range(OWN):
-        s, _ = scores_of(f, h)
+    for h, mask in enumerate(head_masks(rows)):
+        s, _ = scores_of(f["qx"], f["kx"], mask, allowed)
         top = jnp.max(s, axis=0, keepdims=True)
         e = jnp.exp(s - top)
         total = jnp.sum(e, axis=0, keepdims=True)
@@ -488,21 +504,25 @@
         lse_ref[h : h + 1, :] = top + jnp.log(total)
     att = jnp.concatenate(att, axis=0).T
     att_ref[...] = att
-    mixed_ref[0] = fold(att * jax.nn.sigmoid(f["og"]) * f["live"]).astype(BF16)
+    mixed_ref[0] = fold(att * f["g"] * live).astype(BF16)
 
 
 def attn_bwd_kernel(
-    lens_ref, spots_ref, proj_ref, bias_ref, gains_ref, wide_ref, tails_ref, backs_ref, w_ref,
-    att_ref, lse_ref, dm_ref, dp_ref, sums_ref, near_ref, far_ref,
+    lens_ref, spots_ref, gains_ref, wide_ref, backs_ref, w_ref, att_ref, lse_ref, dm_ref, sig_ref, *refs
 ):
+    kept = KEPT + KEPT_LOW
+    f = {name: ref[...] for name, ref in zip(kept, refs)}
+    dp_ref, sums_ref, near_ref, far_ref = refs[len(kept) :]
     bucket = pl.program_id(0)
-    f = front(lens_ref, proj_ref, bias_ref, gains_ref, wide_ref, tails_ref, bucket)
-    rows, same_head = f["rows"], f["same_head"]
-    dm = unfold(dm_ref[0].astype(F32)) * f["live"]
-    g = jax.nn.sigmoid(f["og"])
+    rows = att_ref.shape[0]
+    allowed, live, same_prev = places_of(lens_ref, bucket, rows)
+    masks = head_masks(rows)
+    same_head = wide_ref[0:BLOCK]
+    q_gain, k_gain = gains_ref[0:1, 0:BLOCK], gains_ref[1:2, 0:BLOCK]
+    dm = unfold(dm_ref[0].astype(F32)) * live
+    g, vb = f["g"], f["vb"]
     dab = (dm * g).astype(BF16)
     dog = dm * att_ref[...] * g * (1.0 - g)
-    vb = f["vs"].astype(BF16)
     kt = f["kx"][:, :BLOCK].astype(F32).T.astype(BF16)
     zero = jnp.zeros((rows, BLOCK), BF16)
     dkx = jnp.zeros((rows, SPAN), F32)
@@ -510,9 +530,9 @@
     tail = jnp.zeros((TAIL, rows), F32)
     dqt = []
     for h in range(OWN):
-        s, qh = scores_of(f, h)
+        s, qh = scores_of(f["qx"], f["kx"], masks[h], allowed)
         p = jnp.exp(s - lse_ref[h : h + 1, :])
-        dab_h = jnp.where(f["masks"][h][:, :BLOCK], dab, zero)
+        dab_h = jnp.where(masks[h][:, :BLOCK], dab, zero)
         dvb = dvb + dot(p.astype(BF16), dab_h)
         dp = dot(vb, dab_h, ((1,), (1,)))
         ds = p * (dp - jnp.sum(p * dp, axis=0, keepdims=True))
@@ -528,20 +548,20 @@
     def back(n, r, e):
         return r * (e - n * (dot_split(e * n, same_head, 2) * (1.0 / HEAD_DIM)))
 
-    dq = back(f["qn"], f["rq"], dqb * f["q_gain"])
-    dks = back(f["kn"], f["rk"], dkb * f["k_gain"])
+    dq = back(f["qn"], f["rq"], dqb * q_gain)
+    dks = back(f["kn"], f["rk"], dkb * k_gain)
     last = iota((rows, 1), 0) == rows - 1
 
     def mix_back(grad, rate, cur, prev):
-        ahead = pltpu.roll(rate * grad * f["same_prev"], rows - 1, 0)
+        ahead = pltpu.roll(rate * grad * same_prev, rows - 1, 0)
         return (1.0 - rate) * grad + jnp.where(last, 0.0, ahead), grad * (prev - cur)
 
-    dk, dak = mix_back(dks, f["ak"], f["k"], f["k_prev"])
-    dv, dav = mix_back(dvb, f["av"], f["v"], f["v_prev"])
+    dk, dak = mix_back(dks, f["ak"], f["k"], shifted(f["k"], same_prev))
+    dv, dav = mix_back(dvb, f["av"], f["v"], shifted(f["v"], same_prev))
 
     onward = (iota((rows, rows), 1) >= iota((rows, rows), 0)).astype(BF16)
     keep = sum(dot(onward, term) for term in split(dqx[:, BLOCK:] - dkx[:, BLOCK:], TERMS))
-    sig = f["sig"]
+    sig = sig_ref[...]
     drate = (
         dot_split(dak, backs_ref[0:BLOCK], 2)
         + dot_split(dav, backs_ref[BLOCK : 2 * BLOCK], 2)
@@ -581,6 +601,10 @@
 
 def spot_spec(rows):
     return pl.BlockSpec((1, rows * 3 // 2, EXTRA), lambda i, lens, spots: (spots[i], 0, 0))
+
+
+def kept_specs(rows):
+    return [rows_spec(rows, BLOCK) for _ in KEPT] + [rows_spec(rows, c) for c in (SPAN, SPAN, BLOCK)]
 
 
 def attn_fwd(lens, spots, near, far, w, bias, wide, tails):
@@ -603,23 +627,26 @@
             ],
             out_specs=[
                 rows_spec(rows, width),
-                rows_spec(rows, WIDE),
                 spot_spec(rows),
                 rows_spec(rows, BLOCK),
                 rows_spec(8, rows),
                 whole_spec((8, width)),
                 whole_spec((8, 2 * EXTRA)),
-            ],
+                rows_spec(rows, EXTRA),
+            ]
+            + kept_specs(rows),
         ),
         out_shape=[
             shape((total, width), BF16),
-            shape((total, WIDE), F32),
             shape((buckets, rows * 3 // 2, EXTRA), BF16),
             shape((total, BLOCK), F32),
             shape((8 * buckets, rows), F32),
             shape((8, width), F32),
             shape((8, 2 * EXTRA), F32),
-        ],
+            shape((total, EXTRA), F32),
+        ]
+        + [shape((total, BLOCK), F32) for _ in KEPT]
+        + [shape((total, c), BF16) for c in (SPAN, SPAN, BLOCK)],
         **settings(20, 60),
         name="attn_fwd",
     )(lens, spots, near, far, w, bias, wide, tails)
@@ -633,9 +660,9 @@
     return pl.BlockSpec((rows, width), lambda i, lens, spots: (jnp.maximum(i - 4, 0), 0))
 
 
-def attn_bwd(lens, spots, proj, bias, gains, wide, tails, backs, w, att, lse, dm):
+def attn_bwd(lens, spots, gains, wide, backs, w, att, lse, dm, sig, *kept):
     buckets = lens.shape[0]
-    total = proj.shape[0]
+    total = att.shape[0]
     width = w.shape[0]
     rows = total // buckets
     return pl.pallas_call(
@@ -643,9 +670,9 @@
         grid_spec=pltpu.PrefetchScalarGridSpec(
             num_scalar_prefetch=2,
             grid=(buckets,),
-            in_specs=[rows_spec(rows, WIDE)]
-            + [whole_spec(x.shape) for x in (bias, gains, wide, tails, backs, w)]
-            + [rows_spec(rows, BLOCK), rows_spec(8, rows), spot_spec(rows)],
+            in_specs=[whole_spec(x.shape) for x in (gains, wide, backs, w)]
+            + [rows_spec(rows, BLOCK), rows_spec(8, rows), spot_spec(rows), rows_spec(rows, EXTRA)]
+            + kept_specs(rows),
             out_specs=[
                 rows_spec(rows, WIDE),
                 whole_spec((8, 2 * EXTRA)),
@@ -657,76 +684,75 @@
         + [shape((total // 2, width), BF16)] * 2,
         **settings(24, 60),
         name="attn_bwd",
-    )(lens, spots, proj, bias, gains, wide, tails, backs, w, att, lse, dm)
+    )(lens, spots, gains, wide, backs, w, att, lse, dm, sig, *kept)
 
 
 def mid_fwd_kernel(spots_ref, got_ref, tok_ref, gain_ref, *refs):
     x2_ref, h2_ref = refs[TP:]
     acc = tok_ref[...].astype(F32)
     for i in range(TP):
-        acc = acc + dot(unfold(got_ref[spots_ref[i]]), refs[i][0:BLOCK, :])
+        acc = acc + dot(unfold(got_ref[spots_ref[i]]), refs[i][...])
     x2_ref[...] = acc
     h2_ref[...] = (normed(acc)[0] * gain_ref[...]).astype(BF16)
 
 
+def once(dims):
+    return pl.BlockSpec(dims, lambda i: (0,) * len(dims))
+
+
+def mix_specs(w):
+    return [once((BLOCK, x.shape[1])) for x in w]
+
+
 def mid_fwd(spots, got, w, tok, gain):
+    rows, width = tok.shape
     return pl.pallas_call(
         mid_fwd_kernel,
-        in_specs=[SMEM] + [VMEM] * (3 + TP),
-        out_specs=[VMEM, VMEM],
+        grid=(1,),
+        in_specs=[SMEM, once(got.shape), once(tok.shape), once(gain.shape)] + mix_specs(w),
+        out_specs=[once(tok.shape)] * 2,
         out_shape=[shape(tok.shape, F32), shape(tok.shape, BF16)],
-        **settings(6, 40),
+        **settings(5, 40),
         name="mid_fwd",
     )(spots, got, tok, gain, *w)
 
 
-def mid_bwd_kernel(
-    spots_ref, a_ref, b_ref, c_ref, d_ref, x2_ref, cot_ref, gain_ref, *refs
-):
-    dx2_ref, dxb_ref, dm_ref = refs[TP:]
+def mid_bwd_kernel(spots_ref, a_ref, b_ref, c_ref, d_ref, x2_ref, cot_ref, gain_ref, got_ref, *refs):
+    dx2_ref, dm_ref, near_ref, far_ref = refs[TP:]
     dh2 = a_ref[...] + b_ref[...].astype(F32) + c_ref[...].astype(F32) + d_ref[...].astype(F32)
     n2, r2 = normed(x2_ref[...])
     dx2 = cot_ref[...].astype(F32) + norm_back(n2, r2, dh2 * gain_ref[...])
     dx2_ref[...] = dx2
     dxb = dx2.astype(BF16)
-    dxb_ref[...] = dxb
     for i in range(TP):
-        dm = dot(dxb, refs[i][0:BLOCK, :], ((1,), (1,)))
+        dm = dot(dxb, refs[i][...], ((1,), (1,)))
         dm_ref[spots_ref[i]] = fold(dm).astype(BF16)
-
-
-def mid_bwd(spots, parts, x2, cot, gain, w):
+        out_ref = near_ref if i < 4 else far_ref
+        piece = dot(unfold(got_ref[spots_ref[i]]), dxb, ((0,), (0,)))
+        out_ref[(i % 4) * BLOCK : (i % 4 + 1) * BLOCK, :] = piece.astype(BF16)
+
+
+def mid_bwd(spots, parts, x2, cot, gain, got, w):
     rows, width = x2.shape
+    arrays = (*parts, x2, cot, gain, got)
+    outs = [
+        shape((rows, width), F32),
+        shape((TP, rows * 3 // 2, EXTRA), BF16),
+        shape((4 * BLOCK, width), BF16),
+        shape((4 * BLOCK, width), BF16),
+    ]
     return pl.pallas_call(
         mid_bwd_kernel,
-        in_specs=[SMEM] + [VMEM] * (7 + TP),
-        out_specs=[VMEM] * 3,
-        out_shape=[shape((rows, width), F32), shape((rows, width), BF16), shape((TP, rows * 3 // 2, EXTRA), BF16)],
-        **settings(8, 40),
+        grid=(1,),
+        in_specs=[SMEM] + [once(x.shape) for x in arrays] + mix_specs(w),
+        out_specs=[once(x.shape) for x in outs],
+        out_shape=outs,
+        **settings(9, 48),
         name="mid_bwd",
-    )(spots, *parts, x2, cot, gain, *w)
-
-
-def grad_mix_kernel(spots_ref, got_ref, dxb_ref, near_ref, far_ref):
-    for i in range(TP):
-        out_ref = near_ref if i < 4 else far_ref
-        piece = dot(unfold(got_ref[spots_ref[i]]), dxb_ref[...], ((0,), (0,)))
-        out_ref[(i % 4) * BLOCK : (i % 4 + 1) * BLOCK, :] = piece.astype(BF16)
-
-
-def grad_mix(spots, got, dxb):
-    width = dxb.shape[1]
-    return pl.pallas_call(
-        grad_mix_kernel,
-        in_specs=[SMEM, VMEM, VMEM],
-        out_specs=[VMEM, VMEM],
-        out_shape=[shape((4 * BLOCK, width), BF16)] * 2,
-        **settings(4, 40),
-        name="grad_mix",
-    )(spots, got, dxb)
-
-
-def ffn_kernel(lens_ref, h2_ref, cot_ref, gu_ref, dn_ref, ab_ref, dgu_ref, out_ref, dh2_ref):
+    )(spots, *arrays, *w)
+
+
+def ffn_kernel(lens_ref, h2_ref, cot_ref, gu_ref, dn_ref, ab_ref, dgu_ref, *out_refs):
     rows, ff = h2_ref.shape[0], dn_ref.shape[0]
     total = jnp.int32(0)
     for j in range(lens_ref.shape[1]):
@@ -744,8 +770,19 @@
     dgu_ref[:, :ff] = dgate
     dgu_ref[:, ff:] = dup
     dh2 = dot(dgate, gu_ref[:, :ff], ((1,), (1,))) + dot(dup, gu_ref[:, ff:], ((1,), (1,)))
-    dh2_ref[...] = dh2.astype(BF16)
-    out_ref[...] = dot(ab, dn_ref[...]).astype(BF16)
+    dh2 = dh2.astype(BF16)
+    out = dot(ab, dn_ref[...]).astype(BF16)
+    last = pl.program_id(0) == pl.num_programs(0) - 1
+
+    @pl.when(jnp.logical_not(last))
+    def _():
+        out_refs[0][...] = out
+        out_refs[1][...] = dh2
+
+    @pl.when(last)
+    def _():
+        out_refs[2][...] = out
+        out_refs[3][...] = dh2
 
 
 def ffn(lens, h2, cot, gu, dn):
@@ -760,13 +797,15 @@
     def whole(dims):
         return pl.BlockSpec(dims, lambda i: (0, 0))
 
-    outs = (ff, 2 * ff, width, width)
+    most = pl.BlockSpec((rows, width), lambda i: (jnp.minimum(i, buckets - 2), 0))
     return pl.pallas_call(
         ffn_kernel,
         grid=(buckets,),
         in_specs=[SMEM, block(width), block(width), whole(gu.shape), whole(dn.shape)],
-        out_specs=[block(c) for c in outs],
-        out_shape=[shape((total, c), BF16) for c in outs],
+        out_specs=[block(ff), block(2 * ff), most, most, whole((rows, width)), whole((rows, width))],
+        out_shape=[shape((total, ff), BF16), shape((total, 2 * ff), BF16)]
+        + [shape((total - rows, width), BF16)] * 2
+        + [shape((rows, width), BF16)] * 2,
         **settings(4 * buckets, 40),
         name="ffn",
     )(lens, h2, cot, gu, dn)
@@ -891,15 +930,15 @@
 
     gains = jnp.stack([norm_gain, q_gain, k_gain, ffn_gain])
     packed, w_mix = phase(pack_in(doc_lengths, w_attn_in, w_rates, gains), w_out)
-    got_in, w_mix = phase(swap(packed), gather_shares(w_mix))
+    got_in = swap(packed)
     w_in = lax.all_gather(got_in, "sh", axis=1).reshape(width, WIDE)
     lens_all = got_in[:, 0, CORE + LENS_AT : CORE + LENS_AT + doc_lengths.shape[0]].astype(jnp.int32)
     lens = lens_all[spots]
     bias = lax.dynamic_index_in_dim(rate_bias.reshape(3, TP, OWN), place, 1, False).reshape(1, RATES)
     bias = jnp.pad(bias, ((0, 7), (0, EXTRA - RATES)))
 
-    tok, w_gu, _ = phase(tokens, w_gate_up, got_in)
-    two_four = sides(tok)
+    tok, w_gu, w_mix, _ = phase(tokens, w_gate_up, w_mix, got_in)
+    two_four, w_mix = phase(sides(tok), gather_shares(w_mix))
     tok = join_rows(tok, *two_four, *diagonal(*two_four))
     tok, packed = phase(tok, pack_gu(w_gu))
     joined = join_ffn(swap(packed), w_down)
@@ -909,7 +948,7 @@
     wide, tails, backs = constants()
     beside = phase(join_rows(in_order(w_mix), cotangent), joined)[0]
     two_four = sides(beside)
-    h1, proj, mixed, att, lse, gains, gain_heads = attn_fwd(lens, spots, tok, far, w_in, bias, wide, tails)
+    h1, mixed, att, lse, gains, gain_heads, *kept = attn_fwd(lens, spots, tok, far, w_in, bias, wide, tails)
     gain_one, gain_two = gains[0:1], gains[3:4]
     mixed, two_four = phase(mixed, two_four)
     near = [beside, *two_four]
@@ -919,52 +958,73 @@
     near = [*near, *six]
     x2, h2 = mid_fwd(spots, got_mixed, near[:4] + far[:4], tokens, gain_two)
 
+    first, second = (0, 2, 4, 1), (3, 5, 7, 6)
+    lens_of = [jnp.stack([lens[OFFSETS.index(d)] for d in order]) for order in (first, second)]
     h2, near, far = phase(h2, near, far)
     w_mix = near[:4] + far[:4]
-    two_four = sides(h2)
-    cot = [join_rows(*[(x, BLOCK) for x in half[:4]], half[4]) for half in (near, far)]
-    two_four, cot = phase(two_four, cot)
-    h2 = join_rows(h2, *two_four, *diagonal(*two_four))
-    h2_far, found_near = phase(flip(h2, 1), ffn(lens[:4], h2, cot[0], w_gu, w_dn))
-    h2 = h2, h2_far
-    found_far = ffn(lens[4:], h2_far, cot[1], w_gu, w_dn)
-    ab, dgu, out, dh2 = phase(*zip(found_near, found_far))
+    two, four = sides(h2)
+    one = flip(h2, 1)
+    cot = [
+        join_rows((near[0], BLOCK), (near[1], BLOCK), (near[2], BLOCK), (far[0], BLOCK)),
+        join_rows((far[1], BLOCK), (far[2], BLOCK), (far[3], BLOCK), far[4], (near[3], BLOCK), near[4]),
+    ]
+    one, two, four, cot = phase(one, two, four, cot)
+    six = diagonal(two, four)
+    three, five = flip(two, 1), flip(four, 1)
+    h2 = join_rows(h2, two, four, one)
+    found = ffn(lens_of[0], h2, cot[0], w_gu, w_dn)
+    found, six, three, five = phase(found, six, three, five)
+    out_one, dh2_one = flip(found[4], 1), flip(found[5], 1)
+    six = jnp.concatenate(six, axis=0)
+    six, seven = phase(six, flip(six, 1))
+    h2 = h2, join_rows(three, five, seven, six)
+    found = [found, ffn(lens_of[1], h2[1], cot[1], w_gu, w_dn)]
+    found, dh2_one, out_one = phase(found, dh2_one, out_one)
+    ab, dgu, out, dh2, out_last, dh2_last = zip(*found)
     dh2_far, dw_dn, out_far = phase(flip(dh2[1], 1), grad_down(ab, cot), flip(out[1], 1))
-    own, low = both_cores(dh2[0], dh2_far)
+
+    def folded(near, six, one, far):
+        rows = six.shape[0]
+        parts = [[x[i * rows : (i + 1) * rows] for i in range(3)] for x in (near, far)]
+        return both_cores([*parts[0], six], [one, *parts[1]])
+
+    own, low = folded(dh2[0], dh2_last[1], dh2_one, dh2_far)
     dw_dn = lax.psum_scatter(dw_dn, "sh", scatter_dimension=0, tiled=True)
     own, low, dgu, out_far = phase(own, low, dgu, out_far)
-    layer_own, layer_low = both_cores(out[0], out_far)
+    layer_own, layer_low = folded(out[0], out_last[1], out_one, out_far)
     dh2, dw_gu, dw_dn, own, layer_low = phase(send(low), grad_gu(h2, dgu, share), dw_dn, own, layer_low)
     dw_gu = own_share(dw_gu)
 
-    dx2, dxb, dm = mid_bwd(spots, [own] + dh2, x2, cotangent, gain_two, w_mix)
-    dxb, dm = phase(dxb, dm)
-    got_dm, mix, layer_low = phase(swap(dm), grad_mix(spots, got_mixed, dxb), layer_low)
-    layer, mix_far, found, dw_gu = phase(
-        send(layer_low),
-        flip(mix[1], 1),
-        attn_bwd(lens, spots, proj, bias, gain_heads, wide, tails, backs, w_in, att, lse, got_dm),
-        dw_gu,
+    found, layer_low = phase(
+        mid_bwd(spots, [own] + dh2, x2, cotangent, gain_two, got_mixed, w_mix), relay_six(layer_low)
+    )
+    dx2, dm, mix_near, mix_far = found
+    mix_own, mix_low = both_cores(quarters(mix_near), quarters(flip(mix_far, 1)))
+    got_dm, mix_own, mix_low, layer_low = phase(swap(dm), mix_own, mix_low, add_six(layer_low))
+    layer, mix_low, found = phase(
+        (flip(layer_low[0], 2), flip(layer_low[1], 4)),
+        relay_six(mix_low),
+        attn_bwd(lens, spots, gain_heads, wide, backs, w_in, att, lse, got_dm, *kept),
     )
     dp, sums, dh1_near, dh1_far = found
-    layer_out = (x2 + total_of([layer_own] + layer)).astype(BF16)
-
-    mix_own, low = both_cores(mix[0], mix_far)
-    dh1_far, low, dw_in, got_gu = phase(
-        flip(dh1_far, 1), relay_six(low), grad_in(place.reshape(1), sums, h1, dp, share), swap(dw_gu)
+    layer_out = (x2 + total_of((layer_own, *layer))).astype(BF16)
+
+    mix_low = add_six(mix_low)
+    mix = flip(mix_low[0], 2), flip(mix_low[1], 4)
+    dh1_far, dw_in, got_gu = phase(
+        flip(dh1_far, 1), grad_in(place.reshape(1), sums, h1, dp, share), swap(dw_gu)
     )
     dw_in = own_share(dw_in)
-    low = add_six(low)
-    dh1_own, dh1_low = both_cores(dh1_near, dh1_far)
-    low, dh1_low = phase(low, dh1_low)
-    dh1, mix, dw_in = phase(send(dh1_low), (flip(low[0], 2), flip(low[1], 4)), dw_in)
-    got_in_grad, mix = phase(swap(dw_in), to_shares(total_of((mix_own, *mix)).astype(BF16)))
+    dh1_own, dh1_low = both_cores(quarters(dh1_near), quarters(dh1_far))
+    dh1, dw_in, mix = phase(send(dh1_low), dw_in, mix)
+    mix = to_shares(total_of((mix_own, *mix)).astype(BF16))
     n1, r1 = normed(tokens.astype(F32))
     d_tokens = dx2 + norm_back(n1, r1, total_of([dh1_own] + dh1) * gain_one)
 
-    d_w_attn_in, d_w_rates, small = unpack_in(got_in_grad, w_attn_in, w_rates, norm_gain)
+    d_w_attn_in, d_w_rates, small = unpack_in(swap(dw_in), w_attn_in, w_rates, norm_gain)
     d_w_gate_up, small_gu = unpack_gu(got_gu, w_gate_up, ffn_gain)
     d_ffn_gain = small_gu[0, :own_rows]
+    small, mix = phase(small, mix)
     d_w_out = total_of(mix)
     return (
         layer_out,

time: 480 us -> 470 us (0.979)
  blocking collectives: 0 us -> 31.8 us
  waiting for transfers between devices: 160 us -> 133 us
  starting transfers between devices: 70.4 us -> 59.2 us
  local copies, waits for them, and re-layouts: 49.8 us -> 41.4 us
  Pallas kernels: 153 us -> 148 us
    all_to_all x0 -> x2, blocking collectives: none -> 31.8 us  [swap(): return lax.all_to_all(blocks, 'tp', 0, 0, tiled=True)]
    ppermute x36 -> x42, waiting for transfers between devices: 117 us -> 91.5 us  [flip(): return lax.ppermute(array, 'tp', [(i, i ^ offset) for i in range(TP)])]
    unnamed x128 -> x117, local copies, waits for them, and re-layouts: 38.4 us -> 24.9 us
    all_to_all x6 -> x4, waiting for transfers between devices: 29.8 us -> 16.8 us  [swap(): return lax.all_to_all(blocks, 'tp', 0, 0, tiled=True)]
    all_to_all x6 -> x4, starting transfers between devices: 25.3 us -> 15.8 us  [swap(): return lax.all_to_all(blocks, 'tp', 0, 0, tiled=True)]
    pallas_call x1, Pallas kernels: 34.3 us -> 28.7 us  [attn_bwd(): pl.pallas_call(attn_bwd_kernel, grid_spec=pltpu.PrefetchScalarGridSpec(nu...]
    all_gather x1, waiting for transfers between devices: 0.01 us -> 5.26 us  [body(): w_in = lax.all_gather(got_in, 'sh', axis=1).reshape(width, WIDE)]
    pallas_call x3 -> x2, Pallas kernels: 15 us -> 13.7 us  [the longest x1 9.44 us: mid_bwd(): pl.pallas_call(mid_bwd_kernel, grid=(1,), in_specs=[SMEM] + [once(x.shape...]
  transfers between devices with their start and end apart: 53 -> 57, of which waited for: 22 -> 24; matrix products, arithmetic and copies ran while one was open for 8% -> 9% of each run, Pallas kernels for 28% -> 32%
where the time goes in v3:
time: 470 us; the launch traced here: 463 us
  Pallas kernels  148 us (31%)
  waiting for transfers between devices  133 us (28%)
  starting transfers between devices  59.2 us (13%)
  local copies, waits for them, and re-layouts  41.4 us (9%)
  other arithmetic  34.5 us (7%)
  blocking collectives  31.8 us (7%)
  between operations  15.1 us (3%)
    ppermute x42, waiting for transfers between devices, flip(): return lax.ppermute(array, 'tp', [(i, i ^ offset) for i in range(TP)])  91.5 us
    all_to_all x2, blocking collectives, swap(): return lax.all_to_all(blocks, 'tp', 0, 0, tiled=True)  31.8 us
    ppermute x42, starting transfers between devices, flip(): return lax.ppermute(array, 'tp', [(i, i ^ offset) for i in range(TP)])  31.4 us
    pallas_call x2, Pallas kernels, ffn(): pl.pallas_call(ffn_kernel, grid=(buckets,), in_specs=[SMEM, block(width),...  30.9 us
    pallas_call x1, Pallas kernels, attn_fwd(): pl.pallas_call(attn_fwd_kernel, grid_spec=pltpu.PrefetchScalarGridSpec(nu...  29.6 us
    pallas_call x1, Pallas kernels, attn_bwd(): pl.pallas_call(attn_bwd_kernel, grid_spec=pltpu.PrefetchScalarGridSpec(nu...  28.7 us
    unnamed x117, local copies, waits for them, and re-layouts  24.9 us
    all_to_all x4, waiting for transfers between devices, swap(): return lax.all_to_all(blocks, 'tp', 0, 0, tiled=True)  16.8 us
  transfers between devices with their start and end apart: 57, of which 24 were waited for; matrix products, arithmetic and copies ran while one was open for 9% of the time, Pallas kernels for 32%

profile of v3, /device:TPU:0, one launch (start us, length us, event | category | flops | bytes accessed | tf_op | source)
XLA Modules:
  0.0 463.3 jit_solution(7779246149957073735)
XLA Ops:
  11.2 16.7 %all_to_all.30 = bf16[8,48,896]{2,1,0:T(8,128)(2,1)} all-to-all(bf16[8,48,896]{2,1,0:T(8,128)(2,1)S(1)} %pack_in.1), channel_id=1, replica_groups=mesh['dp'=8,'fsdp'=4] {'dp'}, dimensions={0} | all-to-all | bytes 1376256 | tf_op jit(solution)/shard_map/all_to_all | solution.py:907
  37.9 10.4 %collective-permute-done.3 = bf16[48,1536]{1,0:T(8,128)(2,1)S(1)} collective-permute-done((bf16[48,1536]{1,0:T(8,128)(2,1)S(1)}, bf16[48,1536]{1,0:T(8,128)(2,1)S(1)}, u32[]{:S(2)}, u32[]{:S(2)}) %collective-permute-start.3) | collective-permute-done | bytes 147488 | tf_op jit(solution)/shard_map/ppermute | solution.py:75
  51.2 8.0 %collective-permute-done.5.refs_3_ = bf16[128,1536]{1,0:T(8,128)(2,1)S(1)} collective-permute-done((bf16[128,1536]{1,0:T(8,128)(2,1)S(1)}, bf16[128,1536]{1,0:T(8,128)(2,1)S(1)}, u32[]{:S(2)}, u32[]{:S(2)}) %collective-permute-start.5) | collective-permute-done | bytes 393248 | tf_op jit(solution)/shard_map/ppermute | solution.py:29
  62.6 15.1 %all_to_all.31.got_ref = bf16[8,48,1024]{2,1,0:T(8,128)(2,1)S(1)} all-to-all(bf16[8,48,1024]{2,1,0:T(8,128)(2,1)S(1)} %pack_gu.1), channel_id=1, replica_groups=mesh['dp'=8,'fsdp'=4] {'dp'}, dimensions={0} | all-to-all | bytes 1572864 | tf_op jit(solution)/shard_map/all_to_all | solution.py:907
  85.1 5.3 %all-gather.5.cloned.1.call-done = bf16[8,192,896]{2,1,0:T(8,128)(2,1)} async-done(((bf16[8,48,896]{2,1,0:T(8,128)(2,1)}), bf16[8,192,896]{2,1,0:T(8,128)(2,1)}) %all-gather.5.cloned.1.call-update) | async-done | bytes 2752528 | tf_op jit(solution)/shard_map/all_gather | solution.py:934
  90.4 29.6 %attn_fwd.1 = (bf16[2048,1536]{1,0:T(8,128)(2,1)}, bf16[8,384,128]{2,1,0:T(8,128)(2,1)}, f32[2048,192]{1,0:T(8,128)}, f32[64,256]{1,0:T(8,128)}, f32[8,1536]{1,0...) custom-call(s32[8,4]{1,0:T(8,128)} %gather_fusion, ...), custom_call_target="tpu_custom_call" | custom-call | flops 200000000 | bytes 200000 | tf_op jit(solution)/shard_map/attn_fwd/pallas_call | solution.py:615
  123.5 4.2 all-to-all-start.2
  131.3 9.5 %all-to-all-done.2.got_ref = bf16[8,384,128]{2,1,0:T(8,128)(2,1)} async-done(((bf16[8,384,128]{2,1,0:T(8,128)(2,1)}), bf16[8,384,128]{2,1,0:T(8,128)(2,1)}, u32[]{:S(2)}, u32[]{:S(2)}) %all-to-all-start.2) | async-done | bytes 786464 | tf_op jit(solution)/shard_map/all_to_all | solution.py:907
  140.8 13.3 %collective-permute-done.10.refs_3_.refs_4_ = bf16[224,1536]{1,0:T(8,128)(2,1)} collective-permute-done((bf16[224,1536]{1,0:T(8,128)(2,1)}, bf16[224,1536]{1,0:T(8,128)(2,1)}, u32[]{:S(2)}, u32[]{:S(2)}) %collective-permute-start.10) | collective-permute-done | bytes 688160 | tf_op jit(solution)/shard_map/ppermute | solution.py:29
  156.6 4.3 mid_fwd.1
  170.8 10.2 %collective-permute-done.18.refs_1_ = bf16[256,1536]{1,0:T(8,128)(2,1)} collective-permute-done((bf16[256,1536]{1,0:T(8,128)(2,1)S(1)}, bf16[256,1536]{1,0:T(8,128)(2,1)}, u32[]{:S(2)}, u32[]{:S(2)}) %collective-permute-start.18) | collective-permute-done | bytes 786464 | tf_op jit(solution)/shard_map/ppermute | solution.py:29
  195.3 14.3 %ffn.2 = (bf16[1024,512]{1,0:T(8,128)(2,1)S(1)}, bf16[1024,1024]{1,0:T(8,128)(2,1)S(1)}, bf16[768,1536]{1,0:T(8,128)(2,1)S(1)}, bf16[768,1536]{1,0:T(8,128)(2,1)...) custom-call(s32[4,4]{1,0:T(4,128)S(1)} %get-tuple-element.383.lens_ref, ...), custom_call_target="tpu_custom_call" | custom-call | flops 160000000 | bytes 160000 | tf_op jit(solution)/shard_map/ffn/pallas_call | solution.py:801
  219.7 16.7 %ffn.3 = (bf16[1024,512]{1,0:T(8,128)(2,1)S(1)}, bf16[1024,1024]{1,0:T(8,128)(2,1)S(1)}, bf16[768,1536]{1,0:T(8,128)(2,1)}, bf16[768,1536]{1,0:T(8,128)(2,1)}, b...) custom-call(s32[4,4]{1,0:T(4,128)S(1)} %get-tuple-element.384.lens_ref, ...), custom_call_target="tpu_custom_call" | custom-call | flops 160000000 | bytes 160000 | tf_op jit(solution)/shard_map/ffn/pallas_call | solution.py:801
  240.3 8.4 %grad_down.1 = bf16[512,1536]{1,0:T(8,128)(2,1)} custom-call(bf16[1024,512]{1,0:T(8,128)(2,1)} %copy-done.27, bf16[1024,512]{1,0:T(8,128)(2,1)} %copy-done.28, bf16[1024,1536]{1,0:T(8,128)(2,1)} %copy-done, bf16[1024,1536]{1,0:T(8,128)(2,1)} %copy-done.1), custom_call_target="tpu_custom_call" | custom-call | flops 60000000 | bytes 60000 | tf_op jit(solution)/shard_map/grad_down/pallas_call | solution.py:823
  249.1 4.3 add_convert_fusion.8
  256.9 11.2 %grad_gu.1 = bf16[4,8,48,1024]{3,2,1,0:T(8,128)(2,1)} custom-call(bf16[1024,1536]{1,0:T(8,128)(2,1)} %copy-done.2, bf16[1024,1536]{1,0:T(8,128)(2,1)} %copy-done.3, bf16[1024,1024]{1,0:T(8,128)(2,1)} %copy-done.25, bf16[1024,1024]{1,0:T(8,128)(2,1)} %copy-done.26), custom_call_target="tpu_custom_call" | custom-call | flops 110000000 | bytes 110000 | tf_op jit(solution)/shard_map/grad_gu/pallas_call | solution.py:849
  273.9 16.6 %collective-permute-done.30.c_ref = bf16[256,1536]{1,0:T(8,128)(2,1)S(1)} collective-permute-done((bf16[256,1536]{1,0:T(8,128)(2,1)}, bf16[256,1536]{1,0:T(8,128)(2,1)S(1)}, u32[]{:S(2)}, u32[]{:S(2)}) %collective-permute-start.30) | collective-permute-done | bytes 786464 | tf_op jit(solution)/shard_map/ppermute | solution.py:29
  295.9 9.4 %mid_bwd.1 = (f32[256,1536]{1,0:T(8,128)}, bf16[8,384,128]{2,1,0:T(8,128)(2,1)S(1)}, bf16[768,1536]{1,0:T(8,128)(2,1)}, bf16[768,1536]{1,0:T(8,128)(2,1)}) custom-call(s32[8]{0:T(128)S(1)} %copy-done.34, f32[256,1536]{1,0:T(8,128)} %get-tuple-element.272.a_ref, bf16[256,1536]{1,0:T(8,128)(2,1)S(1)} %collective-permute-done.29.b_ref, ...), custom_call_target="tpu_custom_call" | custom-call | flops 90000000 | bytes 90000 | tf_op jit(solution)/shard_map/mid_bwd/pallas_call | solution.py:744
  306.3 4.2 all-to-all-start.3
  317.1 5.9 %all-to-all-done.3.dm_ref = bf16[8,384,128]{2,1,0:T(8,128)(2,1)} async-done(((bf16[8,384,128]{2,1,0:T(8,128)(2,1)}), bf16[8,384,128]{2,1,0:T(8,128)(2,1)}, u32[]{:S(2)}, u32[]{:S(2)}) %all-to-all-start.3) | async-done | bytes 786464 | tf_op jit(solution)/shard_map/all_to_all | solution.py:907
  327.9 28.7 %attn_bwd.1 = (bf16[2048,896]{1,0:T(8,128)(2,1)}, f32[8,256]{1,0:T(8,128)}, bf16[1024,1536]{1,0:T(8,128)(2,1)}, bf16[1024,1536]{1,0:T(8,128)(2,1)}) custom-call(s32[8,4]{1,0:T(8,128)} %gather_fusion, s32[8]{0:T(128)} %get-tuple-element.382.spots_ref, f32[8,256]{1,0:T(8,128)} %get-tuple-element.295.gains_ref, bf16[448,192]{1,0:T(8,128)(2,1)} %constant.110.clone.wide_ref, ...), custom_call_target="tpu_custom_call" | custom-call | flops 240000000 | bytes 240000 | tf_op jit(solution)/shard_map/attn_bwd/pallas_call | solution.py:668
  363.3 11.0 %grad_in.1 = bf16[4,8,48,896]{3,2,1,0:T(8,128)(2,1)} custom-call(s32[1]{0:T(128)} %bitcast.12.place_ref, f32[8,256]{1,0:T(8,128)} %get-tuple-element.321.sums_ref, bf16[2048,1536]{1,0:T(8,128)(2,1)} %get-tuple-element.322.left_ref, bf16[2048,896]{1,0:T(8,128)(2,1)} %get-tuple-element.323.right_ref), custom_call_target="tpu_custom_call" | custom-call | flops 110000000 | bytes 110000 | tf_op jit(solution)/shard_map/grad_in/pallas_call | solution.py:884
  397.3 15.7 %collective-permute-done.40 = bf16[256,1536]{1,0:T(8,128)(2,1)} collective-permute-done((bf16[256,1536]{1,0:T(8,128)(2,1)S(1)}, bf16[256,1536]{1,0:T(8,128)(2,1)}, u32[]{:S(2)}, u32[]{:S(2)}) %collective-permute-start.40) | collective-permute-done | bytes 786464 | tf_op jit(solution)/shard_map/ppermute | solution.py:29
  413.0 17.0 %collective-permute-done.41 = bf16[256,1536]{1,0:T(8,128)(2,1)} collective-permute-done((bf16[256,1536]{1,0:T(8,128)(2,1)S(1)}, bf16[256,1536]{1,0:T(8,128)(2,1)}, u32[]{:S(2)}, u32[]{:S(2)}) %collective-permute-start.41) | collective-permute-done | bytes 786464 | tf_op jit(solution)/shard_map/ppermute | solution.py:29
  (293 shorter events, 158.1 us)
Async XLA Ops:
  7.2 83.2 %all-gather.5.cloned.1.call-start = ((), (), s32[]{:S(2)}) async-start(), calls=%async_computation.12 | async-start | bytes 3440640 | tf_op jit(solution)/shard_map/all_gather | solution.py:934
  27.9 162.0 %all-gather.7.cloned.1.call-start = ((), (), s32[]{:S(2)}) async-start(), calls=%async_computation.13 | async-start | bytes 5898240 | tf_op jit(solution)/shard_map/all_gather | solution.py:946
  80.0 40.0 %collective-permute-start.8 = (bf16[448,1536]{1,0:T(8,128)(2,1)S(1)}, bf16[448,1536]{1,0:T(8,128)(2,1)S(1)}, u32[]{:S(2)}, u32[]{:S(2)}) collective-permute-start(bf16[448,1536]{1,0:T(8,128)(2,1)S(1)} %join_rows.7.refs_0_), channel_id=1, source_target_pairs={{0,8},{4,12},{8,0},{12,4},{16,24},{20,28},{24,16},{28,20},{1,9},{5... | collective-permute-start | bytes 4128776 | tf_op jit(solution)/shard_map/ppermute | solution.py:29
  80.6 39.4 %collective-permute-start.9 = (bf16[448,1536]{1,0:T(8,128)(2,1)S(1)}, bf16[448,1536]{1,0:T(8,128)(2,1)}, u32[]{:S(2)}, u32[]{:S(2)}) collective-permute-start(bf16[448,1536]{1,0:T(8,128)(2,1)S(1)} %join_rows.7.refs_0_), channel_id=1, source_target_pairs={{0,16},{4,20},{8,24},{12,28},{16,0},{20,4},{24,8},{28,12},{1,17},{... | collective-permute-start | bytes 4128776 | tf_op jit(solution)/shard_map/ppermute | solution.py:29
  85.1 46.2 %collective-permute-start.12 = (bf16[448,1536]{1,0:T(8,128)(2,1)S(1)}, bf16[448,1536]{1,0:T(8,128)(2,1)}, u32[]{:S(2)}, u32[]{:S(2)}) collective-permute-start(bf16[448,1536]{1,0:T(8,128)(2,1)S(1)} %join_rows.7.refs_0_), channel_id=1, source_target_pairs={{0,4},{4,0},{8,12},{12,8},{16,20},{20,16},{24,28},{28,24},{1,5},{5... | collective-permute-start | bytes 4128776 | tf_op jit(solution)/shard_map/ppermute | solution.py:29
  120.0 34.2 %collective-permute-start.13 = (bf16[448,1536]{1,0:T(8,128)(2,1)S(1)}, bf16[448,1536]{1,0:T(8,128)(2,1)}, u32[]{:S(2)}, u32[]{:S(2)}) collective-permute-start(bf16[448,1536]{1,0:T(8,128)(2,1)S(1)} %collective-permute-done.8.refs_1_), channel_id=1, source_target_pairs={{0,4},{4,0},{8,12},{12,8},{16,20},{20,16},{24,28},{28,24},{1,5},{5... | collective-permute-start | bytes 4128776 | tf_op jit(solution)/shard_map/ppermute | solution.py:29
  120.1 34.1 %collective-permute-start.14 = (bf16[448,1536]{1,0:T(8,128)(2,1)}, bf16[448,1536]{1,0:T(8,128)(2,1)}, u32[]{:S(2)}, u32[]{:S(2)}) collective-permute-start(bf16[448,1536]{1,0:T(8,128)(2,1)} %collective-permute-done.9.refs_2_), channel_id=1, source_target_pairs={{0,4},{4,0},{8,12},{12,8},{16,20},{20,16},{24,28},{28,24},{1,5},{5... | collective-permute-start | bytes 4128776 | tf_op jit(solution)/shard_map/ppermute | solution.py:29
  127.7 162.8 %reduce-scatter.4.cloned.1.call-start = ((), (), s32[]{:S(2)}) async-start(), calls=%async_computation.9 | async-start | bytes 1966080 | tf_op jit(solution)/shard_map/reduce_scatter | solution.py:992
  127.9 26.2 %collective-permute-start.10 = (bf16[224,1536]{1,0:T(8,128)(2,1)}, bf16[224,1536]{1,0:T(8,128)(2,1)}, u32[]{:S(2)}, u32[]{:S(2)}) collective-permute-start(bf16[224,1536]{1,0:T(8,128)(2,1)} %slice.183), channel_id=1, source_target_pairs={{0,16},{4,20},{8,24},{12,28},{16,0},{20,4},{24,8},{28,12},{1,17},{... | collective-permute-start | bytes 2064392 | tf_op jit(solution)/shard_map/ppermute | solution.py:29
  182.1 31.3 %collective-permute-start.22 = (bf16[256,1536]{1,0:T(8,128)(2,1)}, bf16[256,1536]{1,0:T(8,128)(2,1)}, u32[]{:S(2)}, u32[]{:S(2)}) collective-permute-start(bf16[256,1536]{1,0:T(8,128)(2,1)} %collective-permute-done.18.refs_1_), channel_id=1, source_target_pairs={{0,4},{4,0},{8,12},{12,8},{16,20},{20,16},{24,28},{28,24},{1,5},{5... | collective-permute-start | bytes 2359304 | tf_op jit(solution)/shard_map/ppermute | solution.py:29
  182.1 31.3 %collective-permute-start.23 = (bf16[256,1536]{1,0:T(8,128)(2,1)}, bf16[256,1536]{1,0:T(8,128)(2,1)}, u32[]{:S(2)}, u32[]{:S(2)}) collective-permute-start(bf16[256,1536]{1,0:T(8,128)(2,1)} %collective-permute-done.19.refs_2_), channel_id=1, source_target_pairs={{0,4},{4,0},{8,12},{12,8},{16,20},{20,16},{24,28},{28,24},{1,5},{5... | collective-permute-start | bytes 2359304 | tf_op jit(solution)/shard_map/ppermute | solution.py:29
  186.2 27.2 %collective-permute-start.20 = (bf16[128,1536]{1,0:T(8,128)(2,1)}, bf16[128,1536]{1,0:T(8,128)(2,1)}, u32[]{:S(2)}, u32[]{:S(2)}) collective-permute-start(bf16[128,1536]{1,0:T(8,128)(2,1)} %slice.188), channel_id=1, source_target_pairs={{0,16},{4,20},{8,24},{12,28},{16,0},{20,4},{24,8},{28,12},{1,17},{... | collective-permute-start | bytes 1179656 | tf_op jit(solution)/shard_map/ppermute | solution.py:29
  186.7 26.7 %collective-permute-start.21 = (bf16[128,1536]{1,0:T(8,128)(2,1)}, bf16[128,1536]{1,0:T(8,128)(2,1)}, u32[]{:S(2)}, u32[]{:S(2)}) collective-permute-start(bf16[128,1536]{1,0:T(8,128)(2,1)} %slice.189), channel_id=1, source_target_pairs={{0,8},{4,12},{8,0},{12,4},{16,24},{20,28},{24,16},{28,20},{1,9},{5... | collective-permute-start | bytes 1179656 | tf_op jit(solution)/shard_map/ppermute | solution.py:29
  248.8 110.5 %reduce-scatter.6.cloned.1.call-start = ((), (), s32[]{:S(2)}) async-start(), calls=%async_computation.10 | async-start | bytes 3932160 | tf_op jit(solution)/shard_map/reduce_scatter | solution.py:902
  253.9 36.6 %collective-permute-start.30 = (bf16[256,1536]{1,0:T(8,128)(2,1)}, bf16[256,1536]{1,0:T(8,128)(2,1)S(1)}, u32[]{:S(2)}, u32[]{:S(2)}) collective-permute-start(bf16[256,1536]{1,0:T(8,128)(2,1)} %get-tuple-element.264), channel_id=1, source_target_pairs={{0,16},{4,20},{8,24},{12,28},{16,0},{20,4},{24,8},{28,12},{1,17},{... | collective-permute-start | bytes 2359304 | tf_op jit(solution)/shard_map/ppermute | solution.py:29
  255.4 35.1 %collective-permute-start.31 = (bf16[256,1536]{1,0:T(8,128)(2,1)}, bf16[256,1536]{1,0:T(8,128)(2,1)}, u32[]{:S(2)}, u32[]{:S(2)}) collective-permute-start(bf16[256,1536]{1,0:T(8,128)(2,1)} %get-tuple-element.265), channel_id=1, source_target_pairs={{0,24},{4,28},{8,16},{12,20},{16,8},{20,12},{24,0},{28,4},{1,25},{... | collective-permute-start | bytes 2359304 | tf_op jit(solution)/shard_map/ppermute | solution.py:29
  323.1 33.6 %collective-permute-start.35 = (bf16[256,1536]{1,0:T(8,128)(2,1)S(1)}, bf16[256,1536]{1,0:T(8,128)(2,1)}, u32[]{:S(2)}, u32[]{:S(2)}) collective-permute-start(bf16[256,1536]{1,0:T(8,128)(2,1)S(1)} %pad_maximum_fusion), channel_id=1, source_target_pairs={{0,8},{4,12},{8,0},{12,4},{16,24},{20,28},{24,16},{28,20},{1,9},{5... | collective-permute-start | bytes 2359304 | tf_op jit(solution)/shard_map/ppermute | solution.py:29
  323.6 33.1 %collective-permute-start.36 = (bf16[256,1536]{1,0:T(8,128)(2,1)}, bf16[256,1536]{1,0:T(8,128)(2,1)}, u32[]{:S(2)}, u32[]{:S(2)}) collective-permute-start(bf16[256,1536]{1,0:T(8,128)(2,1)} %pad_maximum_fusion.1), channel_id=1, source_target_pairs={{0,16},{4,20},{8,24},{12,28},{16,0},{20,4},{24,8},{28,12},{1,17},{... | collective-permute-start | bytes 2359304 | tf_op jit(solution)/shard_map/ppermute | solution.py:29
  325.0 31.7 %collective-permute-start.37 = (bf16[96,1536]{1,0:T(8,128)(2,1)}, bf16[96,1536]{1,0:T(8,128)(2,1)S(1)}, u32[]{:S(2)}, u32[]{:S(2)}) collective-permute-start(bf16[96,1536]{1,0:T(8,128)(2,1)} %get-tuple-element.371), channel_id=1, source_target_pairs={{0,8},{4,12},{8,0},{12,4},{16,24},{20,28},{24,16},{28,20},{1,9},{5... | collective-permute-start | bytes 884744 | tf_op jit(solution)/shard_map/ppermute | solution.py:29
  326.4 30.2 %collective-permute-start.38 = (bf16[96,1536]{1,0:T(8,128)(2,1)S(1)}, bf16[96,1536]{1,0:T(8,128)(2,1)S(1)}, u32[]{:S(2)}, u32[]{:S(2)}) collective-permute-start(bf16[96,1536]{1,0:T(8,128)(2,1)S(1)} %get-tuple-element.370), channel_id=1, source_target_pairs={{0,16},{4,20},{8,24},{12,28},{16,0},{20,4},{24,8},{28,12},{1,17},{... | collective-permute-start | bytes 884744 | tf_op jit(solution)/shard_map/ppermute | solution.py:29
  363.0 68.8 %reduce-scatter.8.cloned.1.call-start = ((), (), s32[]{:S(2)}) async-start(), calls=%async_computation.11 | async-start | bytes 3440640 | tf_op jit(solution)/shard_map/reduce_scatter | solution.py:902
  385.2 27.7 %collective-permute-start.40 = (bf16[256,1536]{1,0:T(8,128)(2,1)S(1)}, bf16[256,1536]{1,0:T(8,128)(2,1)}, u32[]{:S(2)}, u32[]{:S(2)}) collective-permute-start(bf16[256,1536]{1,0:T(8,128)(2,1)S(1)} %get-tuple-element.352), channel_id=1, source_target_pairs={{0,8},{4,12},{8,0},{12,4},{16,24},{20,28},{24,16},{28,20},{1,9},{5... | collective-permute-start | bytes 2359304 | tf_op jit(solution)/shard_map/ppermute | solution.py:29
  385.4 44.6 %collective-permute-start.41 = (bf16[256,1536]{1,0:T(8,128)(2,1)S(1)}, bf16[256,1536]{1,0:T(8,128)(2,1)}, u32[]{:S(2)}, u32[]{:S(2)}) collective-permute-start(bf16[256,1536]{1,0:T(8,128)(2,1)S(1)} %get-tuple-element.351), channel_id=1, source_target_pairs={{0,16},{4,20},{8,24},{12,28},{16,0},{20,4},{24,8},{28,12},{1,17},{... | collective-permute-start | bytes 2359304 | tf_op jit(solution)/shard_map/ppermute | solution.py:29
  386.4 43.6 %collective-permute-start.42 = (bf16[256,1536]{1,0:T(8,128)(2,1)S(1)}, bf16[256,1536]{1,0:T(8,128)(2,1)}, u32[]{:S(2)}, u32[]{:S(2)}) collective-permute-start(bf16[256,1536]{1,0:T(8,128)(2,1)S(1)} %get-tuple-element.350), channel_id=1, source_target_pairs={{0,24},{4,28},{8,16},{12,20},{16,8},{20,12},{24,0},{28,4},{1,25},{... | collective-permute-start | bytes 2359304 | tf_op jit(solution)/shard_map/ppermute | solution.py:29
  (91 other events, 1086.5 us)
Sparse Core Ops, SparseCore 0:
  28.0 62.3 all-gather.4
  92.5 88.5 all-gather.6
  248.9 39.5 reduce-scatter.3
  294.7 64.5 reduce-scatter.5
  375.7 56.0 reduce-scatter.7

commit v4 on v3

--- a/solution.py
+++ b/solution.py
@@ -45,6 +45,11 @@
 def both_cores(near, far):
     sums = [x.astype(F32) + y.astype(F32) for x, y in zip(near, far)]
     return sums[0], [x.astype(BF16) for x in sums[1:]]
+
+
+def two_sums(near, far):
+    rows = near.shape[0] // 2
+    return [near[i : i + rows].astype(F32) + far[i : i + rows].astype(F32) for i in (0, rows)]
 
 
 def quarters(array):
@@ -752,6 +757,26 @@
     )(spots, *arrays, *w)
 
 
+def last_norm(tok, gain, dx2, *parts):
+    rows, width = tok.shape
+    steps = 4
+
+    def kernel(tok_ref, gain_ref, dx2_ref, *refs):
+        n1, r1 = normed(tok_ref[...].astype(F32))
+        refs[-1][...] = dx2_ref[...] + norm_back(n1, r1, total_of([x[...] for x in refs[:-1]]) * gain_ref[...])
+
+    block = pl.BlockSpec((rows // steps, width), lambda i: (i, 0))
+    return pl.pallas_call(
+        kernel,
+        grid=(steps,),
+        in_specs=[block, once(gain.shape), block] + [block] * len(parts),
+        out_specs=block,
+        out_shape=shape((rows, width), F32),
+        **settings(3, 24),
+        name="last_norm",
+    )(tok, gain, dx2, *parts)
+
+
 def ffn_kernel(lens_ref, h2_ref, cot_ref, gu_ref, dn_ref, ab_ref, dgu_ref, *out_refs):
     rows, ff = h2_ref.shape[0], dn_ref.shape[0]
     total = jnp.int32(0)
@@ -772,14 +797,14 @@
     dh2 = dot(dgate, gu_ref[:, :ff], ((1,), (1,))) + dot(dup, gu_ref[:, ff:], ((1,), (1,)))
     dh2 = dh2.astype(BF16)
     out = dot(ab, dn_ref[...]).astype(BF16)
-    last = pl.program_id(0) == pl.num_programs(0) - 1
-
-    @pl.when(jnp.logical_not(last))
+    near = pl.program_id(0) < pl.num_programs(0) // 2
+
+    @pl.when(near)
     def _():
         out_refs[0][...] = out
         out_refs[1][...] = dh2
 
-    @pl.when(last)
+    @pl.when(jnp.logical_not(near))
     def _():
         out_refs[2][...] = out
         out_refs[3][...] = dh2
@@ -787,6 +812,7 @@
 
 def ffn(lens, h2, cot, gu, dn):
     buckets = lens.shape[0]
+    half = buckets // 2
     total, width = h2.shape
     rows = total // buckets
     ff = dn.shape[0]
@@ -797,28 +823,31 @@
     def whole(dims):
         return pl.BlockSpec(dims, lambda i: (0, 0))
 
-    most = pl.BlockSpec((rows, width), lambda i: (jnp.minimum(i, buckets - 2), 0))
+    near = pl.BlockSpec((rows, width), lambda i: (jnp.minimum(i, half - 1), 0))
+    far = pl.BlockSpec((rows, width), lambda i: (jnp.maximum(i - half, 0), 0))
     return pl.pallas_call(
         ffn_kernel,
         grid=(buckets,),
         in_specs=[SMEM, block(width), block(width), whole(gu.shape), whole(dn.shape)],
-        out_specs=[block(ff), block(2 * ff), most, most, whole((rows, width)), whole((rows, width))],
-        out_shape=[shape((total, ff), BF16), shape((total, 2 * ff), BF16)]
-        + [shape((total - rows, width), BF16)] * 2
-        + [shape((rows, width), BF16)] * 2,
+        out_specs=[block(ff), block(2 * ff), near, near, far, far],
+        out_shape=[shape((total, ff), BF16), shape((total, 2 * ff), BF16)] + [shape((total // 2, width), BF16)] * 4,
         **settings(4 * buckets, 40),
         name="ffn",
     )(lens, h2, cot, gu, dn)
+
+
+def sum_of_dots(lefts, rights):
+    return sum(dot(x[...], y[...], ((0,), (0,))) for x, y in zip(lefts, rights))
 
 
 def grad_down(ab, cot):
     ff, width = ab[0].shape[1], cot[0].shape[1]
     steps = 4
     columns = width // steps
-
-    def kernel(ab0_ref, ab1_ref, cot0_ref, cot1_ref, out_ref):
-        res = dot(ab0_ref[...], cot0_ref[...], ((0,), (0,))) + dot(ab1_ref[...], cot1_ref[...], ((0,), (0,)))
-        out_ref[...] = res.astype(BF16)
+    count = len(ab)
+
+    def kernel(*refs):
+        refs[-1][...] = sum_of_dots(refs[:count], refs[count : 2 * count]).astype(BF16)
 
     return pl.pallas_call(
         kernel,
@@ -833,24 +862,24 @@
 
 
 def grad_gu(h2, dgu, share):
-    rows, width = h2[0].shape
+    width = h2[0].shape[1]
     own_rows = width // (TP * share)
     columns = dgu[0].shape[1]
     steps = TP // 2
-
-    def kernel(left0_ref, left1_ref, right0_ref, right1_ref, out_ref):
-        res = dot(left0_ref[...], right0_ref[...], ((0,), (0,)))
-        res = res + dot(left1_ref[...], right1_ref[...], ((0,), (0,)))
+    count = len(h2)
+
+    def kernel(*refs):
+        res = sum_of_dots(refs[:count], refs[count : 2 * count])
         for k in range(2):
             for z in range(share):
                 at = (k * share + z) * own_rows
-                out_ref[z, k] = res[at : at + own_rows].astype(BF16)
+                refs[-1][z, k] = res[at : at + own_rows].astype(BF16)
 
     return pl.pallas_call(
         kernel,
         grid=(steps,),
-        in_specs=[pl.BlockSpec((rows, width // steps), lambda i: (0, i))] * 2
-        + [pl.BlockSpec((rows, columns), lambda i: (0, 0))] * 2,
+        in_specs=[pl.BlockSpec((x.shape[0], width // steps), lambda i: (0, i)) for x in h2]
+        + [pl.BlockSpec(x.shape, lambda i: (0, 0)) for x in dgu],
         out_specs=pl.BlockSpec((share, 2, own_rows, columns), lambda i: (0, i, 0, 0)),
         out_shape=shape((share, TP, own_rows, columns), BF16),
         **settings(11, 60),
@@ -952,74 +981,78 @@
     gain_one, gain_two = gains[0:1], gains[3:4]
     mixed, two_four = phase(mixed, two_four)
     near = [beside, *two_four]
-    six = diagonal(*two_four)
-    got_mixed, six, far = phase(swap(mixed), six, [flip(x, 1) for x in near])
-    far = [*far, *[flip(x, 1) for x in six]]
-    near = [*near, *six]
-    x2, h2 = mid_fwd(spots, got_mixed, near[:4] + far[:4], tokens, gain_two)
-
-    first, second = (0, 2, 4, 1), (3, 5, 7, 6)
-    lens_of = [jnp.stack([lens[OFFSETS.index(d)] for d in order]) for order in (first, second)]
+    got_mixed, mix_six, far = phase(
+        swap(mixed), diagonal(*[x[:BLOCK] for x in two_four]), [flip(x, 1) for x in near]
+    )
+    mix_six = jnp.concatenate(mix_six, axis=0)
+    w_mix = [*near, mix_six, *far, flip(mix_six, 1)]
+    x2, h2 = mid_fwd(spots, got_mixed, w_mix, tokens, gain_two)
+
+    orders = (2, 4, 3, 5), (0, 1), (6, 7)
+    lens_of = [jnp.stack([lens[OFFSETS.index(d)] for d in order]) for order in orders]
     h2, near, far = phase(h2, near, far)
-    w_mix = near[:4] + far[:4]
-    two, four = sides(h2)
-    one = flip(h2, 1)
     cot = [
-        join_rows((near[0], BLOCK), (near[1], BLOCK), (near[2], BLOCK), (far[0], BLOCK)),
-        join_rows((far[1], BLOCK), (far[2], BLOCK), (far[3], BLOCK), far[4], (near[3], BLOCK), near[4]),
+        join_rows(*[(half[i], BLOCK) for half in (near, far) for i in (1, 2)]),
+        join_rows((near[0], BLOCK), (far[0], BLOCK)),
     ]
-    one, two, four, cot = phase(one, two, four, cot)
+    (two, four), one, cot = phase(sides(h2), flip(h2, 1), cot)
     six = diagonal(two, four)
-    three, five = flip(two, 1), flip(four, 1)
-    h2 = join_rows(h2, two, four, one)
-    found = ffn(lens_of[0], h2, cot[0], w_gu, w_dn)
-    found, six, three, five = phase(found, six, three, five)
-    out_one, dh2_one = flip(found[4], 1), flip(found[5], 1)
-    six = jnp.concatenate(six, axis=0)
-    six, seven = phase(six, flip(six, 1))
-    h2 = h2, join_rows(three, five, seven, six)
-    found = [found, ffn(lens_of[1], h2[1], cot[1], w_gu, w_dn)]
-    found, dh2_one, out_one = phase(found, dh2_one, out_one)
-    ab, dgu, out, dh2, out_last, dh2_last = zip(*found)
-    dh2_far, dw_dn, out_far = phase(flip(dh2[1], 1), grad_down(ab, cot), flip(out[1], 1))
-
-    def folded(near, six, one, far):
-        rows = six.shape[0]
-        parts = [[x[i * rows : (i + 1) * rows] for i in range(3)] for x in (near, far)]
-        return both_cores([*parts[0], six], [one, *parts[1]])
-
-    own, low = folded(dh2[0], dh2_last[1], dh2_one, dh2_far)
+    two, four, three, five, one = phase(two, four, flip(two, 1), flip(four, 1), one)
+    h2 = [join_rows(two, four, three, five), join_rows(h2, one)]
+    found = [ffn(lens_of[0], h2[0], cot[0], w_gu, w_dn)]
+    found, six, h2[1], cot_six = phase(found, six, h2[1], diagonal(*[x[BLOCK:] for x in near[1:3]]))
+    six, cot_six = [jnp.concatenate(x, axis=0) for x in (six, cot_six)]
+    seven, cot_seven, far, more = phase(
+        flip(six, 1),
+        flip(cot_six, 1),
+        [flip(x, 1) for x in found[0][4:]],
+        ffn(lens_of[1], h2[1], cot[1], w_gu, w_dn),
+    )
+    found.append(more)
+    layer_side, side = [[x.astype(BF16) for x in two_sums(*pair)] for pair in zip(found[0][2:4], far)]
+    h2.append(join_rows(six, seven))
+    cot.append(join_rows(cot_six, cot_seven))
+    side, layer_side, h2[2], cot[2], one = phase(side, layer_side, h2[2], cot[2], found[1][5])
+    side = flip(side[0], 2), flip(side[1], 4)
+    one, more = phase(flip(one, 1), ffn(lens_of[2], h2[2], cot[2], w_gu, w_dn))
+    found.append(more)
+    ab, dgu, out_near, dh2_near, out_far, dh2_far = zip(*found)
+    seven, dw_gu, side = phase(flip(dh2_far[2], 1), grad_gu(h2, dgu, share), side)
+    dw_gu = own_share(dw_gu)
+    low = (dh2_near[2].astype(F32) + seven.astype(F32)).astype(BF16)
+    low, ab, out_far = phase(low, ab, out_far)
+    own = dh2_near[1].astype(F32) + one.astype(F32)
+    six, dw_dn, out_far, own = phase(flip(low, 6), grad_down(ab, cot), [flip(x, 1) for x in out_far[1:]], own)
     dw_dn = lax.psum_scatter(dw_dn, "sh", scatter_dimension=0, tiled=True)
-    own, low, dgu, out_far = phase(own, low, dgu, out_far)
-    layer_own, layer_low = folded(out[0], out_last[1], out_one, out_far)
-    dh2, dw_gu, dw_dn, own, layer_low = phase(send(low), grad_gu(h2, dgu, share), dw_dn, own, layer_low)
-    dw_gu = own_share(dw_gu)
+    layer_six = (out_near[2].astype(F32) + out_far[1].astype(F32)).astype(BF16)
+    dh2, layer_low = phase((own, *side, six), (*layer_side, layer_six))
 
     found, layer_low = phase(
-        mid_bwd(spots, [own] + dh2, x2, cotangent, gain_two, got_mixed, w_mix), relay_six(layer_low)
+        mid_bwd(spots, dh2, x2, cotangent, gain_two, got_mixed, w_mix), relay_six(layer_low)
     )
     dx2, dm, mix_near, mix_far = found
     mix_own, mix_low = both_cores(quarters(mix_near), quarters(flip(mix_far, 1)))
     got_dm, mix_own, mix_low, layer_low = phase(swap(dm), mix_own, mix_low, add_six(layer_low))
-    layer, mix_low, found = phase(
+    layer, mix_low, found, dw_gu = phase(
         (flip(layer_low[0], 2), flip(layer_low[1], 4)),
         relay_six(mix_low),
         attn_bwd(lens, spots, gain_heads, wide, backs, w_in, att, lse, got_dm, *kept),
+        dw_gu,
     )
     dp, sums, dh1_near, dh1_far = found
-    layer_out = (x2 + total_of((layer_own, *layer))).astype(BF16)
 
     mix_low = add_six(mix_low)
     mix = flip(mix_low[0], 2), flip(mix_low[1], 4)
-    dh1_far, dw_in, got_gu = phase(
-        flip(dh1_far, 1), grad_in(place.reshape(1), sums, h1, dp, share), swap(dw_gu)
+    dh1_far, dw_in, got_gu, dw_dn = phase(
+        flip(dh1_far, 1), grad_in(place.reshape(1), sums, h1, dp, share), swap(dw_gu), dw_dn
     )
     dw_in = own_share(dw_in)
     dh1_own, dh1_low = both_cores(quarters(dh1_near), quarters(dh1_far))
-    dh1, dw_in, mix = phase(send(dh1_low), dw_in, mix)
+    layer_own = out_near[1].astype(F32) + out_far[0].astype(F32)
+    layer_out = (x2 + total_of((layer_own, *layer))).astype(BF16)
+    dh1, mix, dw_in, layer_out = phase(send(dh1_low), mix, dw_in, layer_out)
     mix = to_shares(total_of((mix_own, *mix)).astype(BF16))
-    n1, r1 = normed(tokens.astype(F32))
-    d_tokens = dx2 + norm_back(n1, r1, total_of([dh1_own] + dh1) * gain_one)
+    d_tokens = last_norm(tokens, gain_one, dx2, dh1_own, *dh1)
 
     d_w_attn_in, d_w_rates, small = unpack_in(swap(dw_in), w_attn_in, w_rates, norm_gain)
     d_w_gate_up, small_gu = unpack_gu(got_gu, w_gate_up, ffn_gain)

time: 470 us -> 456 us (0.970)
  the two profiles are of different devices: /device:TPU:0 before, /device:TPU:26 now
where the time goes in v4:
time: 456 us; the launch traced here: 448 us
  Pallas kernels  150 us (33%)
  waiting for transfers between devices  127 us (28%)
  starting transfers between devices  66 us (14%)
  local copies, waits for them, and re-layouts  49.8 us (11%)
  other arithmetic  25.8 us (6%)
  between operations  15.2 us (3%)
  blocking collectives  14.3 us (3%)
    ppermute x46, waiting for transfers between devices, flip(): return lax.ppermute(array, 'tp', [(i, i ^ offset) for i in range(TP)])  80.8 us
    unnamed x165, local copies, waits for them, and re-layouts  35 us
    ppermute x46, starting transfers between devices, flip(): return lax.ppermute(array, 'tp', [(i, i ^ offset) for i in range(TP)])  33.3 us
    pallas_call x3, Pallas kernels, ffn(): pl.pallas_call(ffn_kernel, grid=(buckets,), in_specs=[SMEM, block(width),...  29.9 us
    pallas_call x1, Pallas kernels, attn_fwd(): pl.pallas_call(attn_fwd_kernel, grid_spec=pltpu.PrefetchScalarGridSpec(nu...  29.6 us
    pallas_call x1, Pallas kernels, attn_bwd(): pl.pallas_call(attn_bwd_kernel, grid_spec=pltpu.PrefetchScalarGridSpec(nu...  28.7 us
    ppermute x3, waiting for transfers between devices, gather_shares(): lax.ppermute(own, 'sh', [(i, (i + k) % share) for i in range(share)])  26 us
    all_to_all x5, starting transfers between devices, swap(): return lax.all_to_all(blocks, 'tp', 0, 0, tiled=True)  23.2 us
  transfers between devices with their start and end apart: 62, of which 14 were waited for; matrix products, arithmetic and copies ran while one was open for 9% of the time, Pallas kernels for 33%

profile of v4, /device:TPU:26, one launch (start us, length us, event | category | flops | bytes accessed | tf_op | source)
XLA Modules:
  0.0 447.6 jit_solution(8186782408895766315)
XLA Ops:
  11.2 14.3 %all_to_all.30 = bf16[8,48,896]{2,1,0:T(8,128)(2,1)} all-to-all(bf16[8,48,896]{2,1,0:T(8,128)(2,1)S(1)} %pack_in.1), channel_id=1, replica_groups=mesh['dp'=8,'fsdp'=4] {'dp'}, dimensions={0} | all-to-all | bytes 1376256 | tf_op jit(solution)/shard_map/all_to_all | solution.py:936
  33.5 22.6 %collective-permute-done.3 = bf16[48,1536]{1,0:T(8,128)(2,1)S(1)} collective-permute-done((bf16[48,1536]{1,0:T(8,128)(2,1)S(1)}, bf16[48,1536]{1,0:T(8,128)(2,1)S(1)}, u32[]{:S(2)}, u32[]{:S(2)}) %collective-permute-start.3) | collective-permute-done | bytes 147488 | tf_op jit(solution)/shard_map/ppermute | solution.py:80
  59.5 4.4 collective-permute-done.5.refs_3_
  67.3 4.4 all-to-all-start.1
  72.0 10.9 %all-to-all-done.1.got_ref = bf16[8,48,1024]{2,1,0:T(8,128)(2,1)S(1)} async-done(((bf16[8,48,1024]{2,1,0:T(8,128)(2,1)}), bf16[8,48,1024]{2,1,0:T(8,128)(2,1)S(1)}, u32[]{:S(2)}, u32[]{:S(2)}) %all-to-all-start.1) | async-done | bytes 786464 | tf_op jit(solution)/shard_map/all_to_all | solution.py:936
  90.6 29.6 %attn_fwd.1 = (bf16[2048,1536]{1,0:T(8,128)(2,1)}, bf16[8,384,128]{2,1,0:T(8,128)(2,1)}, f32[2048,192]{1,0:T(8,128)}, f32[64,256]{1,0:T(8,128)}, f32[8,1536]{1,0...) custom-call(s32[8,4]{1,0:T(8,128)} %gather_fusion, ...), custom_call_target="tpu_custom_call" | custom-call | flops 200000000 | bytes 200000 | tf_op jit(solution)/shard_map/attn_fwd/pallas_call | solution.py:620
  120.9 4.3 all-to-all-start.2
  128.2 14.3 %collective-permute-done.10 = bf16[96,1536]{1,0:T(8,128)(2,1)S(1)} collective-permute-done((bf16[96,1536]{1,0:T(8,128)(2,1)S(1)}, bf16[96,1536]{1,0:T(8,128)(2,1)S(1)}, u32[]{:S(2)}, u32[]{:S(2)}) %collective-permute-start.10) | collective-permute-done | bytes 294944 | tf_op jit(solution)/shard_map/ppermute | solution.py:29
  160.2 11.5 %collective-permute-done.16.refs_0_ = bf16[256,1536]{1,0:T(8,128)(2,1)S(1)} collective-permute-done((bf16[256,1536]{1,0:T(8,128)(2,1)S(1)}, bf16[256,1536]{1,0:T(8,128)(2,1)S(1)}, u32[]{:S(2)}, u32[]{:S(2)}) %collective-permute-start.16) | collective-permute-done | bytes 786464 | tf_op jit(solution)/shard_map/ppermute | solution.py:29
  187.5 15.9 %ffn.3 = (bf16[1024,512]{1,0:T(8,128)(2,1)S(1)}, bf16[1024,1024]{1,0:T(8,128)(2,1)S(1)}, bf16[512,1536]{1,0:T(8,128)(2,1)S(1)}, bf16[512,1536]{1,0:T(8,128)(2,1)...) custom-call(s32[4,4]{1,0:T(4,128)S(1)} %pad_add_fusion.lens_ref, ...), custom_call_target="tpu_custom_call" | custom-call | flops 160000000 | bytes 160000 | tf_op jit(solution)/shard_map/ffn/pallas_call | solution.py:828
  210.3 6.6 %ffn.4 = (bf16[512,512]{1,0:T(8,128)(2,1)S(1)}, bf16[512,1024]{1,0:T(8,128)(2,1)S(1)}, bf16[256,1536]{1,0:T(8,128)(2,1)S(1)}, bf16[256,1536]{1,0:T(8,128)(2,1)S(...) custom-call(s32[2,4]{1,0:T(2,128)S(1)} %get-tuple-element.431.lens_ref, ...), custom_call_target="tpu_custom_call" | custom-call | flops 80000000 | bytes 80000 | tf_op jit(solution)/shard_map/ffn/pallas_call | solution.py:828
  225.5 7.4 %ffn.5 = (bf16[512,512]{1,0:T(8,128)(2,1)S(1)}, bf16[512,1024]{1,0:T(8,128)(2,1)S(1)}, bf16[256,1536]{1,0:T(8,128)(2,1)S(1)}, bf16[256,1536]{1,0:T(8,128)(2,1)S(...) custom-call(s32[2,4]{1,0:T(2,128)S(1)} %get-tuple-element.432.lens_ref, ...), custom_call_target="tpu_custom_call" | custom-call | flops 80000000 | bytes 80000 | tf_op jit(solution)/shard_map/ffn/pallas_call | solution.py:828
  237.4 11.4 %grad_gu.1 = bf16[4,8,48,1024]{3,2,1,0:T(8,128)(2,1)} custom-call(bf16[1024,1536]{1,0:T(8,128)(2,1)} %copy-done.3, bf16[512,1536]{1,0:T(8,128)(2,1)} %copy-done.9, bf16[512,1536]{1,0:T(8,128)(2,1)} %copy-done.11, bf16[1024,1024]{1,0:T(8,128)(2,1)} %copy-done.30, bf16[512,1024]{1,0:T(8,128)(2,1)} %copy-done.33, bf16[512,1024]{1,0:T(8,128)(2,1)} %copy-done.34), custom_call_target="tpu_custom_call" | custom-call | flops 110000000 | bytes 110000 | tf_op jit(solution)/shard_map/grad_gu/pallas_call | solution.py:878
  256.1 8.7 %grad_down.1 = bf16[512,1536]{1,0:T(8,128)(2,1)} custom-call(bf16[1024,512]{1,0:T(8,128)(2,1)} %copy-done.32, bf16[512,512]{1,0:T(8,128)(2,1)} %copy-done.51, bf16[512,512]{1,0:T(8,128)(2,1)} %copy-done.52, bf16[1024,1536]{1,0:T(8,128)(2,1)} %copy-done, bf16[512,1536]{1,0:T(8,128)(2,1)} %copy-done.6, bf16[512,1536]{1,0:T(8,128)(2,1)} %copy-done.8), custom_call_target="tpu_custom_call" | custom-call | flops 60000000 | bytes 60000 | tf_op jit(solution)/shard_map/grad_down/pallas_call | solution.py:852
  264.8 8.5 %collective-permute-done.33.d_ref = bf16[256,1536]{1,0:T(8,128)(2,1)S(1)} collective-permute-done((bf16[256,1536]{1,0:T(8,128)(2,1)}, bf16[256,1536]{1,0:T(8,128)(2,1)S(1)}, u32[]{:S(2)}, u32[]{:S(2)}) %collective-permute-start.33) | collective-permute-done | bytes 786464 | tf_op jit(solution)/shard_map/ppermute | solution.py:29
  277.0 9.8 %mid_bwd.1 = (f32[256,1536]{1,0:T(8,128)}, bf16[8,384,128]{2,1,0:T(8,128)(2,1)}, bf16[768,1536]{1,0:T(8,128)(2,1)}, bf16[768,1536]{1,0:T(8,128)(2,1)}) custom-call(s32[8]{0:T(128)S(1)} %copy-done.57, f32[256,1536]{1,0:T(8,128)} %convert_add_fusion.1.a_ref, bf16[256,1536]{1,0:T(8,128)(2,1)} %collective-permute-done.31.b_ref, ...), custom_call_target="tpu_custom_call" | custom-call | flops 90000000 | bytes 90000 | tf_op jit(solution)/shard_map/mid_bwd/pallas_call | solution.py:749
  287.0 5.1 %all-to-all-start.3 = ((bf16[8,384,128]{2,1,0:T(8,128)(2,1)}), bf16[8,384,128]{2,1,0:T(8,128)(2,1)S(1)}, u32[]{:S(2)}, u32[]{:S(2)}) async-start(bf16[8,384,128]{2,1,0:T(8,128)(2,1)} %get-tuple-element.326), calls=%async_computation.3 | async-start | bytes 1572864 | tf_op jit(solution)/shard_map/all_to_all | solution.py:936
  298.2 5.0 %all-to-all-done.3.dm_ref = bf16[8,384,128]{2,1,0:T(8,128)(2,1)S(1)} async-done(((bf16[8,384,128]{2,1,0:T(8,128)(2,1)}), bf16[8,384,128]{2,1,0:T(8,128)(2,1)S(1)}, u32[]{:S(2)}, u32[]{:S(2)}) %all-to-all-start.3) | async-done | bytes 786464 | tf_op jit(solution)/shard_map/all_to_all | solution.py:936
  309.2 28.7 %attn_bwd.1 = (bf16[2048,896]{1,0:T(8,128)(2,1)}, f32[8,256]{1,0:T(8,128)}, bf16[1024,1536]{1,0:T(8,128)(2,1)}, bf16[1024,1536]{1,0:T(8,128)(2,1)}) custom-call(s32[8,4]{1,0:T(8,128)} %gather_fusion, s32[8]{0:T(128)} %get-tuple-element.430.spots_ref, f32[8,256]{1,0:T(8,128)} %get-tuple-element.338.gains_ref, bf16[448,192]{1,0:T(8,128)(2,1)} %constant.103.clone.wide_ref, ...), custom_call_target="tpu_custom_call" | custom-call | flops 240000000 | bytes 240000 | tf_op jit(solution)/shard_map/attn_bwd/pallas_call | solution.py:673
  338.1 5.1 %all-to-all-start.4 = ((bf16[8,48,1024]{2,1,0:T(8,128)(2,1)}), bf16[8,48,1024]{2,1,0:T(8,128)(2,1)S(1)}, u32[]{:S(2)}, u32[]{:S(2)}) async-start(bf16[8,48,1024]{2,1,0:T(8,128)(2,1)} %bitcast.47), calls=%async_computation.5 | async-start | bytes 1572864 | tf_op jit(solution)/shard_map/all_to_all | solution.py:936
  343.2 11.2 %grad_in.1 = bf16[4,8,48,896]{3,2,1,0:T(8,128)(2,1)} custom-call(s32[1]{0:T(128)} %bitcast.14.place_ref, f32[8,256]{1,0:T(8,128)} %get-tuple-element.362.sums_ref, bf16[2048,1536]{1,0:T(8,128)(2,1)} %get-tuple-element.363.left_ref, bf16[2048,896]{1,0:T(8,128)(2,1)} %get-tuple-element.364.right_ref), custom_call_target="tpu_custom_call" | custom-call | flops 110000000 | bytes 110000 | tf_op jit(solution)/shard_map/grad_in/pallas_call | solution.py:913
  372.6 37.4 %collective-permute-done.48 = bf16[192,1536]{1,0:T(8,128)(2,1)S(1)} collective-permute-done((bf16[192,1536]{1,0:T(8,128)(2,1)S(1)}, bf16[192,1536]{1,0:T(8,128)(2,1)S(1)}, u32[]{:S(2)}, u32[]{:S(2)}) %collective-permute-start.48) | collective-permute-done | bytes 589856 | tf_op jit(solution)/shard_map/ppermute | solution.py:29
  412.9 4.3 all-to-all-start.5
  419.0 5.1 %collective-permute-start.50 = (bf16[48,1536]{1,0:T(8,128)(2,1)S(1)}, bf16[48,1536]{1,0:T(8,128)(2,1)}, u32[]{:S(2)}, u32[]{:S(2)}) collective-permute-start(bf16[48,1536]{1,0:T(8,128)(2,1)S(1)} %get-tuple-element.413), channel_id=1, source_target_pairs={{0,2},{1,3},{2,0},{3,1},{4,6},{5,7},{6,4},{7,5},{8,10},{9,11},{10,... | collective-permute-start | bytes 442376 | tf_op jit(solution)/shard_map/ppermute | solution.py:98
  (357 shorter events, 145.9 us)
Async XLA Ops:
  7.2 83.4 %all-gather.5.cloned.1.call-start = ((), (), s32[]{:S(2)}) async-start(), calls=%async_computation.12 | async-start | bytes 3440640 | tf_op jit(solution)/shard_map/all_gather | solution.py:963
  25.5 30.5 %collective-permute-start = (bf16[256,1536]{1,0:T(8,128)(2,1)S(1)}, bf16[256,1536]{1,0:T(8,128)(2,1)S(1)}, u32[]{:S(2)}, u32[]{:S(2)}) collective-permute-start(bf16[256,1536]{1,0:T(8,128)(2,1)S(1)} %copy-done.14), channel_id=1, source_target_pairs={{0,8},{4,12},{8,0},{12,4},{16,24},{20,28},{24,16},{28,20},{1,9},{5... | collective-permute-start | bytes 2359304 | tf_op jit(solution)/shard_map/ppermute | solution.py:29
  27.1 29.0 %collective-permute-start.1 = (bf16[256,1536]{1,0:T(8,128)(2,1)S(1)}, bf16[256,1536]{1,0:T(8,128)(2,1)S(1)}, u32[]{:S(2)}, u32[]{:S(2)}) collective-permute-start(bf16[256,1536]{1,0:T(8,128)(2,1)S(1)} %copy-done.14), channel_id=1, source_target_pairs={{0,16},{4,20},{8,24},{12,28},{16,0},{20,4},{24,8},{28,12},{1,17},{... | collective-permute-start | bytes 2359304 | tf_op jit(solution)/shard_map/ppermute | solution.py:29
  27.9 28.2 %collective-permute-start.3 = (bf16[48,1536]{1,0:T(8,128)(2,1)S(1)}, bf16[48,1536]{1,0:T(8,128)(2,1)S(1)}, u32[]{:S(2)}, u32[]{:S(2)}) collective-permute-start(bf16[48,1536]{1,0:T(8,128)(2,1)S(1)} %copy-done.75), channel_id=1, source_target_pairs={{0,2},{1,3},{2,0},{3,1},{4,6},{5,7},{6,4},{7,5},{8,10},{9,11},{10,... | collective-permute-start | bytes 442376 | tf_op jit(solution)/shard_map/ppermute | solution.py:80
  29.5 26.5 %collective-permute-start.4 = (bf16[48,1536]{1,0:T(8,128)(2,1)S(1)}, bf16[48,1536]{1,0:T(8,128)(2,1)S(1)}, u32[]{:S(2)}, u32[]{:S(2)}) collective-permute-start(bf16[48,1536]{1,0:T(8,128)(2,1)S(1)} %copy-done.75), channel_id=1, source_target_pairs={{0,3},{1,0},{2,1},{3,2},{4,7},{5,4},{6,5},{7,6},{8,11},{9,8},{10,9... | collective-permute-start | bytes 442376 | tf_op jit(solution)/shard_map/ppermute | solution.py:80
  71.7 110.4 %all-gather.7.cloned.1.call-start = ((), (), s32[]{:S(2)}) async-start(), calls=%async_computation.13 | async-start | bytes 5898240 | tf_op jit(solution)/shard_map/all_gather | solution.py:975
  85.2 35.0 %collective-permute-start.8 = (bf16[448,1536]{1,0:T(8,128)(2,1)S(1)}, bf16[448,1536]{1,0:T(8,128)(2,1)S(1)}, u32[]{:S(2)}, u32[]{:S(2)}) collective-permute-start(bf16[448,1536]{1,0:T(8,128)(2,1)S(1)} %join_rows.9.refs_0_), channel_id=1, source_target_pairs={{0,8},{4,12},{8,0},{12,4},{16,24},{20,28},{24,16},{28,20},{1,9},{5... | collective-permute-start | bytes 4128776 | tf_op jit(solution)/shard_map/ppermute | solution.py:29
  86.8 33.5 %collective-permute-start.9 = (bf16[448,1536]{1,0:T(8,128)(2,1)S(1)}, bf16[448,1536]{1,0:T(8,128)(2,1)}, u32[]{:S(2)}, u32[]{:S(2)}) collective-permute-start(bf16[448,1536]{1,0:T(8,128)(2,1)S(1)} %join_rows.9.refs_0_), channel_id=1, source_target_pairs={{0,16},{4,20},{8,24},{12,28},{16,0},{20,4},{24,8},{28,12},{1,17},{... | collective-permute-start | bytes 4128776 | tf_op jit(solution)/shard_map/ppermute | solution.py:29
  90.6 37.7 %collective-permute-start.12 = (bf16[448,1536]{1,0:T(8,128)(2,1)S(1)}, bf16[448,1536]{1,0:T(8,128)(2,1)}, u32[]{:S(2)}, u32[]{:S(2)}) collective-permute-start(bf16[448,1536]{1,0:T(8,128)(2,1)S(1)} %join_rows.9.refs_0_), channel_id=1, source_target_pairs={{0,4},{4,0},{8,12},{12,8},{16,20},{20,16},{24,28},{28,24},{1,5},{5... | collective-permute-start | bytes 4128776 | tf_op jit(solution)/shard_map/ppermute | solution.py:29
  125.1 212.9 %reduce-scatter.4.cloned.1.call-start = ((), (), s32[]{:S(2)}) async-start(), calls=%async_computation.9 | async-start | bytes 3932160 | tf_op jit(solution)/shard_map/reduce_scatter | solution.py:931
  175.0 28.4 %collective-permute-start.23 = (bf16[128,1536]{1,0:T(8,128)(2,1)}, bf16[128,1536]{1,0:T(8,128)(2,1)}, u32[]{:S(2)}, u32[]{:S(2)}) collective-permute-start(bf16[128,1536]{1,0:T(8,128)(2,1)} %slice.196), channel_id=1, source_target_pairs={{0,16},{4,20},{8,24},{12,28},{16,0},{20,4},{24,8},{28,12},{1,17},{... | collective-permute-start | bytes 1179656 | tf_op jit(solution)/shard_map/ppermute | solution.py:29
  175.9 27.5 %collective-permute-start.24 = (bf16[128,1536]{1,0:T(8,128)(2,1)}, bf16[128,1536]{1,0:T(8,128)(2,1)}, u32[]{:S(2)}, u32[]{:S(2)}) collective-permute-start(bf16[128,1536]{1,0:T(8,128)(2,1)} %slice.197), channel_id=1, source_target_pairs={{0,8},{4,12},{8,0},{12,4},{16,24},{20,28},{24,16},{28,20},{1,9},{5... | collective-permute-start | bytes 1179656 | tf_op jit(solution)/shard_map/ppermute | solution.py:29
  178.4 25.0 %collective-permute-start.21 = (bf16[128,1536]{1,0:T(8,128)(2,1)}, bf16[128,1536]{1,0:T(8,128)(2,1)}, u32[]{:S(2)}, u32[]{:S(2)}) collective-permute-start(bf16[128,1536]{1,0:T(8,128)(2,1)} %slice.194), channel_id=1, source_target_pairs={{0,16},{4,20},{8,24},{12,28},{16,0},{20,4},{24,8},{28,12},{1,17},{... | collective-permute-start | bytes 1179656 | tf_op jit(solution)/shard_map/ppermute | solution.py:29
  223.7 25.1 %collective-permute-start.31 = (bf16[256,1536]{1,0:T(8,128)(2,1)S(1)}, bf16[256,1536]{1,0:T(8,128)(2,1)}, u32[]{:S(2)}, u32[]{:S(2)}) collective-permute-start(bf16[256,1536]{1,0:T(8,128)(2,1)S(1)} %get-tuple-element.290), channel_id=1, source_target_pairs={{0,8},{4,12},{8,0},{12,4},{16,24},{20,28},{24,16},{28,20},{1,9},{5... | collective-permute-start | bytes 2359304 | tf_op jit(solution)/shard_map/ppermute | solution.py:29
  292.1 62.3 %reduce-scatter.6.cloned.1.call-start = ((), (), s32[]{:S(2)}) async-start(), calls=%async_computation.10 | async-start | bytes 1966080 | tf_op jit(solution)/shard_map/reduce_scatter | solution.py:1026
  303.2 34.8 %collective-permute-start.39 = (bf16[256,1536]{1,0:T(8,128)(2,1)}, bf16[256,1536]{1,0:T(8,128)(2,1)}, u32[]{:S(2)}, u32[]{:S(2)}) collective-permute-start(bf16[256,1536]{1,0:T(8,128)(2,1)} %pad_maximum_fusion), channel_id=1, source_target_pairs={{0,8},{4,12},{8,0},{12,4},{16,24},{20,28},{24,16},{28,20},{1,9},{5... | collective-permute-start | bytes 2359304 | tf_op jit(solution)/shard_map/ppermute | solution.py:29
  304.7 33.3 %collective-permute-start.40 = (bf16[256,1536]{1,0:T(8,128)(2,1)}, bf16[256,1536]{1,0:T(8,128)(2,1)}, u32[]{:S(2)}, u32[]{:S(2)}) collective-permute-start(bf16[256,1536]{1,0:T(8,128)(2,1)} %pad_maximum_fusion.1), channel_id=1, source_target_pairs={{0,16},{4,20},{8,24},{12,28},{16,0},{20,4},{24,8},{28,12},{1,17},{... | collective-permute-start | bytes 2359304 | tf_op jit(solution)/shard_map/ppermute | solution.py:29
  307.2 30.8 %collective-permute-start.41 = (bf16[96,1536]{1,0:T(8,128)(2,1)}, bf16[96,1536]{1,0:T(8,128)(2,1)S(1)}, u32[]{:S(2)}, u32[]{:S(2)}) collective-permute-start(bf16[96,1536]{1,0:T(8,128)(2,1)} %get-tuple-element.417), channel_id=1, source_target_pairs={{0,8},{4,12},{8,0},{12,4},{16,24},{20,28},{24,16},{28,20},{1,9},{5... | collective-permute-start | bytes 884744 | tf_op jit(solution)/shard_map/ppermute | solution.py:29
  307.8 30.2 %collective-permute-start.42 = (bf16[96,1536]{1,0:T(8,128)(2,1)}, bf16[96,1536]{1,0:T(8,128)(2,1)}, u32[]{:S(2)}, u32[]{:S(2)}) collective-permute-start(bf16[96,1536]{1,0:T(8,128)(2,1)} %get-tuple-element.416), channel_id=1, source_target_pairs={{0,16},{4,20},{8,24},{12,28},{16,0},{20,4},{24,8},{28,12},{1,17},{... | collective-permute-start | bytes 884744 | tf_op jit(solution)/shard_map/ppermute | solution.py:29
  343.2 69.7 %reduce-scatter.8.cloned.1.call-start = ((), (), s32[]{:S(2)}) async-start(), calls=%async_computation.11 | async-start | bytes 3440640 | tf_op jit(solution)/shard_map/reduce_scatter | solution.py:931
  360.2 49.8 %collective-permute-start.44 = (bf16[256,1536]{1,0:T(8,128)(2,1)S(1)}, bf16[256,1536]{1,0:T(8,128)(2,1)S(1)}, u32[]{:S(2)}, u32[]{:S(2)}) collective-permute-start(bf16[256,1536]{1,0:T(8,128)(2,1)S(1)} %get-tuple-element.401), channel_id=1, source_target_pairs={{0,8},{4,12},{8,0},{12,4},{16,24},{20,28},{24,16},{28,20},{1,9},{5... | collective-permute-start | bytes 2359304 | tf_op jit(solution)/shard_map/ppermute | solution.py:29
  361.5 49.5 %collective-permute-start.45 = (bf16[256,1536]{1,0:T(8,128)(2,1)S(1)}, bf16[256,1536]{1,0:T(8,128)(2,1)S(1)}, u32[]{:S(2)}, u32[]{:S(2)}) collective-permute-start(bf16[256,1536]{1,0:T(8,128)(2,1)S(1)} %get-tuple-element.400), channel_id=1, source_target_pairs={{0,16},{4,20},{8,24},{12,28},{16,0},{20,4},{24,8},{28,12},{1,17},{... | collective-permute-start | bytes 2359304 | tf_op jit(solution)/shard_map/ppermute | solution.py:29
  362.9 49.1 %collective-permute-start.46 = (bf16[256,1536]{1,0:T(8,128)(2,1)S(1)}, bf16[256,1536]{1,0:T(8,128)(2,1)S(1)}, u32[]{:S(2)}, u32[]{:S(2)}) collective-permute-start(bf16[256,1536]{1,0:T(8,128)(2,1)S(1)} %get-tuple-element.399), channel_id=1, source_target_pairs={{0,24},{4,28},{8,16},{12,20},{16,8},{20,12},{24,0},{28,4},{1,25},{... | collective-permute-start | bytes 2359304 | tf_op jit(solution)/shard_map/ppermute | solution.py:29
  363.8 46.2 %collective-permute-start.48 = (bf16[192,1536]{1,0:T(8,128)(2,1)S(1)}, bf16[192,1536]{1,0:T(8,128)(2,1)S(1)}, u32[]{:S(2)}, u32[]{:S(2)}) collective-permute-start(bf16[192,1536]{1,0:T(8,128)(2,1)S(1)} %pad_maximum_fusion.3), channel_id=1, source_target_pairs={{0,16},{4,20},{8,24},{12,28},{16,0},{20,4},{24,8},{28,12},{1,17},{... | collective-permute-start | bytes 1769480 | tf_op jit(solution)/shard_map/ppermute | solution.py:29
  (119 other events, 1189.4 us)
Sparse Core Ops, SparseCore 0:
  25.6 61.0 all-gather.4
  88.9 87.7 all-gather.6
  249.8 63.0 reduce-scatter.3
  315.1 34.3 reduce-scatter.5
  354.6 56.4 reduce-scatter.7

commit v5 on v4

--- a/solution.py
+++ b/solution.py
@@ -757,6 +757,30 @@
     )(spots, *arrays, *w)
 
 
+def fold_cores(near, far):
+    width = near.shape[1]
+    rows = near.shape[0] // 4
+    steps = 4
+
+    def kernel(*refs):
+        for i in range(4):
+            both = refs[i][...].astype(F32) + refs[4 + i][...].astype(F32)
+            refs[8 + i][...] = both.astype(refs[8 + i].dtype)
+
+    def quarter(i):
+        return pl.BlockSpec((rows // steps, width), lambda j: (i * steps + j, 0))
+
+    return pl.pallas_call(
+        kernel,
+        grid=(steps,),
+        in_specs=[quarter(i) for i in range(4)] * 2,
+        out_specs=[pl.BlockSpec((rows // steps, width), lambda j: (j, 0))] * 4,
+        out_shape=[shape((rows, width), F32)] + [shape((rows, width), BF16)] * 3,
+        **settings(4, 32),
+        name="fold_cores",
+    )(near, near, near, near, far, far, far, far)
+
+
 def last_norm(tok, gain, dx2, *parts):
     rows, width = tok.shape
     steps = 4
@@ -1017,13 +1041,13 @@
     one, more = phase(flip(one, 1), ffn(lens_of[2], h2[2], cot[2], w_gu, w_dn))
     found.append(more)
     ab, dgu, out_near, dh2_near, out_far, dh2_far = zip(*found)
-    seven, dw_gu, side = phase(flip(dh2_far[2], 1), grad_gu(h2, dgu, share), side)
+    seven, dw_dn, side = phase(flip(dh2_far[2], 1), grad_down(ab, cot), side)
+    dw_dn = lax.psum_scatter(dw_dn, "sh", scatter_dimension=0, tiled=True)
+    low = (dh2_near[2].astype(F32) + seven.astype(F32)).astype(BF16)
+    low, dgu, out_far = phase(low, dgu, out_far)
+    own = dh2_near[1].astype(F32) + one.astype(F32)
+    six, dw_gu, out_far, own = phase(flip(low, 6), grad_gu(h2, dgu, share), [flip(x, 1) for x in out_far[1:]], own)
     dw_gu = own_share(dw_gu)
-    low = (dh2_near[2].astype(F32) + seven.astype(F32)).astype(BF16)
-    low, ab, out_far = phase(low, ab, out_far)
-    own = dh2_near[1].astype(F32) + one.astype(F32)
-    six, dw_dn, out_far, own = phase(flip(low, 6), grad_down(ab, cot), [flip(x, 1) for x in out_far[1:]], own)
-    dw_dn = lax.psum_scatter(dw_dn, "sh", scatter_dimension=0, tiled=True)
     layer_six = (out_near[2].astype(F32) + out_far[1].astype(F32)).astype(BF16)
     dh2, layer_low = phase((own, *side, six), (*layer_side, layer_six))
 
@@ -1033,24 +1057,24 @@
     dx2, dm, mix_near, mix_far = found
     mix_own, mix_low = both_cores(quarters(mix_near), quarters(flip(mix_far, 1)))
     got_dm, mix_own, mix_low, layer_low = phase(swap(dm), mix_own, mix_low, add_six(layer_low))
-    layer, mix_low, found, dw_gu = phase(
+    layer, mix_low, found, dw_dn = phase(
         (flip(layer_low[0], 2), flip(layer_low[1], 4)),
         relay_six(mix_low),
         attn_bwd(lens, spots, gain_heads, wide, backs, w_in, att, lse, got_dm, *kept),
-        dw_gu,
+        dw_dn,
     )
     dp, sums, dh1_near, dh1_far = found
 
     mix_low = add_six(mix_low)
     mix = flip(mix_low[0], 2), flip(mix_low[1], 4)
-    dh1_far, dw_in, got_gu, dw_dn = phase(
-        flip(dh1_far, 1), grad_in(place.reshape(1), sums, h1, dp, share), swap(dw_gu), dw_dn
-    )
+    dh1_far, dw_in, dw_gu = phase(flip(dh1_far, 1), grad_in(place.reshape(1), sums, h1, dp, share), dw_gu)
     dw_in = own_share(dw_in)
-    dh1_own, dh1_low = both_cores(quarters(dh1_near), quarters(dh1_far))
+    dh1_own, *dh1_low = fold_cores(dh1_near, dh1_far)
+    dh1_low, mix = phase(relay_six(dh1_low), mix)
     layer_own = out_near[1].astype(F32) + out_far[0].astype(F32)
     layer_out = (x2 + total_of((layer_own, *layer))).astype(BF16)
-    dh1, mix, dw_in, layer_out = phase(send(dh1_low), mix, dw_in, layer_out)
+    two, four = add_six(dh1_low)
+    dh1, got_gu, dw_in, layer_out = phase((flip(two, 2), flip(four, 4)), swap(dw_gu), dw_in, layer_out)
     mix = to_shares(total_of((mix_own, *mix)).astype(BF16))
     d_tokens = last_norm(tokens, gain_one, dx2, dh1_own, *dh1)
 

time: 456 us -> 445 us (0.976)
  the two profiles are of different devices: /device:TPU:26 before, /device:TPU:0 now
where the time goes in v5:
time: 445 us; the launch traced here: 436 us
  Pallas kernels  152 us (34%)
  waiting for transfers between devices  118 us (27%)
  starting transfers between devices  68 us (15%)
  local copies, waits for them, and re-layouts  43.7 us (10%)
  other arithmetic  23.1 us (5%)
  blocking collectives  16.7 us (4%)
  between operations  15.4 us (3%)
    ppermute x47, waiting for transfers between devices, flip(): return lax.ppermute(array, 'tp', [(i, i ^ offset) for i in range(TP)])  60.4 us
    all_to_all x5, waiting for transfers between devices, swap(): return lax.all_to_all(blocks, 'tp', 0, 0, tiled=True)  35.5 us
    ppermute x47, starting transfers between devices, flip(): return lax.ppermute(array, 'tp', [(i, i ^ offset) for i in range(TP)])  34.7 us
    pallas_call x3, Pallas kernels, ffn(): pl.pallas_call(ffn_kernel, grid=(buckets,), in_specs=[SMEM, block(width),...  30.2 us
    pallas_call x1, Pallas kernels, attn_fwd(): pl.pallas_call(attn_fwd_kernel, grid_spec=pltpu.PrefetchScalarGridSpec(nu...  29.6 us
    pallas_call x1, Pallas kernels, attn_bwd(): pl.pallas_call(attn_bwd_kernel, grid_spec=pltpu.PrefetchScalarGridSpec(nu...  29 us
    unnamed x151, local copies, waits for them, and re-layouts  28.7 us
    all_to_all x5, starting transfers between devices, swap(): return lax.all_to_all(blocks, 'tp', 0, 0, tiled=True)  18.1 us
  transfers between devices with their start and end apart: 63, of which 20 were waited for; matrix products, arithmetic and copies ran while one was open for 9% of the time, Pallas kernels for 35%

profile of v5, /device:TPU:0, one launch (start us, length us, event | category | flops | bytes accessed | tf_op | source)
XLA Modules:
  0.0 436.4 jit_solution(9254549032031696720)
XLA Ops:
  11.2 16.7 %all_to_all.30 = bf16[8,48,896]{2,1,0:T(8,128)(2,1)} all-to-all(bf16[8,48,896]{2,1,0:T(8,128)(2,1)S(1)} %pack_in.1), channel_id=1, replica_groups=mesh['dp'=8,'fsdp'=4] {'dp'}, dimensions={0} | all-to-all | bytes 1376256 | tf_op jit(solution)/shard_map/all_to_all | solution.py:960
  37.8 10.4 %collective-permute-done.3 = bf16[48,1536]{1,0:T(8,128)(2,1)S(1)} collective-permute-done((bf16[48,1536]{1,0:T(8,128)(2,1)S(1)}, bf16[48,1536]{1,0:T(8,128)(2,1)S(1)}, u32[]{:S(2)}, u32[]{:S(2)}) %collective-permute-start.3) | collective-permute-done | bytes 147488 | tf_op jit(solution)/shard_map/ppermute | solution.py:80
  52.0 7.1 %collective-permute-done.5.refs_3_ = bf16[128,1536]{1,0:T(8,128)(2,1)S(1)} collective-permute-done((bf16[128,1536]{1,0:T(8,128)(2,1)S(1)}, bf16[128,1536]{1,0:T(8,128)(2,1)S(1)}, u32[]{:S(2)}, u32[]{:S(2)}) %collective-permute-start.5) | collective-permute-done | bytes 393248 | tf_op jit(solution)/shard_map/ppermute | solution.py:29
  66.7 12.0 %all-to-all-done.1.got_ref = bf16[8,48,1024]{2,1,0:T(8,128)(2,1)S(1)} async-done(((bf16[8,48,1024]{2,1,0:T(8,128)(2,1)}), bf16[8,48,1024]{2,1,0:T(8,128)(2,1)S(1)}, u32[]{:S(2)}, u32[]{:S(2)}) %all-to-all-start.1) | async-done | bytes 786464 | tf_op jit(solution)/shard_map/all_to_all | solution.py:960
  85.5 4.8 %all-gather.5.cloned.1.call-done = bf16[8,192,896]{2,1,0:T(8,128)(2,1)} async-done(((bf16[8,48,896]{2,1,0:T(8,128)(2,1)}), bf16[8,192,896]{2,1,0:T(8,128)(2,1)}) %all-gather.5.cloned.1.call-update) | async-done | bytes 2752528 | tf_op jit(solution)/shard_map/all_gather | solution.py:987
  90.3 29.6 %attn_fwd.1 = (bf16[2048,1536]{1,0:T(8,128)(2,1)}, bf16[8,384,128]{2,1,0:T(8,128)(2,1)}, f32[2048,192]{1,0:T(8,128)}, f32[64,256]{1,0:T(8,128)}, f32[8,1536]{1,0...) custom-call(s32[8,4]{1,0:T(8,128)} %gather_fusion, ...), custom_call_target="tpu_custom_call" | custom-call | flops 200000000 | bytes 200000 | tf_op jit(solution)/shard_map/attn_fwd/pallas_call | solution.py:620
  128.6 13.4 %collective-permute-done.10 = bf16[96,1536]{1,0:T(8,128)(2,1)S(1)} collective-permute-done((bf16[96,1536]{1,0:T(8,128)(2,1)S(1)}, bf16[96,1536]{1,0:T(8,128)(2,1)S(1)}, u32[]{:S(2)}, u32[]{:S(2)}) %collective-permute-start.10) | collective-permute-done | bytes 294944 | tf_op jit(solution)/shard_map/ppermute | solution.py:29
  160.0 11.1 %collective-permute-done.16.refs_0_ = bf16[256,1536]{1,0:T(8,128)(2,1)S(1)} collective-permute-done((bf16[256,1536]{1,0:T(8,128)(2,1)S(1)}, bf16[256,1536]{1,0:T(8,128)(2,1)S(1)}, u32[]{:S(2)}, u32[]{:S(2)}) %collective-permute-start.16) | collective-permute-done | bytes 786464 | tf_op jit(solution)/shard_map/ppermute | solution.py:29
  188.0 15.9 %ffn.3 = (bf16[1024,512]{1,0:T(8,128)(2,1)S(1)}, bf16[1024,1024]{1,0:T(8,128)(2,1)S(1)}, bf16[512,1536]{1,0:T(8,128)(2,1)S(1)}, bf16[512,1536]{1,0:T(8,128)(2,1)...) custom-call(s32[4,4]{1,0:T(4,128)S(1)} %pad_add_fusion.lens_ref, ...), custom_call_target="tpu_custom_call" | custom-call | flops 160000000 | bytes 160000 | tf_op jit(solution)/shard_map/ffn/pallas_call | solution.py:852
  210.7 6.6 %ffn.4 = (bf16[512,512]{1,0:T(8,128)(2,1)S(1)}, bf16[512,1024]{1,0:T(8,128)(2,1)S(1)}, bf16[256,1536]{1,0:T(8,128)(2,1)S(1)}, bf16[256,1536]{1,0:T(8,128)(2,1)S(...) custom-call(s32[2,4]{1,0:T(2,128)S(1)} %get-tuple-element.443.lens_ref, ...), custom_call_target="tpu_custom_call" | custom-call | flops 80000000 | bytes 80000 | tf_op jit(solution)/shard_map/ffn/pallas_call | solution.py:852
  223.5 7.7 %ffn.5 = (bf16[512,512]{1,0:T(8,128)(2,1)S(1)}, bf16[512,1024]{1,0:T(8,128)(2,1)S(1)}, bf16[256,1536]{1,0:T(8,128)(2,1)S(1)}, bf16[256,1536]{1,0:T(8,128)(2,1)S(...) custom-call(s32[2,4]{1,0:T(2,128)S(1)} %get-tuple-element.444.lens_ref, ...), custom_call_target="tpu_custom_call" | custom-call | flops 80000000 | bytes 80000 | tf_op jit(solution)/shard_map/ffn/pallas_call | solution.py:852
  235.7 8.3 %grad_down.1 = bf16[512,1536]{1,0:T(8,128)(2,1)} custom-call(bf16[1024,512]{1,0:T(8,128)(2,1)} %copy-done.35, bf16[512,512]{1,0:T(8,128)(2,1)} %copy-done.46, bf16[512,512]{1,0:T(8,128)(2,1)} %copy-done.47, bf16[1024,1536]{1,0:T(8,128)(2,1)} %copy-done.1, bf16[512,1536]{1,0:T(8,128)(2,1)} %copy-done.7, bf16[512,1536]{1,0:T(8,128)(2,1)} %copy-done.9), custom_call_target="tpu_custom_call" | custom-call | flops 60000000 | bytes 60000 | tf_op jit(solution)/shard_map/grad_down/pallas_call | solution.py:876
  251.4 11.3 %grad_gu.1 = bf16[4,8,48,1024]{3,2,1,0:T(8,128)(2,1)} custom-call(bf16[1024,1536]{1,0:T(8,128)(2,1)} %copy-done.4, bf16[512,1536]{1,0:T(8,128)(2,1)} %copy-done.10, bf16[512,1536]{1,0:T(8,128)(2,1)} %copy-done.12, bf16[1024,1024]{1,0:T(8,128)(2,1)} %copy-done.31, bf16[512,1024]{1,0:T(8,128)(2,1)} %copy-done.36, bf16[512,1024]{1,0:T(8,128)(2,1)} %copy-done.37), custom_call_target="tpu_custom_call" | custom-call | flops 110000000 | bytes 110000 | tf_op jit(solution)/shard_map/grad_gu/pallas_call | solution.py:902
  262.8 5.2 %collective-permute-done.33.d_ref = bf16[256,1536]{1,0:T(8,128)(2,1)S(1)} collective-permute-done((bf16[256,1536]{1,0:T(8,128)(2,1)}, bf16[256,1536]{1,0:T(8,128)(2,1)S(1)}, u32[]{:S(2)}, u32[]{:S(2)}) %collective-permute-start.33) | collective-permute-done | bytes 786464 | tf_op jit(solution)/shard_map/ppermute | solution.py:29
  272.1 9.7 %mid_bwd.1 = (f32[256,1536]{1,0:T(8,128)}, bf16[8,384,128]{2,1,0:T(8,128)(2,1)}, bf16[768,1536]{1,0:T(8,128)(2,1)}, bf16[768,1536]{1,0:T(8,128)(2,1)}) custom-call(s32[8]{0:T(128)S(1)} %copy-done.52, f32[256,1536]{1,0:T(8,128)} %convert_add_fusion.a_ref, bf16[256,1536]{1,0:T(8,128)(2,1)S(1)} %collective-permute-done.31.b_ref, ...), custom_call_target="tpu_custom_call" | custom-call | flops 90000000 | bytes 90000 | tf_op jit(solution)/shard_map/mid_bwd/pallas_call | solution.py:749
  281.9 3.7 all-to-all-start.3
  290.9 7.2 %all-to-all-done.3.dm_ref = bf16[8,384,128]{2,1,0:T(8,128)(2,1)S(1)} async-done(((bf16[8,384,128]{2,1,0:T(8,128)(2,1)}), bf16[8,384,128]{2,1,0:T(8,128)(2,1)S(1)}, u32[]{:S(2)}, u32[]{:S(2)}) %all-to-all-start.3) | async-done | bytes 786464 | tf_op jit(solution)/shard_map/all_to_all | solution.py:960
  303.0 29.0 %attn_bwd.1 = (bf16[2048,896]{1,0:T(8,128)(2,1)}, f32[8,256]{1,0:T(8,128)}, bf16[1024,1536]{1,0:T(8,128)(2,1)}, bf16[1024,1536]{1,0:T(8,128)(2,1)}) custom-call(s32[8,4]{1,0:T(8,128)} %gather_fusion, s32[8]{0:T(128)} %get-tuple-element.442.spots_ref, f32[8,256]{1,0:T(8,128)} %get-tuple-element.345.gains_ref, bf16[448,192]{1,0:T(8,128)(2,1)} %constant.103.clone.wide_ref, ...), custom_call_target="tpu_custom_call" | custom-call | flops 240000000 | bytes 240000 | tf_op jit(solution)/shard_map/attn_bwd/pallas_call | solution.py:673
  332.8 11.0 %grad_in.1 = bf16[4,8,48,896]{3,2,1,0:T(8,128)(2,1)} custom-call(s32[1]{0:T(128)} %bitcast.12.place_ref, f32[8,256]{1,0:T(8,128)} %get-tuple-element.369.sums_ref, bf16[2048,1536]{1,0:T(8,128)(2,1)} %get-tuple-element.370.left_ref, bf16[2048,896]{1,0:T(8,128)(2,1)} %get-tuple-element.371.right_ref), custom_call_target="tpu_custom_call" | custom-call | flops 110000000 | bytes 110000 | tf_op jit(solution)/shard_map/grad_in/pallas_call | solution.py:937
  354.8 10.6 %collective-permute-done.46 = bf16[192,1536]{1,0:T(8,128)(2,1)S(1)} collective-permute-done((bf16[192,1536]{1,0:T(8,128)(2,1)S(1)}, bf16[192,1536]{1,0:T(8,128)(2,1)S(1)}, u32[]{:S(2)}, u32[]{:S(2)}) %collective-permute-start.46) | collective-permute-done | bytes 589856 | tf_op jit(solution)/shard_map/ppermute | solution.py:29
  367.2 5.4 %collective-permute-done.44 = bf16[128,1536]{1,0:T(8,128)(2,1)S(1)} collective-permute-done((bf16[128,1536]{1,0:T(8,128)(2,1)S(1)}, bf16[128,1536]{1,0:T(8,128)(2,1)S(1)}, u32[]{:S(2)}, u32[]{:S(2)}) %collective-permute-start.44) | collective-permute-done | bytes 393248 | tf_op jit(solution)/shard_map/ppermute | solution.py:29
  386.8 16.3 %all-to-all-done.4.got_ref = bf16[8,48,1024]{2,1,0:T(8,128)(2,1)S(1)} async-done(((bf16[8,48,1024]{2,1,0:T(8,128)(2,1)}), bf16[8,48,1024]{2,1,0:T(8,128)(2,1)S(1)}, u32[]{:S(2)}, u32[]{:S(2)}) %all-to-all-start.4) | async-done | bytes 786464 | tf_op jit(solution)/shard_map/all_to_all | solution.py:960
  408.6 7.1 %collective-permute-start.50 = (bf16[48,1536]{1,0:T(8,128)(2,1)S(1)}, bf16[48,1536]{1,0:T(8,128)(2,1)S(1)}, u32[]{:S(2)}, u32[]{:S(2)}) collective-permute-start(bf16[48,1536]{1,0:T(8,128)(2,1)S(1)} %get-tuple-element.426), channel_id=1, source_target_pairs={{0,1},{1,2},{2,3},{3,0},{4,5},{5,6},{6,7},{7,4},{8,9},{9,10},{10,1... | collective-permute-start | bytes 442376 | tf_op jit(solution)/shard_map/ppermute | solution.py:98
  419.5 4.0 last_norm.1
  (352 shorter events, 156.9 us)
Async XLA Ops:
  7.2 83.1 %all-gather.5.cloned.1.call-start = ((), (), s32[]{:S(2)}) async-start(), calls=%async_computation.12 | async-start | bytes 3440640 | tf_op jit(solution)/shard_map/all_gather | solution.py:987
  66.2 116.4 %all-gather.7.cloned.1.call-start = ((), (), s32[]{:S(2)}) async-start(), calls=%async_computation.13 | async-start | bytes 5898240 | tf_op jit(solution)/shard_map/all_gather | solution.py:999
  66.3 24.0 %collective-permute-start.7 = (bf16[1024,1536]{1,0:T(8,128)(2,1)}, bf16[1024,1536]{1,0:T(8,128)(2,1)}, u32[]{:S(2)}, u32[]{:S(2)}) collective-permute-start(bf16[1024,1536]{1,0:T(8,128)(2,1)} %join_rows.8.near_ref), channel_id=1, source_target_pairs={{0,4},{4,0},{8,12},{12,8},{16,20},{20,16},{24,28},{28,24},{1,5},{5... | collective-permute-start | bytes 9437192 | tf_op jit(solution)/shard_map/ppermute | solution.py:29
  81.1 38.9 %collective-permute-start.8 = (bf16[448,1536]{1,0:T(8,128)(2,1)S(1)}, bf16[448,1536]{1,0:T(8,128)(2,1)S(1)}, u32[]{:S(2)}, u32[]{:S(2)}) collective-permute-start(bf16[448,1536]{1,0:T(8,128)(2,1)S(1)} %join_rows.9.refs_0_), channel_id=1, source_target_pairs={{0,8},{4,12},{8,0},{12,4},{16,24},{20,28},{24,16},{28,20},{1,9},{5... | collective-permute-start | bytes 4128776 | tf_op jit(solution)/shard_map/ppermute | solution.py:29
  81.6 38.3 %collective-permute-start.9 = (bf16[448,1536]{1,0:T(8,128)(2,1)S(1)}, bf16[448,1536]{1,0:T(8,128)(2,1)}, u32[]{:S(2)}, u32[]{:S(2)}) collective-permute-start(bf16[448,1536]{1,0:T(8,128)(2,1)S(1)} %join_rows.9.refs_0_), channel_id=1, source_target_pairs={{0,16},{4,20},{8,24},{12,28},{16,0},{20,4},{24,8},{28,12},{1,17},{... | collective-permute-start | bytes 4128776 | tf_op jit(solution)/shard_map/ppermute | solution.py:29
  85.5 43.1 %collective-permute-start.12 = (bf16[448,1536]{1,0:T(8,128)(2,1)S(1)}, bf16[448,1536]{1,0:T(8,128)(2,1)}, u32[]{:S(2)}, u32[]{:S(2)}) collective-permute-start(bf16[448,1536]{1,0:T(8,128)(2,1)S(1)} %join_rows.9.refs_0_), channel_id=1, source_target_pairs={{0,4},{4,0},{8,12},{12,8},{16,20},{20,16},{24,28},{28,24},{1,5},{5... | collective-permute-start | bytes 4128776 | tf_op jit(solution)/shard_map/ppermute | solution.py:29
  120.0 22.8 %collective-permute-start.13 = (bf16[448,1536]{1,0:T(8,128)(2,1)S(1)}, bf16[448,1536]{1,0:T(8,128)(2,1)}, u32[]{:S(2)}, u32[]{:S(2)}) collective-permute-start(bf16[448,1536]{1,0:T(8,128)(2,1)S(1)} %collective-permute-done.8.refs_1_.refs_0_), channel_id=1, source_target_pairs={{0,4},{4,0},{8,12},{12,8},{16,20},{20,16},{24,28},{28,24},{1,5},{5... | collective-permute-start | bytes 4128776 | tf_op jit(solution)/shard_map/ppermute | solution.py:29
  120.1 22.7 %collective-permute-start.14 = (bf16[448,1536]{1,0:T(8,128)(2,1)}, bf16[448,1536]{1,0:T(8,128)(2,1)}, u32[]{:S(2)}, u32[]{:S(2)}) collective-permute-start(bf16[448,1536]{1,0:T(8,128)(2,1)} %collective-permute-done.9.refs_2_.refs_1_), channel_id=1, source_target_pairs={{0,4},{4,0},{8,12},{12,8},{16,20},{20,16},{24,28},{28,24},{1,5},{5... | collective-permute-start | bytes 4128776 | tf_op jit(solution)/shard_map/ppermute | solution.py:29
  120.5 22.2 %all-to-all-start.2 = ((bf16[8,384,128]{2,1,0:T(8,128)(2,1)}), bf16[8,384,128]{2,1,0:T(8,128)(2,1)S(1)}, u32[]{:S(2)}, u32[]{:S(2)}) async-start(bf16[8,384,128]{2,1,0:T(8,128)(2,1)} %get-tuple-element.227), calls=%async_computation.2 | async-start | bytes 1572864 | tf_op jit(solution)/shard_map/all_to_all | solution.py:960
  124.1 208.0 %reduce-scatter.4.cloned.1.call-start = ((), (), s32[]{:S(2)}) async-start(), calls=%async_computation.9 | async-start | bytes 1966080 | tf_op jit(solution)/shard_map/reduce_scatter | solution.py:1045
  175.4 28.5 %collective-permute-start.23 = (bf16[128,1536]{1,0:T(8,128)(2,1)}, bf16[128,1536]{1,0:T(8,128)(2,1)}, u32[]{:S(2)}, u32[]{:S(2)}) collective-permute-start(bf16[128,1536]{1,0:T(8,128)(2,1)} %slice.190), channel_id=1, source_target_pairs={{0,16},{4,20},{8,24},{12,28},{16,0},{20,4},{24,8},{28,12},{1,17},{... | collective-permute-start | bytes 1179656 | tf_op jit(solution)/shard_map/ppermute | solution.py:29
  175.7 28.2 %collective-permute-start.24 = (bf16[128,1536]{1,0:T(8,128)(2,1)}, bf16[128,1536]{1,0:T(8,128)(2,1)}, u32[]{:S(2)}, u32[]{:S(2)}) collective-permute-start(bf16[128,1536]{1,0:T(8,128)(2,1)} %slice.191), channel_id=1, source_target_pairs={{0,8},{4,12},{8,0},{12,4},{16,24},{20,28},{24,16},{28,20},{1,9},{5... | collective-permute-start | bytes 1179656 | tf_op jit(solution)/shard_map/ppermute | solution.py:29
  178.4 25.5 %collective-permute-start.21 = (bf16[128,1536]{1,0:T(8,128)(2,1)}, bf16[128,1536]{1,0:T(8,128)(2,1)}, u32[]{:S(2)}, u32[]{:S(2)}) collective-permute-start(bf16[128,1536]{1,0:T(8,128)(2,1)} %slice.188), channel_id=1, source_target_pairs={{0,16},{4,20},{8,24},{12,28},{16,0},{20,4},{24,8},{28,12},{1,17},{... | collective-permute-start | bytes 1179656 | tf_op jit(solution)/shard_map/ppermute | solution.py:29
  179.5 24.5 %collective-permute-start.22 = (bf16[128,1536]{1,0:T(8,128)(2,1)}, bf16[128,1536]{1,0:T(8,128)(2,1)}, u32[]{:S(2)}, u32[]{:S(2)}) collective-permute-start(bf16[128,1536]{1,0:T(8,128)(2,1)} %slice.189), channel_id=1, source_target_pairs={{0,8},{4,12},{8,0},{12,4},{16,24},{20,28},{24,16},{28,20},{1,9},{5... | collective-permute-start | bytes 1179656 | tf_op jit(solution)/shard_map/ppermute | solution.py:29
  222.1 22.0 %collective-permute-start.31 = (bf16[256,1536]{1,0:T(8,128)(2,1)S(1)}, bf16[256,1536]{1,0:T(8,128)(2,1)S(1)}, u32[]{:S(2)}, u32[]{:S(2)}) collective-permute-start(bf16[256,1536]{1,0:T(8,128)(2,1)S(1)} %get-tuple-element.297), channel_id=1, source_target_pairs={{0,8},{4,12},{8,0},{12,4},{16,24},{20,28},{24,16},{28,20},{1,9},{5... | collective-permute-start | bytes 2359304 | tf_op jit(solution)/shard_map/ppermute | solution.py:29
  244.1 102.7 %reduce-scatter.6.cloned.1.call-start = ((), (), s32[]{:S(2)}) async-start(), calls=%async_computation.10 | async-start | bytes 3932160 | tf_op jit(solution)/shard_map/reduce_scatter | solution.py:955
  285.6 117.7 %reduce-scatter.8.cloned.1.call-start = ((), (), s32[]{:S(2)}) async-start(), calls=%async_computation.11 | async-start | bytes 3440640 | tf_op jit(solution)/shard_map/reduce_scatter | solution.py:955
  298.1 34.0 %collective-permute-start.39 = (bf16[256,1536]{1,0:T(8,128)(2,1)S(1)}, bf16[256,1536]{1,0:T(8,128)(2,1)}, u32[]{:S(2)}, u32[]{:S(2)}) collective-permute-start(bf16[256,1536]{1,0:T(8,128)(2,1)S(1)} %pad_maximum_fusion), channel_id=1, source_target_pairs={{0,8},{4,12},{8,0},{12,4},{16,24},{20,28},{24,16},{28,20},{1,9},{5... | collective-permute-start | bytes 2359304 | tf_op jit(solution)/shard_map/ppermute | solution.py:29
  298.6 33.5 %collective-permute-start.40 = (bf16[256,1536]{1,0:T(8,128)(2,1)S(1)}, bf16[256,1536]{1,0:T(8,128)(2,1)}, u32[]{:S(2)}, u32[]{:S(2)}) collective-permute-start(bf16[256,1536]{1,0:T(8,128)(2,1)S(1)} %pad_maximum_fusion.1), channel_id=1, source_target_pairs={{0,16},{4,20},{8,24},{12,28},{16,0},{20,4},{24,8},{28,12},{1,17},{... | collective-permute-start | bytes 2359304 | tf_op jit(solution)/shard_map/ppermute | solution.py:29
  300.1 32.0 %collective-permute-start.41 = (bf16[96,1536]{1,0:T(8,128)(2,1)}, bf16[96,1536]{1,0:T(8,128)(2,1)S(1)}, u32[]{:S(2)}, u32[]{:S(2)}) collective-permute-start(bf16[96,1536]{1,0:T(8,128)(2,1)} %get-tuple-element.429), channel_id=1, source_target_pairs={{0,8},{4,12},{8,0},{12,4},{16,24},{20,28},{24,16},{28,20},{1,9},{5... | collective-permute-start | bytes 884744 | tf_op jit(solution)/shard_map/ppermute | solution.py:29
  301.5 30.6 %collective-permute-start.42 = (bf16[96,1536]{1,0:T(8,128)(2,1)}, bf16[96,1536]{1,0:T(8,128)(2,1)S(1)}, u32[]{:S(2)}, u32[]{:S(2)}) collective-permute-start(bf16[96,1536]{1,0:T(8,128)(2,1)} %get-tuple-element.428), channel_id=1, source_target_pairs={{0,16},{4,20},{8,24},{12,28},{16,0},{20,4},{24,8},{28,12},{1,17},{... | collective-permute-start | bytes 884744 | tf_op jit(solution)/shard_map/ppermute | solution.py:29
  375.1 28.0 %collective-permute-start.48 = (bf16[256,1536]{1,0:T(8,128)(2,1)}, bf16[256,1536]{1,0:T(8,128)(2,1)S(1)}, u32[]{:S(2)}, u32[]{:S(2)}) collective-permute-start(bf16[256,1536]{1,0:T(8,128)(2,1)} %pad_maximum_fusion.2), channel_id=1, source_target_pairs={{0,8},{4,12},{8,0},{12,4},{16,24},{20,28},{24,16},{28,20},{1,9},{5... | collective-permute-start | bytes 2359304 | tf_op jit(solution)/shard_map/ppermute | solution.py:29
  376.7 26.4 %collective-permute-start.49 = (bf16[256,1536]{1,0:T(8,128)(2,1)}, bf16[256,1536]{1,0:T(8,128)(2,1)}, u32[]{:S(2)}, u32[]{:S(2)}) collective-permute-start(bf16[256,1536]{1,0:T(8,128)(2,1)} %pad_maximum_fusion.3), channel_id=1, source_target_pairs={{0,16},{4,20},{8,24},{12,28},{16,0},{20,4},{24,8},{28,12},{1,17},{... | collective-permute-start | bytes 2359304 | tf_op jit(solution)/shard_map/ppermute | solution.py:29
  378.2 24.9 %all-to-all-start.4 = ((bf16[8,48,1024]{2,1,0:T(8,128)(2,1)}), bf16[8,48,1024]{2,1,0:T(8,128)(2,1)S(1)}, u32[]{:S(2)}, u32[]{:S(2)}) async-start(bf16[8,48,1024]{2,1,0:T(8,128)(2,1)} %bitcast.47), calls=%async_computation.6 | async-start | bytes 1572864 | tf_op jit(solution)/shard_map/all_to_all | solution.py:960
  (113 other events, 1176.3 us)
Sparse Core Ops, SparseCore 0:
  28.0 62.2 all-gather.4
  92.5 88.5 all-gather.6
  244.2 40.9 reduce-scatter.3
  287.3 59.4 reduce-scatter.5
  349.0 54.1 reduce-scatter.7

commit v6 on v5

--- a/solution.py
+++ b/solution.py
@@ -236,25 +236,33 @@
     )(joined)
 
 
-def join_rows(*pieces):
-    pieces = [x if isinstance(x, tuple) else (x, 0) for x in pieces]
-    total = sum(x.shape[0] - first for x, first in pieces)
+def join_lists(*lists):
+    lists = [[x if isinstance(x, tuple) else (x, 0) for x in pieces] for pieces in lists]
+    arrays = [x for pieces in lists for x, _ in pieces]
 
     def kernel(*refs):
         at = 0
-        for ref, (x, first) in zip(refs, pieces):
-            more = x.shape[0] - first
-            refs[-1][at : at + more, :] = ref[first:, :]
-            at += more
-
+        for pieces, out_ref in zip(lists, refs[len(arrays) :]):
+            to = 0
+            for (x, first), ref in zip(pieces, refs[at : at + len(pieces)]):
+                more = x.shape[0] - first
+                out_ref[to : to + more, :] = ref[first:, :]
+                to += more
+            at += len(pieces)
+
+    totals = [(sum(x.shape[0] - first for x, first in pieces), pieces[0][0].shape[1]) for pieces in lists]
     return pl.pallas_call(
         kernel,
-        in_specs=[VMEM] * len(pieces),
-        out_specs=VMEM,
-        out_shape=shape((total, pieces[0][0].shape[1]), pieces[0][0].dtype),
+        in_specs=[VMEM] * len(arrays),
+        out_specs=[VMEM] * len(lists),
+        out_shape=[shape(x, BF16) for x in totals],
         **settings(2, 24),
         name="join_rows",
-    )(*[x for x, _ in pieces])
+    )(*arrays)
+
+
+def join_rows(*pieces):
+    return join_lists(pieces)[0]
 
 
 def unpack_in_kernel(got_ref, w_ref, rates_ref, gain_ref, dw_ref, drates_ref, small_ref):
@@ -855,7 +863,7 @@
         in_specs=[SMEM, block(width), block(width), whole(gu.shape), whole(dn.shape)],
         out_specs=[block(ff), block(2 * ff), near, near, far, far],
         out_shape=[shape((total, ff), BF16), shape((total, 2 * ff), BF16)] + [shape((total // 2, width), BF16)] * 4,
-        **settings(4 * buckets, 40),
+        **settings(4 * buckets, 34),
         name="ffn",
     )(lens, h2, cot, gu, dn)
 
@@ -880,7 +888,7 @@
         + [pl.BlockSpec((x.shape[0], columns), lambda i: (0, i)) for x in cot],
         out_specs=pl.BlockSpec((ff, columns), lambda i: (0, i)),
         out_shape=shape((ff, width), BF16),
-        **settings(6, 60),
+        **settings(6, 24),
         name="grad_down",
     )(*ab, *cot)
 
@@ -906,7 +914,7 @@
         + [pl.BlockSpec(x.shape, lambda i: (0, 0)) for x in dgu],
         out_specs=pl.BlockSpec((share, 2, own_rows, columns), lambda i: (0, i, 0, 0)),
         out_shape=shape((share, TP, own_rows, columns), BF16),
-        **settings(11, 60),
+        **settings(11, 36),
         name="grad_gu",
     )(*h2, *dgu)
 
@@ -1025,7 +1033,7 @@
     h2 = [join_rows(two, four, three, five), join_rows(h2, one)]
     found = [ffn(lens_of[0], h2[0], cot[0], w_gu, w_dn)]
     found, six, h2[1], cot_six = phase(found, six, h2[1], diagonal(*[x[BLOCK:] for x in near[1:3]]))
-    six, cot_six = [jnp.concatenate(x, axis=0) for x in (six, cot_six)]
+    six, cot_six = join_lists(six, cot_six)
     seven, cot_seven, far, more = phase(
         flip(six, 1),
         flip(cot_six, 1),
@@ -1033,10 +1041,10 @@
         ffn(lens_of[1], h2[1], cot[1], w_gu, w_dn),
     )
     found.append(more)
-    layer_side, side = [[x.astype(BF16) for x in two_sums(*pair)] for pair in zip(found[0][2:4], far)]
+    side = [x.astype(BF16) for x in two_sums(found[0][3], far[1])]
     h2.append(join_rows(six, seven))
     cot.append(join_rows(cot_six, cot_seven))
-    side, layer_side, h2[2], cot[2], one = phase(side, layer_side, h2[2], cot[2], found[1][5])
+    side, h2[2], cot[2], one = phase(side, h2[2], cot[2], found[1][5])
     side = flip(side[0], 2), flip(side[1], 4)
     one, more = phase(flip(one, 1), ffn(lens_of[2], h2[2], cot[2], w_gu, w_dn))
     found.append(more)
@@ -1044,10 +1052,11 @@
     seven, dw_dn, side = phase(flip(dh2_far[2], 1), grad_down(ab, cot), side)
     dw_dn = lax.psum_scatter(dw_dn, "sh", scatter_dimension=0, tiled=True)
     low = (dh2_near[2].astype(F32) + seven.astype(F32)).astype(BF16)
-    low, dgu, out_far = phase(low, dgu, out_far)
+    low, dgu, out_far, far = phase(low, dgu, out_far, far)
     own = dh2_near[1].astype(F32) + one.astype(F32)
     six, dw_gu, out_far, own = phase(flip(low, 6), grad_gu(h2, dgu, share), [flip(x, 1) for x in out_far[1:]], own)
     dw_gu = own_share(dw_gu)
+    layer_side = [x.astype(BF16) for x in two_sums(out_near[0], far[0])]
     layer_six = (out_near[2].astype(F32) + out_far[1].astype(F32)).astype(BF16)
     dh2, layer_low = phase((own, *side, six), (*layer_side, layer_six))
 
@@ -1074,8 +1083,11 @@
     layer_own = out_near[1].astype(F32) + out_far[0].astype(F32)
     layer_out = (x2 + total_of((layer_own, *layer))).astype(BF16)
     two, four = add_six(dh1_low)
-    dh1, got_gu, dw_in, layer_out = phase((flip(two, 2), flip(four, 4)), swap(dw_gu), dw_in, layer_out)
-    mix = to_shares(total_of((mix_own, *mix)).astype(BF16))
+    mix = total_of((mix_own, *mix)).astype(BF16)
+    dh1, got_gu, dw_in, layer_out, mix = phase(
+        (flip(two, 2), flip(four, 4)), swap(dw_gu), dw_in, layer_out, mix
+    )
+    mix = to_shares(mix)
     d_tokens = last_norm(tokens, gain_one, dx2, dh1_own, *dh1)
 
     d_w_attn_in, d_w_rates, small = unpack_in(swap(dw_in), w_attn_in, w_rates, norm_gain)

time: 445 us -> 438 us (0.984)
  the two profiles are of different devices: /device:TPU:0 before, /device:TPU:11 now
where the time goes in v6:
time: 438 us; the launch traced here: 429 us
  Pallas kernels  144 us (33%)
  waiting for transfers between devices  111 us (25%)
  starting transfers between devices  66.7 us (15%)
  local copies, waits for them, and re-layouts  50.9 us (12%)
  other arithmetic  27.4 us (6%)
  between operations  15.3 us (3%)
  blocking collectives  14.4 us (3%)
    ppermute x47, waiting for transfers between devices, flip(): return lax.ppermute(array, 'tp', [(i, i ^ offset) for i in range(TP)])  64.9 us
    unnamed x181, local copies, waits for them, and re-layouts  36 us
    ppermute x47, starting transfers between devices, flip(): return lax.ppermute(array, 'tp', [(i, i ^ offset) for i in range(TP)])  34.8 us
    pallas_call x1, Pallas kernels, attn_fwd(): pl.pallas_call(attn_fwd_kernel, grid_spec=pltpu.PrefetchScalarGridSpec(nu...  30.1 us
    pallas_call x1, Pallas kernels, attn_bwd(): pl.pallas_call(attn_bwd_kernel, grid_spec=pltpu.PrefetchScalarGridSpec(nu...  29 us
    pallas_call x3, Pallas kernels, ffn(): pl.pallas_call(ffn_kernel, grid=(buckets,), in_specs=[SMEM, block(width),...  26.7 us
    ppermute x3, waiting for transfers between devices, gather_shares(): lax.ppermute(own, 'sh', [(i, (i + k) % share) for i in range(share)])  26.6 us
    all_to_all x5, starting transfers between devices, swap(): return lax.all_to_all(blocks, 'tp', 0, 0, tiled=True)  26.6 us
  transfers between devices with their start and end apart: 63, of which 18 were waited for; matrix products, arithmetic and copies ran while one was open for 9% of the time, Pallas kernels for 33%

profile of v6, /device:TPU:11, one launch (start us, length us, event | category | flops | bytes accessed | tf_op | source)
XLA Modules:
  0.0 429.2 jit_solution(4986653510780926796)
XLA Ops:
  11.2 14.4 %all_to_all.30 = bf16[8,48,896]{2,1,0:T(8,128)(2,1)} all-to-all(bf16[8,48,896]{2,1,0:T(8,128)(2,1)S(1)} %pack_in.1), channel_id=1, replica_groups=mesh['dp'=8,'fsdp'=4] {'dp'}, dimensions={0} | all-to-all | bytes 1376256 | tf_op jit(solution)/shard_map/all_to_all | solution.py:968
  31.2 9.6 %collective-permute-done.3 = bf16[48,1536]{1,0:T(8,128)(2,1)S(1)} collective-permute-done((bf16[48,1536]{1,0:T(8,128)(2,1)S(1)}, bf16[48,1536]{1,0:T(8,128)(2,1)S(1)}, u32[]{:S(2)}, u32[]{:S(2)}) %collective-permute-start.3) | collective-permute-done | bytes 147488 | tf_op jit(solution)/shard_map/ppermute | solution.py:80
  40.7 16.5 %collective-permute-done.4 = bf16[48,1536]{1,0:T(8,128)(2,1)S(1)} collective-permute-done((bf16[48,1536]{1,0:T(8,128)(2,1)S(1)}, bf16[48,1536]{1,0:T(8,128)(2,1)S(1)}, u32[]{:S(2)}, u32[]{:S(2)}) %collective-permute-start.4) | collective-permute-done | bytes 147488 | tf_op jit(solution)/shard_map/ppermute | solution.py:80
  60.4 7.2 %collective-permute-done.5.refs_3_ = bf16[128,1536]{1,0:T(8,128)(2,1)S(1)} collective-permute-done((bf16[128,1536]{1,0:T(8,128)(2,1)S(1)}, bf16[128,1536]{1,0:T(8,128)(2,1)S(1)}, u32[]{:S(2)}, u32[]{:S(2)}) %collective-permute-start.5) | collective-permute-done | bytes 393248 | tf_op jit(solution)/shard_map/ppermute | solution.py:29
  70.3 6.0 %all-to-all-start.1 = ((bf16[8,48,1024]{2,1,0:T(8,128)(2,1)}), bf16[8,48,1024]{2,1,0:T(8,128)(2,1)S(1)}, u32[]{:S(2)}, u32[]{:S(2)}) async-start(bf16[8,48,1024]{2,1,0:T(8,128)(2,1)} %pack_gu.1), calls=%async_computation.1 | async-start | bytes 1572864 | tf_op jit(solution)/shard_map/all_to_all | solution.py:968
  76.7 10.6 %all-to-all-done.1.got_ref = bf16[8,48,1024]{2,1,0:T(8,128)(2,1)S(1)} async-done(((bf16[8,48,1024]{2,1,0:T(8,128)(2,1)}), bf16[8,48,1024]{2,1,0:T(8,128)(2,1)S(1)}, u32[]{:S(2)}, u32[]{:S(2)}) %all-to-all-start.1) | async-done | bytes 786464 | tf_op jit(solution)/shard_map/all_to_all | solution.py:968
  95.5 30.1 %attn_fwd.1 = (bf16[2048,1536]{1,0:T(8,128)(2,1)}, bf16[8,384,128]{2,1,0:T(8,128)(2,1)}, f32[2048,192]{1,0:T(8,128)}, f32[64,256]{1,0:T(8,128)}, f32[8,1536]{1,0...) custom-call(s32[8,4]{1,0:T(8,128)} %gather_fusion, ...), custom_call_target="tpu_custom_call" | custom-call | flops 200000000 | bytes 200000 | tf_op jit(solution)/shard_map/attn_fwd/pallas_call | solution.py:628
  126.2 4.0 all-to-all-start.2
  132.7 14.9 %collective-permute-done.10 = bf16[96,1536]{1,0:T(8,128)(2,1)S(1)} collective-permute-done((bf16[96,1536]{1,0:T(8,128)(2,1)S(1)}, bf16[96,1536]{1,0:T(8,128)(2,1)S(1)}, u32[]{:S(2)}, u32[]{:S(2)}) %collective-permute-start.10) | collective-permute-done | bytes 294944 | tf_op jit(solution)/shard_map/ppermute | solution.py:29
  164.0 12.1 %collective-permute-done.16.refs_0_ = bf16[256,1536]{1,0:T(8,128)(2,1)S(1)} collective-permute-done((bf16[256,1536]{1,0:T(8,128)(2,1)S(1)}, bf16[256,1536]{1,0:T(8,128)(2,1)S(1)}, u32[]{:S(2)}, u32[]{:S(2)}) %collective-permute-start.16) | collective-permute-done | bytes 786464 | tf_op jit(solution)/shard_map/ppermute | solution.py:29
  192.3 12.7 %ffn.3 = (bf16[1024,512]{1,0:T(8,128)(2,1)S(1)}, bf16[1024,1024]{1,0:T(8,128)(2,1)S(1)}, bf16[512,1536]{1,0:T(8,128)(2,1)S(1)}, bf16[512,1536]{1,0:T(8,128)(2,1)...) custom-call(s32[4,4]{1,0:T(4,128)S(1)} %copy-done.62, bf16[1024,1536]{1,0:T(8,128)(2,1)S(1)} %copy-done.2, ...), custom_call_target="tpu_custom_call" | custom-call | flops 160000000 | bytes 160000 | tf_op jit(solution)/shard_map/ffn/pallas_call | solution.py:860
  211.2 6.6 %ffn.4 = (bf16[512,512]{1,0:T(8,128)(2,1)S(1)}, bf16[512,1024]{1,0:T(8,128)(2,1)S(1)}, bf16[256,1536]{1,0:T(8,128)(2,1)S(1)}, bf16[256,1536]{1,0:T(8,128)(2,1)S(...) custom-call(s32[2,4]{1,0:T(2,128)S(1)} %get-tuple-element.447.lens_ref, ...), custom_call_target="tpu_custom_call" | custom-call | flops 80000000 | bytes 80000 | tf_op jit(solution)/shard_map/ffn/pallas_call | solution.py:860
  223.6 7.4 %ffn.5 = (bf16[512,512]{1,0:T(8,128)(2,1)S(1)}, bf16[512,1024]{1,0:T(8,128)(2,1)S(1)}, bf16[256,1536]{1,0:T(8,128)(2,1)S(1)}, bf16[256,1536]{1,0:T(8,128)(2,1)S(...) custom-call(s32[2,4]{1,0:T(2,128)S(1)} %get-tuple-element.448.lens_ref, ...), custom_call_target="tpu_custom_call" | custom-call | flops 80000000 | bytes 80000 | tf_op jit(solution)/shard_map/ffn/pallas_call | solution.py:860
  236.2 5.9 %grad_down.1 = bf16[512,1536]{1,0:T(8,128)(2,1)S(1)} custom-call(bf16[1024,512]{1,0:T(8,128)(2,1)S(1)} %get-tuple-element.296.refs_0_, bf16[512,512]{1,0:T(8,128)(2,1)S(1)} %get-tuple-element.297.refs_1_, bf16[512,512]{1,0:T(8,128)(2,1)S(1)} %get-tuple-element.298.refs_2_, bf16[1024,1536]{1,0:T(8,128)(2,1)S(1)} %join_rows.11.cot_ref.refs_3_, ...), custom_call_target="tpu_custom_call" | custom-call | flops 60000000 | bytes 60000 | tf_op jit(solution)/shard_map/grad_down/pallas_call | solution.py:884
  253.7 9.1 %grad_gu.1 = bf16[4,8,48,1024]{3,2,1,0:T(8,128)(2,1)} custom-call(bf16[1024,1536]{1,0:T(8,128)(2,1)S(1)} %copy-done.3, bf16[512,1536]{1,0:T(8,128)(2,1)S(1)} %copy-done.11, bf16[512,1536]{1,0:T(8,128)(2,1)S(1)} %copy-done.13, bf16[1024,1024]{1,0:T(8,128)(2,1)S(1)} %copy-done.34, bf16[512,1024]{1,0:T(8,128)(2,1)S(1)} %copy-done.41, ...), custom_call_target="tpu_custom_call" | custom-call | flops 110000000 | bytes 110000 | tf_op jit(solution)/shard_map/grad_gu/pallas_call | solution.py:910
  267.8 9.9 %mid_bwd.1 = (f32[256,1536]{1,0:T(8,128)}, bf16[8,384,128]{2,1,0:T(8,128)(2,1)}, bf16[768,1536]{1,0:T(8,128)(2,1)}, bf16[768,1536]{1,0:T(8,128)(2,1)}) custom-call(s32[8]{0:T(128)S(1)} %copy-done.61, f32[256,1536]{1,0:T(8,128)} %convert_add_fusion.a_ref, bf16[256,1536]{1,0:T(8,128)(2,1)} %collective-permute-done.31.b_ref, ...), custom_call_target="tpu_custom_call" | custom-call | flops 90000000 | bytes 90000 | tf_op jit(solution)/shard_map/mid_bwd/pallas_call | solution.py:757
  279.3 5.2 %all-to-all-start.3 = ((bf16[8,384,128]{2,1,0:T(8,128)(2,1)}), bf16[8,384,128]{2,1,0:T(8,128)(2,1)S(1)}, u32[]{:S(2)}, u32[]{:S(2)}) async-start(bf16[8,384,128]{2,1,0:T(8,128)(2,1)} %get-tuple-element.336), calls=%async_computation.3 | async-start | bytes 1572864 | tf_op jit(solution)/shard_map/all_to_all | solution.py:968
  291.6 4.0 all-to-all-done.3.dm_ref
  299.4 29.0 %attn_bwd.1 = (bf16[2048,896]{1,0:T(8,128)(2,1)}, f32[8,256]{1,0:T(8,128)}, bf16[1024,1536]{1,0:T(8,128)(2,1)}, bf16[1024,1536]{1,0:T(8,128)(2,1)}) custom-call(s32[8,4]{1,0:T(8,128)} %gather_fusion, s32[8]{0:T(128)} %get-tuple-element.446.spots_ref, f32[8,256]{1,0:T(8,128)} %get-tuple-element.348.gains_ref, bf16[448,192]{1,0:T(8,128)(2,1)} %constant.103.clone.wide_ref, ...), custom_call_target="tpu_custom_call" | custom-call | flops 240000000 | bytes 240000 | tf_op jit(solution)/shard_map/attn_bwd/pallas_call | solution.py:681
  330.7 11.0 %grad_in.1 = bf16[4,8,48,896]{3,2,1,0:T(8,128)(2,1)} custom-call(s32[1]{0:T(128)} %bitcast.12.place_ref, f32[8,256]{1,0:T(8,128)} %get-tuple-element.372.sums_ref, bf16[2048,1536]{1,0:T(8,128)(2,1)} %get-tuple-element.373.left_ref, bf16[2048,896]{1,0:T(8,128)(2,1)} %get-tuple-element.374.right_ref), custom_call_target="tpu_custom_call" | custom-call | flops 110000000 | bytes 110000 | tf_op jit(solution)/shard_map/grad_in/pallas_call | solution.py:945
  351.8 5.7 %all-to-all-start.4 = ((bf16[8,48,1024]{2,1,0:T(8,128)(2,1)}), bf16[8,48,1024]{2,1,0:T(8,128)(2,1)S(1)}, u32[]{:S(2)}, u32[]{:S(2)}) async-start(bf16[8,48,1024]{2,1,0:T(8,128)(2,1)} %bitcast.14), calls=%async_computation.6 | async-start | bytes 1572864 | tf_op jit(solution)/shard_map/all_to_all | solution.py:968
  361.0 8.4 %collective-permute-done.44 = bf16[128,1536]{1,0:T(8,128)(2,1)S(1)} collective-permute-done((bf16[128,1536]{1,0:T(8,128)(2,1)S(1)}, bf16[128,1536]{1,0:T(8,128)(2,1)S(1)}, u32[]{:S(2)}, u32[]{:S(2)}) %collective-permute-start.44) | collective-permute-done | bytes 393248 | tf_op jit(solution)/shard_map/ppermute | solution.py:29
  379.1 14.7 %collective-permute-done.49.refs_2_ = bf16[256,1536]{1,0:T(8,128)(2,1)S(1)} collective-permute-done((bf16[256,1536]{1,0:T(8,128)(2,1)}, bf16[256,1536]{1,0:T(8,128)(2,1)S(1)}, u32[]{:S(2)}, u32[]{:S(2)}) %collective-permute-start.49) | collective-permute-done | bytes 786464 | tf_op jit(solution)/shard_map/ppermute | solution.py:29
  395.5 5.7 %all-to-all-start.5 = ((bf16[8,48,896]{2,1,0:T(8,128)(2,1)}), bf16[8,48,896]{2,1,0:T(8,128)(2,1)S(1)}, u32[]{:S(2)}, u32[]{:S(2)}) async-start(bf16[8,48,896]{2,1,0:T(8,128)(2,1)} %bitcast.46), calls=%async_computation.8 | async-start | bytes 1376256 | tf_op jit(solution)/shard_map/all_to_all | solution.py:968
  (381 shorter events, 153.4 us)
Async XLA Ops:
  7.2 88.3 %all-gather.5.cloned.1.call-start = ((), (), s32[]{:S(2)}) async-start(), calls=%async_computation.12 | async-start | bytes 3440640 | tf_op jit(solution)/shard_map/all_gather | solution.py:995
  25.6 31.6 %collective-permute-start = (bf16[256,1536]{1,0:T(8,128)(2,1)S(1)}, bf16[256,1536]{1,0:T(8,128)(2,1)S(1)}, u32[]{:S(2)}, u32[]{:S(2)}) collective-permute-start(bf16[256,1536]{1,0:T(8,128)(2,1)S(1)} %copy-done.16), channel_id=1, source_target_pairs={{0,8},{4,12},{8,0},{12,4},{16,24},{20,28},{24,16},{28,20},{1,9},{5... | collective-permute-start | bytes 2359304 | tf_op jit(solution)/shard_map/ppermute | solution.py:29
  26.6 30.7 %collective-permute-start.1 = (bf16[256,1536]{1,0:T(8,128)(2,1)S(1)}, bf16[256,1536]{1,0:T(8,128)(2,1)S(1)}, u32[]{:S(2)}, u32[]{:S(2)}) collective-permute-start(bf16[256,1536]{1,0:T(8,128)(2,1)S(1)} %copy-done.16), channel_id=1, source_target_pairs={{0,16},{4,20},{8,24},{12,28},{16,0},{20,4},{24,8},{28,12},{1,17},{... | collective-permute-start | bytes 2359304 | tf_op jit(solution)/shard_map/ppermute | solution.py:29
  29.2 28.1 %collective-permute-start.4 = (bf16[48,1536]{1,0:T(8,128)(2,1)S(1)}, bf16[48,1536]{1,0:T(8,128)(2,1)S(1)}, u32[]{:S(2)}, u32[]{:S(2)}) collective-permute-start(bf16[48,1536]{1,0:T(8,128)(2,1)S(1)} %copy-done.83), channel_id=1, source_target_pairs={{0,3},{1,0},{2,1},{3,2},{4,7},{5,4},{6,5},{7,6},{8,11},{9,8},{10,9... | collective-permute-start | bytes 442376 | tf_op jit(solution)/shard_map/ppermute | solution.py:80
  76.3 111.8 %all-gather.7.cloned.1.call-start = ((), (), s32[]{:S(2)}) async-start(), calls=%async_computation.13 | async-start | bytes 5898240 | tf_op jit(solution)/shard_map/all_gather | solution.py:1007
  89.6 35.9 %collective-permute-start.8 = (bf16[448,1536]{1,0:T(8,128)(2,1)S(1)}, bf16[448,1536]{1,0:T(8,128)(2,1)S(1)}, u32[]{:S(2)}, u32[]{:S(2)}) collective-permute-start(bf16[448,1536]{1,0:T(8,128)(2,1)S(1)} %join_rows.10.refs_0_), channel_id=1, source_target_pairs={{0,8},{4,12},{8,0},{12,4},{16,24},{20,28},{24,16},{28,20},{1,9},{5... | collective-permute-start | bytes 4128776 | tf_op jit(solution)/shard_map/ppermute | solution.py:29
  89.7 35.9 %collective-permute-start.9 = (bf16[448,1536]{1,0:T(8,128)(2,1)S(1)}, bf16[448,1536]{1,0:T(8,128)(2,1)}, u32[]{:S(2)}, u32[]{:S(2)}) collective-permute-start(bf16[448,1536]{1,0:T(8,128)(2,1)S(1)} %join_rows.10.refs_0_), channel_id=1, source_target_pairs={{0,16},{4,20},{8,24},{12,28},{16,0},{20,4},{24,8},{28,12},{1,17},{... | collective-permute-start | bytes 4128776 | tf_op jit(solution)/shard_map/ppermute | solution.py:29
  93.1 39.6 %collective-permute-start.12 = (bf16[448,1536]{1,0:T(8,128)(2,1)S(1)}, bf16[448,1536]{1,0:T(8,128)(2,1)}, u32[]{:S(2)}, u32[]{:S(2)}) collective-permute-start(bf16[448,1536]{1,0:T(8,128)(2,1)S(1)} %join_rows.10.refs_0_), channel_id=1, source_target_pairs={{0,4},{4,0},{8,12},{12,8},{16,20},{20,16},{24,28},{28,24},{1,5},{5... | collective-permute-start | bytes 4128776 | tf_op jit(solution)/shard_map/ppermute | solution.py:29
  125.6 22.7 %collective-permute-start.13 = (bf16[448,1536]{1,0:T(8,128)(2,1)S(1)}, bf16[448,1536]{1,0:T(8,128)(2,1)}, u32[]{:S(2)}, u32[]{:S(2)}) collective-permute-start(bf16[448,1536]{1,0:T(8,128)(2,1)S(1)} %collective-permute-done.8.refs_1_.refs_0_), channel_id=1, source_target_pairs={{0,4},{4,0},{8,12},{12,8},{16,20},{20,16},{24,28},{28,24},{1,5},{5... | collective-permute-start | bytes 4128776 | tf_op jit(solution)/shard_map/ppermute | solution.py:29
  125.7 22.7 %collective-permute-start.14 = (bf16[448,1536]{1,0:T(8,128)(2,1)}, bf16[448,1536]{1,0:T(8,128)(2,1)}, u32[]{:S(2)}, u32[]{:S(2)}) collective-permute-start(bf16[448,1536]{1,0:T(8,128)(2,1)} %collective-permute-done.9.refs_2_.refs_1_), channel_id=1, source_target_pairs={{0,4},{4,0},{8,12},{12,8},{16,20},{20,16},{24,28},{28,24},{1,5},{5... | collective-permute-start | bytes 4128776 | tf_op jit(solution)/shard_map/ppermute | solution.py:29
  126.2 22.1 %all-to-all-start.2 = ((bf16[8,384,128]{2,1,0:T(8,128)(2,1)}), bf16[8,384,128]{2,1,0:T(8,128)(2,1)S(1)}, u32[]{:S(2)}, u32[]{:S(2)}) async-start(bf16[8,384,128]{2,1,0:T(8,128)(2,1)} %get-tuple-element.229), calls=%async_computation.2 | async-start | bytes 1572864 | tf_op jit(solution)/shard_map/all_to_all | solution.py:968
  130.2 198.3 %reduce-scatter.4.cloned.1.call-start = ((), (), s32[]{:S(2)}) async-start(), calls=%async_computation.9 | async-start | bytes 1966080 | tf_op jit(solution)/shard_map/reduce_scatter | solution.py:1053
  179.9 27.5 %collective-permute-start.23 = (bf16[128,1536]{1,0:T(8,128)(2,1)}, bf16[128,1536]{1,0:T(8,128)(2,1)S(1)}, u32[]{:S(2)}, u32[]{:S(2)}) collective-permute-start(bf16[128,1536]{1,0:T(8,128)(2,1)} %slice.190), channel_id=1, source_target_pairs={{0,16},{4,20},{8,24},{12,28},{16,0},{20,4},{24,8},{28,12},{1,17},{... | collective-permute-start | bytes 1179656 | tf_op jit(solution)/shard_map/ppermute | solution.py:29
  180.6 26.9 %collective-permute-start.24 = (bf16[128,1536]{1,0:T(8,128)(2,1)}, bf16[128,1536]{1,0:T(8,128)(2,1)}, u32[]{:S(2)}, u32[]{:S(2)}) collective-permute-start(bf16[128,1536]{1,0:T(8,128)(2,1)} %slice.191), channel_id=1, source_target_pairs={{0,8},{4,12},{8,0},{12,4},{16,24},{20,28},{24,16},{28,20},{1,9},{5... | collective-permute-start | bytes 1179656 | tf_op jit(solution)/shard_map/ppermute | solution.py:29
  182.8 24.7 %collective-permute-start.21 = (bf16[128,1536]{1,0:T(8,128)(2,1)}, bf16[128,1536]{1,0:T(8,128)(2,1)}, u32[]{:S(2)}, u32[]{:S(2)}) collective-permute-start(bf16[128,1536]{1,0:T(8,128)(2,1)} %slice.188), channel_id=1, source_target_pairs={{0,16},{4,20},{8,24},{12,28},{16,0},{20,4},{24,8},{28,12},{1,17},{... | collective-permute-start | bytes 1179656 | tf_op jit(solution)/shard_map/ppermute | solution.py:29
  184.1 23.3 %collective-permute-start.22 = (bf16[128,1536]{1,0:T(8,128)(2,1)}, bf16[128,1536]{1,0:T(8,128)(2,1)}, u32[]{:S(2)}, u32[]{:S(2)}) collective-permute-start(bf16[128,1536]{1,0:T(8,128)(2,1)} %slice.189), channel_id=1, source_target_pairs={{0,8},{4,12},{8,0},{12,4},{16,24},{20,28},{24,16},{28,20},{1,9},{5... | collective-permute-start | bytes 1179656 | tf_op jit(solution)/shard_map/ppermute | solution.py:29
  243.4 98.3 %reduce-scatter.6.cloned.1.call-start = ((), (), s32[]{:S(2)}) async-start(), calls=%async_computation.10 | async-start | bytes 3932160 | tf_op jit(solution)/shard_map/reduce_scatter | solution.py:963
  284.5 110.1 %reduce-scatter.8.cloned.1.call-start = ((), (), s32[]{:S(2)}) async-start(), calls=%async_computation.11 | async-start | bytes 3440640 | tf_op jit(solution)/shard_map/reduce_scatter | solution.py:963
  295.6 32.9 %collective-permute-start.39 = (bf16[256,1536]{1,0:T(8,128)(2,1)S(1)}, bf16[256,1536]{1,0:T(8,128)(2,1)}, u32[]{:S(2)}, u32[]{:S(2)}) collective-permute-start(bf16[256,1536]{1,0:T(8,128)(2,1)S(1)} %pad_maximum_fusion), channel_id=1, source_target_pairs={{0,8},{4,12},{8,0},{12,4},{16,24},{20,28},{24,16},{28,20},{1,9},{5... | collective-permute-start | bytes 2359304 | tf_op jit(solution)/shard_map/ppermute | solution.py:29
  295.6 32.9 %collective-permute-start.40 = (bf16[256,1536]{1,0:T(8,128)(2,1)S(1)}, bf16[256,1536]{1,0:T(8,128)(2,1)}, u32[]{:S(2)}, u32[]{:S(2)}) collective-permute-start(bf16[256,1536]{1,0:T(8,128)(2,1)S(1)} %copy-done.72), channel_id=1, source_target_pairs={{0,16},{4,20},{8,24},{12,28},{16,0},{20,4},{24,8},{28,12},{1,17},{... | collective-permute-start | bytes 2359304 | tf_op jit(solution)/shard_map/ppermute | solution.py:29
  296.7 31.8 %collective-permute-start.41 = (bf16[96,1536]{1,0:T(8,128)(2,1)}, bf16[96,1536]{1,0:T(8,128)(2,1)S(1)}, u32[]{:S(2)}, u32[]{:S(2)}) collective-permute-start(bf16[96,1536]{1,0:T(8,128)(2,1)} %get-tuple-element.433), channel_id=1, source_target_pairs={{0,8},{4,12},{8,0},{12,4},{16,24},{20,28},{24,16},{28,20},{1,9},{5... | collective-permute-start | bytes 884744 | tf_op jit(solution)/shard_map/ppermute | solution.py:29
  298.0 30.5 %collective-permute-start.42 = (bf16[96,1536]{1,0:T(8,128)(2,1)}, bf16[96,1536]{1,0:T(8,128)(2,1)S(1)}, u32[]{:S(2)}, u32[]{:S(2)}) collective-permute-start(bf16[96,1536]{1,0:T(8,128)(2,1)} %get-tuple-element.432), channel_id=1, source_target_pairs={{0,16},{4,20},{8,24},{12,28},{16,0},{20,4},{24,8},{28,12},{1,17},{... | collective-permute-start | bytes 884744 | tf_op jit(solution)/shard_map/ppermute | solution.py:29
  351.8 27.3 %all-to-all-start.4 = ((bf16[8,48,1024]{2,1,0:T(8,128)(2,1)}), bf16[8,48,1024]{2,1,0:T(8,128)(2,1)S(1)}, u32[]{:S(2)}, u32[]{:S(2)}) async-start(bf16[8,48,1024]{2,1,0:T(8,128)(2,1)} %bitcast.14), calls=%async_computation.6 | async-start | bytes 1572864 | tf_op jit(solution)/shard_map/all_to_all | solution.py:968
  370.5 23.2 %collective-permute-start.49 = (bf16[256,1536]{1,0:T(8,128)(2,1)}, bf16[256,1536]{1,0:T(8,128)(2,1)S(1)}, u32[]{:S(2)}, u32[]{:S(2)}) collective-permute-start(bf16[256,1536]{1,0:T(8,128)(2,1)} %pad_maximum_fusion.3), channel_id=1, source_target_pairs={{0,16},{4,20},{8,24},{12,28},{16,0},{20,4},{24,8},{28,12},{1,17},{... | collective-permute-start | bytes 2359304 | tf_op jit(solution)/shard_map/ppermute | solution.py:29
  (129 other events, 1083.7 us)
Sparse Core Ops, SparseCore 0:
  25.7 60.2 all-gather.4
  88.6 88.3 all-gather.6
  243.5 32.1 reduce-scatter.3
  279.3 59.1 reduce-scatter.5
  341.9 52.6 reduce-scatter.7

commit v7 on v6

--- a/solution.py
+++ b/solution.py
@@ -1074,9 +1074,10 @@
     )
     dp, sums, dh1_near, dh1_far = found
 
-    mix_low = add_six(mix_low)
+    dh1_far, dw_in, dw_gu, mix_low = phase(
+        flip(dh1_far, 1), grad_in(place.reshape(1), sums, h1, dp, share), dw_gu, add_six(mix_low)
+    )
     mix = flip(mix_low[0], 2), flip(mix_low[1], 4)
-    dh1_far, dw_in, dw_gu = phase(flip(dh1_far, 1), grad_in(place.reshape(1), sums, h1, dp, share), dw_gu)
     dw_in = own_share(dw_in)
     dh1_own, *dh1_low = fold_cores(dh1_near, dh1_far)
     dh1_low, mix = phase(relay_six(dh1_low), mix)

time: 438 us -> 437 us (level)
  the two profiles are of different devices: /device:TPU:11 before, /device:TPU:0 now
where the time goes in v7:
time: 437 us; the launch traced here: 428 us
  Pallas kernels  146 us (33%)
  waiting for transfers between devices  110 us (25%)
  starting transfers between devices  65.3 us (15%)
  local copies, waits for them, and re-layouts  47.3 us (11%)
  other arithmetic  27.1 us (6%)
  blocking collectives  16.7 us (4%)
  between operations  15.3 us (4%)
    ppermute x47, waiting for transfers between devices, flip(): return lax.ppermute(array, 'tp', [(i, i ^ offset) for i in range(TP)])  64.6 us
    ppermute x47, starting transfers between devices, flip(): return lax.ppermute(array, 'tp', [(i, i ^ offset) for i in range(TP)])  36.3 us
    unnamed x169, local copies, waits for them, and re-layouts  34.3 us
    pallas_call x1, Pallas kernels, attn_fwd(): pl.pallas_call(attn_fwd_kernel, grid_spec=pltpu.PrefetchScalarGridSpec(nu...  29.6 us
    pallas_call x1, Pallas kernels, attn_bwd(): pl.pallas_call(attn_bwd_kernel, grid_spec=pltpu.PrefetchScalarGridSpec(nu...  29 us
    pallas_call x3, Pallas kernels, ffn(): pl.pallas_call(ffn_kernel, grid=(buckets,), in_specs=[SMEM, block(width),...  26.7 us
    all_to_all x5, starting transfers between devices, swap(): return lax.all_to_all(blocks, 'tp', 0, 0, tiled=True)  18.1 us
    all_to_all x5, waiting for transfers between devices, swap(): return lax.all_to_all(blocks, 'tp', 0, 0, tiled=True)  17.3 us
  transfers between devices with their start and end apart: 63, of which 18 were waited for; matrix products, arithmetic and copies ran while one was open for 8% of the time, Pallas kernels for 34%

profile of v7, /device:TPU:0, one launch (start us, length us, event | category | flops | bytes accessed | tf_op | source)
XLA Modules:
  0.0 428.2 jit_solution(13409545576364731497)
XLA Ops:
  11.2 16.7 %all_to_all.30 = bf16[8,48,896]{2,1,0:T(8,128)(2,1)} all-to-all(bf16[8,48,896]{2,1,0:T(8,128)(2,1)S(1)} %pack_in.1), channel_id=1, replica_groups=mesh['dp'=8,'fsdp'=4] {'dp'}, dimensions={0} | all-to-all | bytes 1376256 | tf_op jit(solution)/shard_map/all_to_all | solution.py:968
  37.8 10.4 %collective-permute-done.3 = bf16[48,1536]{1,0:T(8,128)(2,1)S(1)} collective-permute-done((bf16[48,1536]{1,0:T(8,128)(2,1)S(1)}, bf16[48,1536]{1,0:T(8,128)(2,1)S(1)}, u32[]{:S(2)}, u32[]{:S(2)}) %collective-permute-start.3) | collective-permute-done | bytes 147488 | tf_op jit(solution)/shard_map/ppermute | solution.py:80
  52.0 7.1 %collective-permute-done.5.refs_3_ = bf16[128,1536]{1,0:T(8,128)(2,1)S(1)} collective-permute-done((bf16[128,1536]{1,0:T(8,128)(2,1)S(1)}, bf16[128,1536]{1,0:T(8,128)(2,1)S(1)}, u32[]{:S(2)}, u32[]{:S(2)}) %collective-permute-start.5) | collective-permute-done | bytes 393248 | tf_op jit(solution)/shard_map/ppermute | solution.py:29
  62.5 3.7 all-to-all-start.1
  66.7 12.0 %all-to-all-done.1.got_ref = bf16[8,48,1024]{2,1,0:T(8,128)(2,1)S(1)} async-done(((bf16[8,48,1024]{2,1,0:T(8,128)(2,1)}), bf16[8,48,1024]{2,1,0:T(8,128)(2,1)S(1)}, u32[]{:S(2)}, u32[]{:S(2)}) %all-to-all-start.1) | async-done | bytes 786464 | tf_op jit(solution)/shard_map/all_to_all | solution.py:968
  85.5 4.8 %all-gather.5.cloned.1.call-done = bf16[8,192,896]{2,1,0:T(8,128)(2,1)} async-done(((bf16[8,48,896]{2,1,0:T(8,128)(2,1)}), bf16[8,192,896]{2,1,0:T(8,128)(2,1)}) %all-gather.5.cloned.1.call-update) | async-done | bytes 2752528 | tf_op jit(solution)/shard_map/all_gather | solution.py:995
  90.3 29.6 %attn_fwd.1 = (bf16[2048,1536]{1,0:T(8,128)(2,1)}, bf16[8,384,128]{2,1,0:T(8,128)(2,1)}, f32[2048,192]{1,0:T(8,128)}, f32[64,256]{1,0:T(8,128)}, f32[8,1536]{1,0...) custom-call(s32[8,4]{1,0:T(8,128)} %gather_fusion, ...), custom_call_target="tpu_custom_call" | custom-call | flops 200000000 | bytes 200000 | tf_op jit(solution)/shard_map/attn_fwd/pallas_call | solution.py:628
  128.6 13.4 %collective-permute-done.10 = bf16[96,1536]{1,0:T(8,128)(2,1)S(1)} collective-permute-done((bf16[96,1536]{1,0:T(8,128)(2,1)S(1)}, bf16[96,1536]{1,0:T(8,128)(2,1)S(1)}, u32[]{:S(2)}, u32[]{:S(2)}) %collective-permute-start.10) | collective-permute-done | bytes 294944 | tf_op jit(solution)/shard_map/ppermute | solution.py:29
  158.3 12.7 %collective-permute-done.16.refs_0_ = bf16[256,1536]{1,0:T(8,128)(2,1)S(1)} collective-permute-done((bf16[256,1536]{1,0:T(8,128)(2,1)S(1)}, bf16[256,1536]{1,0:T(8,128)(2,1)S(1)}, u32[]{:S(2)}, u32[]{:S(2)}) %collective-permute-start.16) | collective-permute-done | bytes 786464 | tf_op jit(solution)/shard_map/ppermute | solution.py:29
  188.9 12.7 %ffn.3 = (bf16[1024,512]{1,0:T(8,128)(2,1)S(1)}, bf16[1024,1024]{1,0:T(8,128)(2,1)S(1)}, bf16[512,1536]{1,0:T(8,128)(2,1)S(1)}, bf16[512,1536]{1,0:T(8,128)(2,1)...) custom-call(s32[4,4]{1,0:T(4,128)S(1)} %copy-done.62, bf16[1024,1536]{1,0:T(8,128)(2,1)S(1)} %copy-done.2, ...), custom_call_target="tpu_custom_call" | custom-call | flops 160000000 | bytes 160000 | tf_op jit(solution)/shard_map/ffn/pallas_call | solution.py:860
  206.6 6.6 %ffn.4 = (bf16[512,512]{1,0:T(8,128)(2,1)S(1)}, bf16[512,1024]{1,0:T(8,128)(2,1)S(1)}, bf16[256,1536]{1,0:T(8,128)(2,1)S(1)}, bf16[256,1536]{1,0:T(8,128)(2,1)S(...) custom-call(s32[2,4]{1,0:T(2,128)S(1)} %get-tuple-element.451.lens_ref, ...), custom_call_target="tpu_custom_call" | custom-call | flops 80000000 | bytes 80000 | tf_op jit(solution)/shard_map/ffn/pallas_call | solution.py:860
  218.8 7.4 %ffn.5 = (bf16[512,512]{1,0:T(8,128)(2,1)S(1)}, bf16[512,1024]{1,0:T(8,128)(2,1)S(1)}, bf16[256,1536]{1,0:T(8,128)(2,1)S(1)}, bf16[256,1536]{1,0:T(8,128)(2,1)S(...) custom-call(s32[2,4]{1,0:T(2,128)S(1)} %get-tuple-element.452.lens_ref, ...), custom_call_target="tpu_custom_call" | custom-call | flops 80000000 | bytes 80000 | tf_op jit(solution)/shard_map/ffn/pallas_call | solution.py:860
  230.7 5.9 %grad_down.1 = bf16[512,1536]{1,0:T(8,128)(2,1)S(1)} custom-call(bf16[1024,512]{1,0:T(8,128)(2,1)S(1)} %get-tuple-element.298.refs_0_, bf16[512,512]{1,0:T(8,128)(2,1)S(1)} %get-tuple-element.299.refs_1_, bf16[512,512]{1,0:T(8,128)(2,1)S(1)} %get-tuple-element.300.refs_2_, bf16[1024,1536]{1,0:T(8,128)(2,1)S(1)} %join_rows.11.cot_ref.refs_3_, ...), custom_call_target="tpu_custom_call" | custom-call | flops 60000000 | bytes 60000 | tf_op jit(solution)/shard_map/grad_down/pallas_call | solution.py:884
  248.8 9.2 %grad_gu.1 = bf16[4,8,48,1024]{3,2,1,0:T(8,128)(2,1)} custom-call(bf16[1024,1536]{1,0:T(8,128)(2,1)S(1)} %copy-done.3, bf16[512,1536]{1,0:T(8,128)(2,1)S(1)} %copy-done.11, bf16[512,1536]{1,0:T(8,128)(2,1)S(1)} %copy-done.13, bf16[1024,1024]{1,0:T(8,128)(2,1)S(1)} %copy-done.34, bf16[512,1024]{1,0:T(8,128)(2,1)S(1)} %copy-done.41, ...), custom_call_target="tpu_custom_call" | custom-call | flops 110000000 | bytes 110000 | tf_op jit(solution)/shard_map/grad_gu/pallas_call | solution.py:910
  264.1 9.9 %mid_bwd.1 = (f32[256,1536]{1,0:T(8,128)}, bf16[8,384,128]{2,1,0:T(8,128)(2,1)}, bf16[768,1536]{1,0:T(8,128)(2,1)}, bf16[768,1536]{1,0:T(8,128)(2,1)}) custom-call(s32[8]{0:T(128)S(1)} %copy-done.61, f32[256,1536]{1,0:T(8,128)} %convert_add_fusion.a_ref, bf16[256,1536]{1,0:T(8,128)(2,1)} %collective-permute-done.31.b_ref, ...), custom_call_target="tpu_custom_call" | custom-call | flops 90000000 | bytes 90000 | tf_op jit(solution)/shard_map/mid_bwd/pallas_call | solution.py:757
  285.6 5.3 %all-to-all-done.3.dm_ref = bf16[8,384,128]{2,1,0:T(8,128)(2,1)S(1)} async-done(((bf16[8,384,128]{2,1,0:T(8,128)(2,1)}), bf16[8,384,128]{2,1,0:T(8,128)(2,1)S(1)}, u32[]{:S(2)}, u32[]{:S(2)}) %all-to-all-start.3) | async-done | bytes 786464 | tf_op jit(solution)/shard_map/all_to_all | solution.py:968
  295.0 29.0 %attn_bwd.1 = (bf16[2048,896]{1,0:T(8,128)(2,1)}, f32[8,256]{1,0:T(8,128)}, bf16[1024,1536]{1,0:T(8,128)(2,1)}, bf16[1024,1536]{1,0:T(8,128)(2,1)}) custom-call(s32[8,4]{1,0:T(8,128)} %gather_fusion, s32[8]{0:T(128)} %get-tuple-element.450.spots_ref, f32[8,256]{1,0:T(8,128)} %get-tuple-element.350.gains_ref, bf16[448,192]{1,0:T(8,128)(2,1)} %constant.103.clone.wide_ref, ...), custom_call_target="tpu_custom_call" | custom-call | flops 240000000 | bytes 240000 | tf_op jit(solution)/shard_map/attn_bwd/pallas_call | solution.py:681
  324.3 11.0 %grad_in.1 = bf16[4,8,48,896]{3,2,1,0:T(8,128)(2,1)} custom-call(s32[1]{0:T(128)} %bitcast.12.place_ref, f32[8,256]{1,0:T(8,128)} %get-tuple-element.374.sums_ref, bf16[2048,1536]{1,0:T(8,128)(2,1)} %get-tuple-element.375.left_ref, bf16[2048,896]{1,0:T(8,128)(2,1)} %get-tuple-element.376.right_ref), custom_call_target="tpu_custom_call" | custom-call | flops 110000000 | bytes 110000 | tf_op jit(solution)/shard_map/grad_in/pallas_call | solution.py:945
  350.3 3.7 all-to-all-start.4
  354.0 11.5 %collective-permute-done.44 = bf16[128,1536]{1,0:T(8,128)(2,1)S(1)} collective-permute-done((bf16[128,1536]{1,0:T(8,128)(2,1)S(1)}, bf16[128,1536]{1,0:T(8,128)(2,1)S(1)}, u32[]{:S(2)}, u32[]{:S(2)}) %collective-permute-start.44) | collective-permute-done | bytes 393248 | tf_op jit(solution)/shard_map/ppermute | solution.py:29
  379.4 11.2 %collective-permute-done.49.refs_2_ = bf16[256,1536]{1,0:T(8,128)(2,1)S(1)} collective-permute-done((bf16[256,1536]{1,0:T(8,128)(2,1)}, bf16[256,1536]{1,0:T(8,128)(2,1)S(1)}, u32[]{:S(2)}, u32[]{:S(2)}) %collective-permute-start.49) | collective-permute-done | bytes 786464 | tf_op jit(solution)/shard_map/ppermute | solution.py:29
  390.6 6.2 %reduce-scatter.8.cloned.1.call-done = bf16[384,896]{1,0:T(8,128)(2,1)} async-done(((bf16[1536,896]{1,0:T(8,128)(2,1)}), bf16[384,896]{1,0:T(8,128)(2,1)}) %reduce-scatter.8.cloned.1.call-update) | async-done | bytes 688144 | tf_op jit(solution)/shard_map/reduce_scatter | solution.py:963
  396.9 3.7 all-to-all-start.5
  414.3 3.6 unpack_in.1
  (369 shorter events, 165.6 us)
Async XLA Ops:
  7.2 83.1 %all-gather.5.cloned.1.call-start = ((), (), s32[]{:S(2)}) async-start(), calls=%async_computation.12 | async-start | bytes 3440640 | tf_op jit(solution)/shard_map/all_gather | solution.py:995
  66.2 118.4 %all-gather.7.cloned.1.call-start = ((), (), s32[]{:S(2)}) async-start(), calls=%async_computation.13 | async-start | bytes 5898240 | tf_op jit(solution)/shard_map/all_gather | solution.py:1007
  66.3 24.0 %collective-permute-start.7 = (bf16[1024,1536]{1,0:T(8,128)(2,1)}, bf16[1024,1536]{1,0:T(8,128)(2,1)}, u32[]{:S(2)}, u32[]{:S(2)}) collective-permute-start(bf16[1024,1536]{1,0:T(8,128)(2,1)} %join_rows.9.near_ref), channel_id=1, source_target_pairs={{0,4},{4,0},{8,12},{12,8},{16,20},{20,16},{24,28},{28,24},{1,5},{5... | collective-permute-start | bytes 9437192 | tf_op jit(solution)/shard_map/ppermute | solution.py:29
  81.1 38.9 %collective-permute-start.8 = (bf16[448,1536]{1,0:T(8,128)(2,1)S(1)}, bf16[448,1536]{1,0:T(8,128)(2,1)S(1)}, u32[]{:S(2)}, u32[]{:S(2)}) collective-permute-start(bf16[448,1536]{1,0:T(8,128)(2,1)S(1)} %join_rows.10.refs_0_), channel_id=1, source_target_pairs={{0,8},{4,12},{8,0},{12,4},{16,24},{20,28},{24,16},{28,20},{1,9},{5... | collective-permute-start | bytes 4128776 | tf_op jit(solution)/shard_map/ppermute | solution.py:29
  81.6 38.3 %collective-permute-start.9 = (bf16[448,1536]{1,0:T(8,128)(2,1)S(1)}, bf16[448,1536]{1,0:T(8,128)(2,1)}, u32[]{:S(2)}, u32[]{:S(2)}) collective-permute-start(bf16[448,1536]{1,0:T(8,128)(2,1)S(1)} %join_rows.10.refs_0_), channel_id=1, source_target_pairs={{0,16},{4,20},{8,24},{12,28},{16,0},{20,4},{24,8},{28,12},{1,17},{... | collective-permute-start | bytes 4128776 | tf_op jit(solution)/shard_map/ppermute | solution.py:29
  85.5 43.1 %collective-permute-start.12 = (bf16[448,1536]{1,0:T(8,128)(2,1)S(1)}, bf16[448,1536]{1,0:T(8,128)(2,1)}, u32[]{:S(2)}, u32[]{:S(2)}) collective-permute-start(bf16[448,1536]{1,0:T(8,128)(2,1)S(1)} %join_rows.10.refs_0_), channel_id=1, source_target_pairs={{0,4},{4,0},{8,12},{12,8},{16,20},{20,16},{24,28},{28,24},{1,5},{5... | collective-permute-start | bytes 4128776 | tf_op jit(solution)/shard_map/ppermute | solution.py:29
  119.9 22.8 %collective-permute-start.13 = (bf16[448,1536]{1,0:T(8,128)(2,1)S(1)}, bf16[448,1536]{1,0:T(8,128)(2,1)}, u32[]{:S(2)}, u32[]{:S(2)}) collective-permute-start(bf16[448,1536]{1,0:T(8,128)(2,1)S(1)} %collective-permute-done.8.refs_1_.refs_0_), channel_id=1, source_target_pairs={{0,4},{4,0},{8,12},{12,8},{16,20},{20,16},{24,28},{28,24},{1,5},{5... | collective-permute-start | bytes 4128776 | tf_op jit(solution)/shard_map/ppermute | solution.py:29
  120.1 22.7 %collective-permute-start.14 = (bf16[448,1536]{1,0:T(8,128)(2,1)}, bf16[448,1536]{1,0:T(8,128)(2,1)}, u32[]{:S(2)}, u32[]{:S(2)}) collective-permute-start(bf16[448,1536]{1,0:T(8,128)(2,1)} %collective-permute-done.9.refs_2_.refs_1_), channel_id=1, source_target_pairs={{0,4},{4,0},{8,12},{12,8},{16,20},{20,16},{24,28},{28,24},{1,5},{5... | collective-permute-start | bytes 4128776 | tf_op jit(solution)/shard_map/ppermute | solution.py:29
  120.5 22.2 %all-to-all-start.2 = ((bf16[8,384,128]{2,1,0:T(8,128)(2,1)}), bf16[8,384,128]{2,1,0:T(8,128)(2,1)S(1)}, u32[]{:S(2)}, u32[]{:S(2)}) async-start(bf16[8,384,128]{2,1,0:T(8,128)(2,1)} %get-tuple-element.231), calls=%async_computation.2 | async-start | bytes 1572864 | tf_op jit(solution)/shard_map/all_to_all | solution.py:968
  124.1 200.0 %reduce-scatter.4.cloned.1.call-start = ((), (), s32[]{:S(2)}) async-start(), calls=%async_computation.9 | async-start | bytes 1966080 | tf_op jit(solution)/shard_map/reduce_scatter | solution.py:1053
  175.4 28.6 %collective-permute-start.23 = (bf16[128,1536]{1,0:T(8,128)(2,1)}, bf16[128,1536]{1,0:T(8,128)(2,1)S(1)}, u32[]{:S(2)}, u32[]{:S(2)}) collective-permute-start(bf16[128,1536]{1,0:T(8,128)(2,1)} %slice.190), channel_id=1, source_target_pairs={{0,16},{4,20},{8,24},{12,28},{16,0},{20,4},{24,8},{28,12},{1,17},{... | collective-permute-start | bytes 1179656 | tf_op jit(solution)/shard_map/ppermute | solution.py:29
  175.7 28.3 %collective-permute-start.24 = (bf16[128,1536]{1,0:T(8,128)(2,1)}, bf16[128,1536]{1,0:T(8,128)(2,1)}, u32[]{:S(2)}, u32[]{:S(2)}) collective-permute-start(bf16[128,1536]{1,0:T(8,128)(2,1)} %slice.191), channel_id=1, source_target_pairs={{0,8},{4,12},{8,0},{12,4},{16,24},{20,28},{24,16},{28,20},{1,9},{5... | collective-permute-start | bytes 1179656 | tf_op jit(solution)/shard_map/ppermute | solution.py:29
  178.3 25.7 %collective-permute-start.21 = (bf16[128,1536]{1,0:T(8,128)(2,1)}, bf16[128,1536]{1,0:T(8,128)(2,1)}, u32[]{:S(2)}, u32[]{:S(2)}) collective-permute-start(bf16[128,1536]{1,0:T(8,128)(2,1)} %slice.188), channel_id=1, source_target_pairs={{0,16},{4,20},{8,24},{12,28},{16,0},{20,4},{24,8},{28,12},{1,17},{... | collective-permute-start | bytes 1179656 | tf_op jit(solution)/shard_map/ppermute | solution.py:29
  179.5 24.6 %collective-permute-start.22 = (bf16[128,1536]{1,0:T(8,128)(2,1)}, bf16[128,1536]{1,0:T(8,128)(2,1)}, u32[]{:S(2)}, u32[]{:S(2)}) collective-permute-start(bf16[128,1536]{1,0:T(8,128)(2,1)} %slice.189), channel_id=1, source_target_pairs={{0,8},{4,12},{8,0},{12,4},{16,24},{20,28},{24,16},{28,20},{1,9},{5... | collective-permute-start | bytes 1179656 | tf_op jit(solution)/shard_map/ppermute | solution.py:29
  237.9 102.6 %reduce-scatter.6.cloned.1.call-start = ((), (), s32[]{:S(2)}) async-start(), calls=%async_computation.10 | async-start | bytes 3932160 | tf_op jit(solution)/shard_map/reduce_scatter | solution.py:963
  278.3 118.5 %reduce-scatter.8.cloned.1.call-start = ((), (), s32[]{:S(2)}) async-start(), calls=%async_computation.11 | async-start | bytes 3440640 | tf_op jit(solution)/shard_map/reduce_scatter | solution.py:963
  290.9 33.3 %collective-permute-start.39 = (bf16[256,1536]{1,0:T(8,128)(2,1)}, bf16[256,1536]{1,0:T(8,128)(2,1)}, u32[]{:S(2)}, u32[]{:S(2)}) collective-permute-start(bf16[256,1536]{1,0:T(8,128)(2,1)} %pad_maximum_fusion), channel_id=1, source_target_pairs={{0,8},{4,12},{8,0},{12,4},{16,24},{20,28},{24,16},{28,20},{1,9},{5... | collective-permute-start | bytes 2359304 | tf_op jit(solution)/shard_map/ppermute | solution.py:29
  291.4 32.8 %collective-permute-start.40 = (bf16[256,1536]{1,0:T(8,128)(2,1)}, bf16[256,1536]{1,0:T(8,128)(2,1)}, u32[]{:S(2)}, u32[]{:S(2)}) collective-permute-start(bf16[256,1536]{1,0:T(8,128)(2,1)} %pad_maximum_fusion.1), channel_id=1, source_target_pairs={{0,16},{4,20},{8,24},{12,28},{16,0},{20,4},{24,8},{28,12},{1,17},{... | collective-permute-start | bytes 2359304 | tf_op jit(solution)/shard_map/ppermute | solution.py:29
  292.1 32.1 %collective-permute-start.41 = (bf16[96,1536]{1,0:T(8,128)(2,1)S(1)}, bf16[96,1536]{1,0:T(8,128)(2,1)S(1)}, u32[]{:S(2)}, u32[]{:S(2)}) collective-permute-start(bf16[96,1536]{1,0:T(8,128)(2,1)S(1)} %get-tuple-element.437), channel_id=1, source_target_pairs={{0,8},{4,12},{8,0},{12,4},{16,24},{20,28},{24,16},{28,20},{1,9},{5... | collective-permute-start | bytes 884744 | tf_op jit(solution)/shard_map/ppermute | solution.py:29
  293.6 30.6 %collective-permute-start.42 = (bf16[96,1536]{1,0:T(8,128)(2,1)S(1)}, bf16[96,1536]{1,0:T(8,128)(2,1)S(1)}, u32[]{:S(2)}, u32[]{:S(2)}) collective-permute-start(bf16[96,1536]{1,0:T(8,128)(2,1)S(1)} %get-tuple-element.436), channel_id=1, source_target_pairs={{0,16},{4,20},{8,24},{12,28},{16,0},{20,4},{24,8},{28,12},{1,17},{... | collective-permute-start | bytes 884744 | tf_op jit(solution)/shard_map/ppermute | solution.py:29
  340.6 27.5 %collective-permute-start.46 = (bf16[192,1536]{1,0:T(8,128)(2,1)}, bf16[192,1536]{1,0:T(8,128)(2,1)}, u32[]{:S(2)}, u32[]{:S(2)}) collective-permute-start(bf16[192,1536]{1,0:T(8,128)(2,1)} %pad_maximum_fusion.4), channel_id=1, source_target_pairs={{0,8},{4,12},{8,0},{12,4},{16,24},{20,28},{24,16},{28,20},{1,9},{5... | collective-permute-start | bytes 1769480 | tf_op jit(solution)/shard_map/ppermute | solution.py:29
  342.1 26.0 %collective-permute-start.47 = (bf16[192,1536]{1,0:T(8,128)(2,1)}, bf16[192,1536]{1,0:T(8,128)(2,1)}, u32[]{:S(2)}, u32[]{:S(2)}) collective-permute-start(bf16[192,1536]{1,0:T(8,128)(2,1)} %pad_maximum_fusion.5), channel_id=1, source_target_pairs={{0,16},{4,20},{8,24},{12,28},{16,0},{20,4},{24,8},{28,12},{1,17},{... | collective-permute-start | bytes 1769480 | tf_op jit(solution)/shard_map/ppermute | solution.py:29
  350.3 29.2 %all-to-all-start.4 = ((bf16[8,48,1024]{2,1,0:T(8,128)(2,1)}), bf16[8,48,1024]{2,1,0:T(8,128)(2,1)S(1)}, u32[]{:S(2)}, u32[]{:S(2)}) async-start(bf16[8,48,1024]{2,1,0:T(8,128)(2,1)} %bitcast.14), calls=%async_computation.6 | async-start | bytes 1572864 | tf_op jit(solution)/shard_map/all_to_all | solution.py:968
  369.2 21.5 %collective-permute-start.49 = (bf16[256,1536]{1,0:T(8,128)(2,1)}, bf16[256,1536]{1,0:T(8,128)(2,1)S(1)}, u32[]{:S(2)}, u32[]{:S(2)}) collective-permute-start(bf16[256,1536]{1,0:T(8,128)(2,1)} %pad_maximum_fusion.3), channel_id=1, source_target_pairs={{0,16},{4,20},{8,24},{12,28},{16,0},{20,4},{24,8},{28,12},{1,17},{... | collective-permute-start | bytes 2359304 | tf_op jit(solution)/shard_map/ppermute | solution.py:29
  (123 other events, 1121.1 us)
Sparse Core Ops, SparseCore 0:
  28.0 62.2 all-gather.4
  92.5 88.5 all-gather.6
  238.0 41.0 reduce-scatter.3
  281.2 59.2 reduce-scatter.5
  342.7 54.1 reduce-scatter.7
